TPU v7x, 32 devices: a whole 2x2x4 slice. The times are simulated.
32 devices in a mesh: ctx: 8 (over z, y), wt: 4 (over x, core).
Axes of the slice: x: 2, y: 2, z: 4, core: 2. Of those that a mesh axis runs over, the one named last changes fastest.
Arguments:
- tokens: bfloat16 [2, 4, 3072, 2560], P(None, 'wt', 'ctx'), may hold values from -6 to 6
- segment_ids: int32 [2, 4, 3072], P(None, 'wt', 'ctx'), may hold values from 0 to 3, never falling along the last dimension, each value on 1 to 2304 neighbouring positions
- cotangent: bfloat16 [2, 4, 3072, 2560], P(None, 'wt', 'ctx'), may hold values from -6 to 6
- gain_attn: bfloat16 [2560], P(('ctx', 'wt')), may hold values from 0.5 to 1.5
- w_query: bfloat16 [2560, 2560], P(('ctx', 'wt')), may hold values from -0.125 to 0.125
- w_key: bfloat16 [2560, 256], P(('ctx', 'wt')), may hold values from -0.125 to 0.125
- w_value: bfloat16 [2560, 256], P(('ctx', 'wt')), may hold values from -0.125 to 0.125
- w_out: bfloat16 [2560, 2560], P(None, ('ctx', 'wt')), may hold values from -1 to 1
- gain_mlp: bfloat16 [2560], P(('ctx', 'wt')), may hold values from 0.5 to 1.5
- w_gate: bfloat16 [2560, 7680], P('ctx', 'wt'), may hold values from -0.125 to 0.125
- w_up: bfloat16 [2560, 7680], P('ctx', 'wt'), may hold values from -0.125 to 0.125
- w_down: bfloat16 [7680, 2560], P('wt', 'ctx'), may hold values from -0.0625 to 0.0625
Outputs:
- output: float32 [2, 4, 3072, 2560], P(None, 'wt', 'ctx')
- grad_tokens: float32 [2, 4, 3072, 2560], P(None, 'wt', 'ctx')
- grad_gain_attn: float32 [2560], P(('ctx', 'wt'))
- grad_w_query: float32 [2560, 2560], P(('ctx', 'wt'))
- grad_w_key: float32 [2560, 256], P(('ctx', 'wt'))
- grad_w_value: float32 [2560, 256], P(('ctx', 'wt'))
- grad_w_out: float32 [2560, 2560], P(None, ('ctx', 'wt'))
- grad_gain_mlp: float32 [2560], P(('ctx', 'wt'))
- grad_w_gate: float32 [2560, 7680], P('ctx', 'wt')
- grad_w_up: float32 [2560, 7680], P('ctx', 'wt')
- grad_w_down: float32 [7680, 2560], P('wt', 'ctx')
Inputs may be any that keep to these rules, and one draw needn't show every extreme that they name: `segment_ids`: along each sequence the ids never fall and run through all 4 documents; each document has 1 to 2304 tokens and one has exactly that many.
All inputs are finite; a program needn't handle non-finite values.
Results may differ from a plain program's by a relative error of at most 0.017.
Values may be sent and summed in bfloat16 or wider, within the bound.
No kernel may reach another device: no remote copies, remote signals or barrier semaphores. Data moves between devices by JAX's collectives and lax.ppermute only.
A program may use at most 512 MiB of HBM per device.

v0:
```python
import jax
import jax.numpy as jnp
from jax import lax
from jax.sharding import PartitionSpec as P

WINDOW = 2048


EPSILON = 1e-06
NEGATIVE = -1e30


def rms_scale(values, gain):
    return values * lax.rsqrt(jnp.mean(values * values, axis=-1, keepdims=True) + EPSILON) * gain


def doc_positions(doc_ids):
    index = jnp.arange(doc_ids.shape[0], dtype=jnp.int32)
    starts = jnp.concatenate([jnp.ones((1,), dtype=jnp.bool_), doc_ids[1:] != doc_ids[:-1]])
    first = lax.cummax(jnp.where(starts, index, 0), axis=0)
    return index - first


def rope_tables(positions, half_size):
    freqs = 10000.0 ** (-jnp.arange(half_size, dtype=jnp.float32) / half_size)
    angles = positions.astype(jnp.float32)[:, None] * freqs[None, :]
    return (jnp.cos(angles), jnp.sin(angles))


def rotate(values, cosine_table, sine_table):
    half_size = values.shape[-1] // 2
    first_half = values[..., :half_size]
    second_half = values[..., half_size:]
    return jnp.concatenate(
        [
            first_half * cosine_table - second_half * sine_table,
            second_half * cosine_table + first_half * sine_table,
        ],
        axis=-1,
    )


def contract_rows(left, right):
    return lax.dot_general(
        left, right, (((0,), (0,)), ((), ())), preferred_element_type=jnp.float32
    )


def contract_last(left, right):
    return lax.dot_general(
        left, right, (((1,), (1,)), ((), ())), preferred_element_type=jnp.float32
    )


def softmax_rows(query_rot, key_rot, visible):
    scores = jnp.einsum("rhd,kd->hrk", query_rot, key_rot, preferred_element_type=jnp.float32)
    scores = jnp.where(visible[None], scores, NEGATIVE)
    largest = jnp.max(scores, axis=-1, keepdims=True)
    exponent = jnp.exp(scores - largest)
    return exponent / jnp.sum(exponent, axis=-1, keepdims=True)


def key_window(key_all, value_all, ids_all, key_start, key_len, first_row, rows_dev):
    half_size = key_all.shape[1] // 2
    cosine_all, sine_all = rope_tables(doc_positions(ids_all), half_size)
    cosine_win = lax.dynamic_slice_in_dim(cosine_all, key_start, key_len, 0)
    sine_win = lax.dynamic_slice_in_dim(sine_all, key_start, key_len, 0)
    key_part = lax.dynamic_slice_in_dim(key_all, key_start, key_len, 0).astype(jnp.float32)
    key_rot = rotate(key_part, cosine_win, sine_win).astype(jnp.bfloat16)
    value_win = lax.dynamic_slice_in_dim(value_all, key_start, key_len, 0)
    ids_win = lax.dynamic_slice_in_dim(ids_all, key_start, key_len, 0)
    ids_query = lax.dynamic_slice_in_dim(ids_all, first_row, rows_dev, 0)
    cosine_query = lax.dynamic_slice_in_dim(cosine_all, first_row, rows_dev, 0)
    sine_query = lax.dynamic_slice_in_dim(sine_all, first_row, rows_dev, 0)
    query_index = first_row + jnp.arange(rows_dev, dtype=jnp.int32)
    key_index = key_start + jnp.arange(key_len, dtype=jnp.int32)
    distance = query_index[:, None] - key_index[None, :]
    visible = (ids_query[:, None] == ids_win[None, :]) & (distance >= 0) & (distance < WINDOW)
    return (key_rot, value_win, cosine_win, sine_win, cosine_query, sine_query, visible)


def add_tuples(running, update):
    if running is None:
        return tuple(update)
    return tuple((first + second for first, second in zip(running, update)))


def local(
    tokens,
    segment_ids,
    cotangent,
    gain_attn,
    w_query,
    w_key,
    w_value,
    w_out,
    gain_mlp,
    w_gate,
    w_up,
    w_down,
):
    micro_count = tokens.shape[0]
    rows_dev = tokens.shape[2]
    head_size = w_key.shape[1]
    query_width = w_query.shape[1]
    head_count = query_width // head_size
    seq_total = rows_dev * lax.axis_size("ctx")
    first_row = lax.axis_index("ctx") * rows_dev
    key_len = min(seq_total, WINDOW + rows_dev)
    key_start = jnp.clip(first_row + rows_dev - key_len, 0, seq_total - key_len)
    scaling = head_size ** (-0.5)
    attn_total = None
    mlp_total = None
    outputs = []
    input_grads = []
    for micro_step in range(micro_count):
        attn_part = (
            lax.all_gather(gain_attn, ("ctx", "wt"), axis=0, tiled=True),
            lax.all_gather(w_query, ("ctx", "wt"), axis=0, tiled=True),
            lax.all_gather(w_key, ("ctx", "wt"), axis=0, tiled=True),
            lax.all_gather(w_value, ("ctx", "wt"), axis=0, tiled=True),
            lax.all_gather(w_out, ("ctx", "wt"), axis=1, tiled=True),
            lax.all_gather(gain_mlp, ("ctx", "wt"), axis=0, tiled=True),
        )
        mlp_part = (
            lax.all_gather(w_gate, "ctx", axis=0, tiled=True),
            lax.all_gather(w_up, "ctx", axis=0, tiled=True),
            lax.all_gather(w_down, "ctx", axis=1, tiled=True),
        )
        weights = tuple(attn_part) + tuple(mlp_part)
        (
            gain_one,
            query_full,
            key_full,
            value_full,
            out_full,
            gain_two,
            gate_full,
            up_full,
            down_full,
        ) = weights
        gain_first = gain_one.astype(jnp.float32)
        gain_second = gain_two.astype(jnp.float32)
        inputs = tokens[micro_step, 0].astype(jnp.float32)
        own_ids = segment_ids[micro_step, 0]
        normed = rms_scale(inputs, gain_first).astype(jnp.bfloat16)
        queries = jnp.dot(normed, query_full, preferred_element_type=jnp.float32)
        key_rows = jnp.dot(normed, key_full, preferred_element_type=jnp.float32).astype(
            jnp.bfloat16
        )
        value_rows = jnp.dot(normed, value_full, preferred_element_type=jnp.float32).astype(
            jnp.bfloat16
        )
        key_all, value_all, ids_all = (
            lax.all_gather(key_rows, "ctx", axis=0, tiled=True),
            lax.all_gather(value_rows, "ctx", axis=0, tiled=True),
            lax.all_gather(own_ids, "ctx", axis=0, tiled=True),
        )
        key_rot, value_win, cosine_win, sine_win, cosine_query, sine_query, visible = key_window(
            key_all, value_all, ids_all, key_start, key_len, first_row, rows_dev
        )
        query_rot = rotate(
            queries.reshape(rows_dev, head_count, head_size),
            cosine_query[:, None, :],
            sine_query[:, None, :],
        )
        query_rot = (query_rot * scaling).astype(jnp.bfloat16)
        attn_probs = softmax_rows(query_rot, key_rot, visible)
        attended = jnp.einsum(
            "hrk,kd->rhd",
            attn_probs.astype(jnp.bfloat16),
            value_win,
            preferred_element_type=jnp.float32,
        )
        attended = attended.reshape(rows_dev, query_width).astype(jnp.bfloat16)
        middle = inputs + jnp.dot(attended, out_full, preferred_element_type=jnp.float32)
        normed_mlp = rms_scale(middle, gain_second).astype(jnp.bfloat16)
        normed_all = lax.all_gather(normed_mlp, "wt", axis=0, tiled=True)
        gate_rows = jnp.dot(normed_all, gate_full, preferred_element_type=jnp.float32)
        up_rows = jnp.dot(normed_all, up_full, preferred_element_type=jnp.float32)
        hidden = (jax.nn.gelu(gate_rows) * up_rows).astype(jnp.bfloat16)
        mlp_out = lax.psum_scatter(
            jnp.dot(hidden, down_full, preferred_element_type=jnp.float32).astype(jnp.bfloat16),
            "wt",
            scatter_dimension=0,
            tiled=True,
        ).astype(jnp.float32)
        outputs.append(middle + mlp_out)
        cot_rows = cotangent[micro_step, 0]
        cot_all = lax.all_gather(cot_rows, "wt", axis=0, tiled=True)
        step_down = contract_rows(cot_all, hidden)
        hidden_grad = contract_last(cot_all, down_full)
        gelu_gate, gelu_back = jax.vjp(jax.nn.gelu, gate_rows)
        gate_grad = gelu_back(hidden_grad * up_rows)[0].astype(jnp.bfloat16)
        up_grad = (hidden_grad * gelu_gate).astype(jnp.bfloat16)
        step_gate = contract_rows(normed_all, gate_grad)
        step_up = contract_rows(normed_all, up_grad)
        mlp_in_grad = lax.psum_scatter(
            (contract_last(gate_grad, gate_full) + contract_last(up_grad, up_full)).astype(
                jnp.bfloat16
            ),
            "wt",
            scatter_dimension=0,
            tiled=True,
        ).astype(jnp.float32)
        norm_two_back = jax.vjp(rms_scale, middle, gain_second)[1]
        middle_part, gain_second_grad = norm_two_back(mlp_in_grad)
        middle_grad = middle_part + cot_rows.astype(jnp.float32)
        branch_grad = middle_grad.astype(jnp.bfloat16)
        step_out = contract_rows(branch_grad, attended)
        attended_grad = contract_last(branch_grad, out_full).astype(jnp.bfloat16)
        attended_grad = attended_grad.reshape(rows_dev, head_count, head_size)
        attn_probs = softmax_rows(query_rot, key_rot, visible)
        probs_grad = jnp.einsum(
            "rhd,kd->hrk", attended_grad, value_win, preferred_element_type=jnp.float32
        )
        value_grad = jnp.einsum(
            "hrk,rhd->kd",
            attn_probs.astype(jnp.bfloat16),
            attended_grad,
            preferred_element_type=jnp.float32,
        )
        row_delta = jnp.sum(attn_probs * probs_grad, axis=-1, keepdims=True)
        score_grad = (attn_probs * (probs_grad - row_delta)).astype(jnp.bfloat16)
        query_grad = (
            jnp.einsum("hrk,kd->rhd", score_grad, key_rot, preferred_element_type=jnp.float32)
            * scaling
        )
        query_grad = rotate(query_grad, cosine_query[:, None, :], -sine_query[:, None, :])
        query_grad = query_grad.reshape(rows_dev, query_width).astype(jnp.bfloat16)
        key_grad = jnp.einsum(
            "hrk,rhd->kd", score_grad, query_rot, preferred_element_type=jnp.float32
        )
        key_grad = rotate(key_grad, cosine_win, -sine_win)
        kv_term = jnp.zeros((seq_total, 2 * head_size), jnp.float32)
        kv_term = lax.dynamic_update_slice_in_dim(
            kv_term, jnp.concatenate([key_grad, value_grad], axis=1), key_start, 0
        )
        kv_own = lax.psum_scatter(
            kv_term.astype(jnp.bfloat16), "ctx", scatter_dimension=0, tiled=True
        ).astype(jnp.float32)
        key_own = kv_own[:, :head_size].astype(jnp.bfloat16)
        value_own = kv_own[:, head_size:].astype(jnp.bfloat16)
        step_query = contract_rows(normed, query_grad)
        step_key = contract_rows(normed, key_own)
        step_value = contract_rows(normed, value_own)
        attn_in_grad = (
            contract_last(query_grad, query_full)
            + contract_last(key_own, key_full)
            + contract_last(value_own, value_full)
        )
        norm_one_back = jax.vjp(rms_scale, inputs, gain_first)[1]
        input_part, gain_first_grad = norm_one_back(attn_in_grad)
        input_grads.append(middle_grad + input_part)
        attn_step = (gain_first_grad, step_query, step_key, step_value, step_out, gain_second_grad)
        mlp_step = (step_gate, step_up, step_down)
        attn_total = add_tuples(attn_total, attn_step)
        mlp_total = add_tuples(mlp_total, mlp_step)
    attn_grads = (
        lax.psum_scatter(attn_total[0], ("ctx", "wt"), scatter_dimension=0, tiled=True),
        lax.psum_scatter(attn_total[1], ("ctx", "wt"), scatter_dimension=0, tiled=True),
        lax.psum_scatter(attn_total[2], ("ctx", "wt"), scatter_dimension=0, tiled=True),
        lax.psum_scatter(attn_total[3], ("ctx", "wt"), scatter_dimension=0, tiled=True),
        lax.psum_scatter(attn_total[4], ("ctx", "wt"), scatter_dimension=0, tiled=True),
        lax.psum_scatter(attn_total[5], ("ctx", "wt"), scatter_dimension=0, tiled=True),
    )
    mlp_grads = (
        lax.psum_scatter(
            mlp_total[0].astype(jnp.bfloat16), "ctx", scatter_dimension=0, tiled=True
        ).astype(jnp.float32),
        lax.psum_scatter(
            mlp_total[1].astype(jnp.bfloat16), "ctx", scatter_dimension=0, tiled=True
        ).astype(jnp.float32),
        lax.psum_scatter(
            mlp_total[2].astype(jnp.bfloat16), "ctx", scatter_dimension=0, tiled=True
        ).astype(jnp.float32),
    )
    output = jnp.stack(outputs)[:, None]
    grad_tokens = jnp.stack(input_grads)[:, None]
    return (
        output,
        grad_tokens,
        attn_grads[0],
        attn_grads[1],
        attn_grads[2],
        attn_grads[3],
        attn_grads[4].T,
        attn_grads[5],
        mlp_grads[0],
        mlp_grads[1],
        mlp_grads[2].T,
    )


def solution(mesh):
    placed = (
        P(None, "wt", "ctx", None),
        P(None, "wt", "ctx"),
        P(None, "wt", "ctx", None),
        P(("ctx", "wt")),
        P(("ctx", "wt"), None),
        P(("ctx", "wt"), None),
        P(("ctx", "wt"), None),
        P(None, ("ctx", "wt")),
        P(("ctx", "wt")),
        P("ctx", "wt"),
        P("ctx", "wt"),
        P("wt", "ctx"),
    )
    return jax.shard_map(
        local,
        mesh=mesh,
        in_specs=placed,
        out_specs=(
            P(None, "wt", "ctx", None),
            P(None, "wt", "ctx", None),
            P(("ctx", "wt")),
            P(("ctx", "wt"), None),
            P(("ctx", "wt"), None),
            P(("ctx", "wt"), None),
            P(None, ("ctx", "wt")),
            P(("ctx", "wt")),
            P("ctx", "wt"),
            P("ctx", "wt"),
            P("wt", "ctx"),
        ),
        check_vma=False,
    )
```

profile of v0, /device:TPU:0, one launch (start us, length us, event | category | flops | bytes accessed | tf_op | source)
XLA Modules:
  0.0 3251.5 jit_solution(916325265245997010)
XLA Ops:
  10.4 42.2 %all-reduce.5 = (bf16[2560]{0:T(1024)(128)(2,1)S(1)}, bf16[2560]{0:T(1024)(128)(2,1)}) all-reduce(bf16[2560]{0:T(1024)(128)(2,1)S(1)} %dynamic-update-slice, bf16[2560]{0:T(1024)(128)(2,1)S(1)} %dynamic-update-slice.1), channel_id=1, replica_groups=mesh['ctx'=8,'wt'=4] {'ctx','wt'}, use_global_device_ids=true, to_apply=%add | all-reduce | flops 5120 | bytes 20480
  71.9 52.1 %all-gather.20.cloned.1.call-done = bf16[2560,256]{1,0:T(8,128)(2,1)} async-done(((bf16[80,256]{1,0:T(8,128)(2,1)}), bf16[2560,256]{1,0:T(8,128)(2,1)}) %all-gather.20.cloned.1.call-update) | async-done | bytes 1310736 | tf_op jit(solution)/shard_map/all_gather | solution.py:121
  128.8 26.0 all-gather.1
  155.9 26.1 all-gather
  208.6 61.3 %all-gather.28.cloned.1.call-done = bf16[2560,2560]{1,0:T(8,128)(2,1)} async-done(((bf16[80,2560]{1,0:T(8,128)(2,1)}), bf16[2560,2560]{1,0:T(8,128)(2,1)}) %all-gather.28.cloned.1.call-update) | async-done | bytes 13107216 | tf_op jit(solution)/shard_map/all_gather | solution.py:119
  335.1 79.9 %all-gather.30.cloned.1.call-done = bf16[2560,2560]{0,1:T(8,128)(2,1)} async-done(((bf16[2560,80]{0,1:T(8,128)(2,1)}), bf16[2560,2560]{0,1:T(8,128)(2,1)}) %all-gather.30.cloned.1.call-update) | async-done | bytes 13107216 | tf_op jit(solution)/shard_map/all_gather | solution.py:122
  439.7 118.6 %all-gather.34.cloned.1.call-done = bf16[2560,1920]{1,0:T(8,128)(2,1)} async-done(((bf16[320,1920]{1,0:T(8,128)(2,1)}), bf16[2560,1920]{1,0:T(8,128)(2,1)}) %all-gather.34.cloned.1.call-update) | async-done | bytes 9830416 | tf_op jit(solution)/shard_map/all_gather | solution.py:126
  558.2 55.7 %all-gather.32.cloned.1.call-done = bf16[1536,2560]{1,0:T(8,128)(2,1)} async-done(((bf16[384,2560]{1,0:T(8,128)(2,1)}), bf16[1536,2560]{1,0:T(8,128)(2,1)}) %all-gather.32.cloned.1.call-update) | async-done | bytes 7864336 | tf_op jit(solution)/shard_map/all_gather | solution.py:178
  637.1 121.9 %all-gather.36.cloned.1.call-done = bf16[2560,1920]{1,0:T(8,128)(2,1)} async-done(((bf16[320,1920]{1,0:T(8,128)(2,1)}), bf16[2560,1920]{1,0:T(8,128)(2,1)}) %all-gather.36.cloned.1.call-update) | async-done | bytes 9830416 | tf_op jit(solution)/shard_map/all_gather | solution.py:127
  781.6 32.9 %all-gather.46.cloned.1.call-done = bf16[1,1,1536,2560]{3,2,1,0:T(8,128)(2,1)} async-done(((bf16[1,1,384,2560]{3,2,1,0:T(8,128)(2,1)}), bf16[1,1,1536,2560]{3,2,1,0:T(8,128)(2,1)}) %all-gather.46.cloned.1.call-update) | async-done | bytes 7864336 | tf_op jit(solution)/shard_map/all_gather | solution.py:190
  814.5 145.1 %all-gather.38.cloned.1.call-done = bf16[1920,2560]{0,1:T(8,128)(2,1)} async-done(((bf16[1920,320]{0,1:T(8,128)(2,1)}), bf16[1920,2560]{0,1:T(8,128)(2,1)}) %all-gather.38.cloned.1.call-update) | async-done | bytes 9830416 | tf_op jit(solution)/shard_map/all_gather | solution.py:128
  959.6 34.0 %multiply_convert_fusion.1 = (bf16[1536,1920]{1,0:T(8,128)(2,1)}, bf16[1536,1920]{1,0:T(8,128)(2,1)S(1)}, bf16[1536,1920]{1,0:T(8,128)(2,1)}) fusion(f32[1536,1920]{1,0:T(8,128)} %fusion.196, f32[1536,1920]{1,0:T(8,128)} %fusion.197, bf16[1920,2560]{0,1:T(8,128)(2,1)} %all-gather.38.cloned.1.call-done, ...), kind=kOutput, calls=%fused_computation.50 | convolution fusion | flops 15176171520 | bytes 58982400 | tf_op jit(solution)/shard_map/dot_general | solution.py:50
  1128.6 54.8 %all-gather.44.cloned.1.call-done = bf16[1536,2560]{1,0:T(8,128)(2,1)} async-done(((bf16[384,2560]{1,0:T(8,128)(2,1)}), bf16[1536,2560]{1,0:T(8,128)(2,1)}) %all-gather.44.cloned.1.call-update) | async-done | bytes 7864336 | tf_op jit(solution)/shard_map/all_gather | solution.py:178
  1240.8 33.9 %multiply_convert_fusion = (bf16[1536,1920]{1,0:T(8,128)(2,1)}, bf16[1536,1920]{1,0:T(8,128)(2,1)S(1)}, bf16[1536,1920]{1,0:T(8,128)(2,1)}) fusion(f32[1536,1920]{1,0:T(8,128)} %fusion.198, f32[1536,1920]{1,0:T(8,128)} %fusion.199, bf16[1920,2560]{0,1:T(8,128)(2,1)} %all-gather.38.cloned.1.call-done, ...), kind=kOutput, calls=%fused_computation.49 | convolution fusion | flops 15176171520 | bytes 58982400 | tf_op jit(solution)/shard_map/dot_general | solution.py:50
  1297.9 24.4 add_convert_fusion.3
  1396.0 66.9 %reduce-scatter.20.cloned.1.call-done = bf16[384,2560]{1,0:T(8,128)(2,1)} async-done(((bf16[1536,2560]{1,0:T(8,128)(2,1)}), bf16[384,2560]{1,0:T(8,128)(2,1)}) %reduce-scatter.20.cloned.1.call-update) | async-done | bytes 1966096 | tf_op jit(solution)/shard_map/reduce_scatter | solution.py:182
  1462.8 72.3 %reduce-scatter.22.cloned.1.call-done = bf16[384,2560]{1,0:T(8,128)(2,1)} async-done(((bf16[1536,2560]{1,0:T(8,128)(2,1)}), bf16[384,2560]{1,0:T(8,128)(2,1)}) %reduce-scatter.22.cloned.1.call-update) | async-done | bytes 1966096 | tf_op jit(solution)/shard_map/reduce_scatter | solution.py:182
  1578.8 27.7 fusion.5
  1606.5 30.9 fusion.7
  1650.7 25.9 dynamic_update_slice.6
  1692.7 29.2 fusion.2
  1721.9 31.3 fusion.4
  1784.1 25.9 dynamic_update_slice.7
  1896.8 26.3 add_convert_fusion.1
  1946.1 25.8 add_convert_fusion.2
  2104.8 125.9 %reduce-scatter.38.cloned.1.call-done = bf16[320,1920]{1,0:T(8,128)(2,1)} async-done(((bf16[2560,1920]{1,0:T(8,128)(2,1)}), bf16[320,1920]{1,0:T(8,128)(2,1)}) %reduce-scatter.38.cloned.1.call-update) | async-done | bytes 1228816 | tf_op jit(solution)/shard_map/reduce_scatter | solution.py:271
  2233.6 168.5 %reduce-scatter.36.cloned.1.call-done = bf16[320,1920]{1,0:T(8,128)(2,1)} async-done(((bf16[2560,1920]{1,0:T(8,128)(2,1)}), bf16[320,1920]{1,0:T(8,128)(2,1)}) %reduce-scatter.36.cloned.1.call-update) | async-done | bytes 1228816 | tf_op jit(solution)/shard_map/reduce_scatter | solution.py:268
  2416.4 40.3 %all-reduce.4 = (f32[2560]{0:T(1024)S(1)}, f32[2560]{0:T(1024)S(1)}) all-reduce(f32[2560]{0:T(1024)S(1)} %add.271, f32[2560]{0:T(1024)S(1)} %add.276), channel_id=12, replica_groups=mesh['ctx'=8,'wt'=4] {'ctx','wt'}, use_global_device_ids=true, to_apply=%region_26.27.clone | all-reduce | flops 5120 | bytes 40960
  2469.6 72.5 %reduce-scatter.32.cloned.1.call-done = f32[80,256]{1,0:T(8,128)} async-done(((f32[2560,256]{1,0:T(8,128)}), f32[80,256]{1,0:T(8,128)}) %reduce-scatter.32.cloned.1.call-update) | async-done | bytes 81936 | tf_op jit(solution)/shard_map/reduce_scatter | solution.py:263
  2542.1 136.5 %reduce-scatter.30.cloned.1.call-done = f32[80,256]{1,0:T(8,128)} async-done(((f32[2560,256]{1,0:T(8,128)}), f32[80,256]{1,0:T(8,128)}) %reduce-scatter.30.cloned.1.call-update) | async-done | bytes 81936 | tf_op jit(solution)/shard_map/reduce_scatter | solution.py:262
  2678.6 277.4 %reduce-scatter.34.cloned.1.call-done = f32[80,2560]{1,0:T(8,128)} async-done(((f32[2560,2560]{1,0:T(8,128)}), f32[80,2560]{1,0:T(8,128)}) %reduce-scatter.34.cloned.1.call-update) | async-done | bytes 819216 | tf_op jit(solution)/shard_map/reduce_scatter | solution.py:264
  2956.0 288.2 %reduce-scatter.28.cloned.1.call-done = f32[80,2560]{1,0:T(8,128)} async-done(((f32[2560,2560]{1,0:T(8,128)}), f32[80,2560]{1,0:T(8,128)}) %reduce-scatter.28.cloned.1.call-update) | async-done | bytes 819216 | tf_op jit(solution)/shard_map/reduce_scatter | solution.py:261
  (391 shorter events, 855.2 us)
Async XLA Ops:
  7.2 60.7 %all-gather.24.cloned.1.call-start = ((), (), s32[]{:S(2)}) async-start(), calls=%async_computation.15 | async-start | bytes 1351680 | tf_op jit(solution)/shard_map/all_gather | solution.py:120
  7.9 116.1 %all-gather.20.cloned.1.call-start = ((), (), s32[]{:S(2)}) async-start(), calls=%async_computation.13 | async-start | bytes 1351680 | tf_op jit(solution)/shard_map/all_gather | solution.py:121
  8.7 196.8 %all-gather.26.cloned.1.call-start = ((), (), s32[]{:S(2)}) async-start(), calls=%async_computation.16 | async-start | bytes 1769472 | tf_op jit(solution)/shard_map/all_gather | solution.py:155
  52.7 384.0 %copy-start.44 = (f32[2560]{0:T(1024)}, f32[2560]{0:T(1024)S(1)}, u32[]{:S(2)}) copy-start(f32[2560]{0:T(1024)S(1)} %convert_element_type.243) | copy-start | bytes 30724
  57.0 230.6 %copy-start.57 = (f32[384]{0:T(512)}, f32[384]{0:T(512)S(1)}, u32[]{:S(2)}) copy-start(f32[384]{0:T(512)S(1)} %fusion.154) | copy-start | bytes 4612
  71.2 198.7 %all-gather.28.cloned.1.call-start = ((), (), s32[]{:S(2)}) async-start(), calls=%async_computation.17 | async-start | bytes 13516800 | tf_op jit(solution)/shard_map/all_gather | solution.py:119
  71.8 247.6 %all-gather.22.cloned.1.call-start = ((), (), s32[]{:S(2)}) async-start(), calls=%async_computation.14 | async-start | bytes 1769472 | tf_op jit(solution)/shard_map/all_gather | solution.py:156
  127.4 287.6 %all-gather.30.cloned.1.call-start = ((), (), s32[]{:S(2)}) async-start(), calls=%async_computation.18 | async-start | bytes 13516800 | tf_op jit(solution)/shard_map/all_gather | solution.py:122
  127.9 430.3 %all-gather.34.cloned.1.call-start = ((), (), s32[]{:S(2)}) async-start(), calls=%async_computation.20 | async-start | bytes 11059200 | tf_op jit(solution)/shard_map/all_gather | solution.py:126
  128.7 485.2 %all-gather.32.cloned.1.call-start = ((), (), s32[]{:S(2)}) async-start(), calls=%async_computation.19 | async-start | bytes 9830400 | tf_op jit(solution)/shard_map/all_gather | solution.py:178
  427.4 331.6 %all-gather.36.cloned.1.call-start = ((), (), s32[]{:S(2)}) async-start(), calls=%async_computation.21 | async-start | bytes 11059200 | tf_op jit(solution)/shard_map/all_gather | solution.py:127
  428.2 386.3 %all-gather.46.cloned.1.call-start = ((), (), s32[]{:S(2)}) async-start(), calls=%async_computation.36 | async-start | bytes 9830400 | tf_op jit(solution)/shard_map/all_gather | solution.py:190
  432.7 526.9 %all-gather.38.cloned.1.call-start = ((), (), s32[]{:S(2)}) async-start(), calls=%async_computation.22 | async-start | bytes 11059200 | tf_op jit(solution)/shard_map/all_gather | solution.py:128
  433.4 610.8 %all-gather.42.cloned.1.call-start = ((), (), s32[]{:S(2)}) async-start(), calls=%async_computation.25 | async-start | bytes 1769472 | tf_op jit(solution)/shard_map/all_gather | solution.py:155
  436.6 643.7 %all-gather.40.cloned.1.call-start = ((), (), s32[]{:S(2)}) async-start(), calls=%async_computation.24 | async-start | bytes 1769472 | tf_op jit(solution)/shard_map/all_gather | solution.py:156
  439.6 681.0 %reduce-scatter.24.cloned.1.call-start = ((), (), s32[]{:S(2)}) async-start(), calls=%async_computation.28 | async-start | bytes 9830400 | tf_op jit(solution)/shard_map/reduce_scatter | solution.py:198
  1041.2 142.2 %all-gather.44.cloned.1.call-start = ((), (), s32[]{:S(2)}) async-start(), calls=%async_computation.26 | async-start | bytes 9830400 | tf_op jit(solution)/shard_map/all_gather | solution.py:178
  1127.9 112.9 %all-gather.48.cloned.1.call-start = ((), (), s32[]{:S(2)}) async-start(), calls=%async_computation.37 | async-start | bytes 9830400 | tf_op jit(solution)/shard_map/all_gather | solution.py:190
  1128.5 262.9 %reduce-scatter.26.cloned.1.call-start = ((), (), s32[]{:S(2)}) async-start(), calls=%async_computation.29 | async-start | bytes 9830400 | tf_op jit(solution)/shard_map/reduce_scatter | solution.py:198
  1322.3 140.5 %reduce-scatter.20.cloned.1.call-start = ((), (), s32[]{:S(2)}) async-start(), calls=%async_computation.23 | async-start | bytes 9830400 | tf_op jit(solution)/shard_map/reduce_scatter | solution.py:182
  1345.0 190.2 %reduce-scatter.22.cloned.1.call-start = ((), (), s32[]{:S(2)}) async-start(), calls=%async_computation.27 | async-start | bytes 9830400 | tf_op jit(solution)/shard_map/reduce_scatter | solution.py:182
  1368.6 603.8 %reduce-scatter.40.cloned.1.call-start = ((), (), s32[]{:S(2)}) async-start(), calls=%async_computation.38 | async-start | bytes 3538944
  1679.4 295.7 %reduce-scatter.42.cloned.1.call-start = ((), (), s32[]{:S(2)}) async-start(), calls=%async_computation.39 | async-start | bytes 3538944
  1812.8 285.6 %reduce-scatter.44.cloned.1.call-start = ((), (), s32[]{:S(2)}) async-start(), calls=%async_computation.40 | async-start | bytes 11059200
  1874.0 356.8 %reduce-scatter.38.cloned.1.call-start = ((), (), s32[]{:S(2)}) async-start(), calls=%async_computation.35 | async-start | bytes 11059200 | tf_op jit(solution)/shard_map/reduce_scatter | solution.py:271
  1923.1 479.0 %reduce-scatter.36.cloned.1.call-start = ((), (), s32[]{:S(2)}) async-start(), calls=%async_computation.34 | async-start | bytes 11059200 | tf_op jit(solution)/shard_map/reduce_scatter | solution.py:268
  1971.9 570.2 %reduce-scatter.32.cloned.1.call-start = ((), (), s32[]{:S(2)}) async-start(), calls=%async_computation.32 | async-start | bytes 2703360 | tf_op jit(solution)/shard_map/reduce_scatter | solution.py:263
  1979.4 699.2 %reduce-scatter.30.cloned.1.call-start = ((), (), s32[]{:S(2)}) async-start(), calls=%async_computation.31 | async-start | bytes 2703360 | tf_op jit(solution)/shard_map/reduce_scatter | solution.py:262
  1985.2 970.8 %reduce-scatter.34.cloned.1.call-start = ((), (), s32[]{:S(2)}) async-start(), calls=%async_computation.33 | async-start | bytes 27033600 | tf_op jit(solution)/shard_map/reduce_scatter | solution.py:264
  2018.9 1225.3 %reduce-scatter.28.cloned.1.call-start = ((), (), s32[]{:S(2)}) async-start(), calls=%async_computation.30 | async-start | bytes 27033600 | tf_op jit(solution)/shard_map/reduce_scatter | solution.py:261
  2104.8 300.2 %copy-start.18 = (bf16[2560,256]{1,0:T(8,128)(2,1)S(1)}, bf16[2560,256]{1,0:T(8,128)(2,1)}, u32[]{:S(2)}) copy-start(bf16[2560,256]{1,0:T(8,128)(2,1)} %all-gather.24.cloned.1.call-done) | copy-start | bytes 3932164
  2104.8 300.2 %copy-start.52 = (bf16[384,512]{1,0:T(8,128)(2,1)S(1)}, bf16[384,512]{1,0:T(8,128)(2,1)}, u32[]{:S(2)}) copy-start(bf16[384,512]{1,0:T(8,128)(2,1)} %reduce-scatter.40.cloned.1.call-done) | copy-start | bytes 1179652
  (88 other events, 1610.3 us)
Sparse Core Ops, SparseCore 0:
  10.9 56.9 all-gather.23
  70.8 53.2 all-gather.19
  126.8 42.9 all-gather.25
  172.5 97.3 all-gather.27
  272.5 42.3 all-gather.21
  317.6 97.2 all-gather.29
  417.2 141.0 all-gather.33
  560.4 53.4 all-gather.31
  616.1 142.8 all-gather.35
  761.0 53.4 all-gather.45
  816.7 142.8 all-gather.37
  961.6 42.3 all-gather.41
  1006.8 42.9 all-gather.39
  1052.8 67.7 reduce-scatter.23
  1128.0 55.3 all-gather.43
  1185.5 55.3 all-gather.47
  1322.4 68.9 reduce-scatter.25
  1393.8 68.9 reduce-scatter.19
  1466.1 68.9 reduce-scatter.21
  1679.5 74.1 reduce-scatter.39
  1813.0 74.4 reduce-scatter.41
  1891.1 168.0 reduce-scatter.43
  2062.8 167.8 reduce-scatter.37
  2234.2 167.8 reduce-scatter.35
  2405.0 137.0 reduce-scatter.31
  2544.8 133.7 reduce-scatter.29
  2681.3 274.6 reduce-scatter.33
  2958.9 285.2 reduce-scatter.27
where the time goes:
time: 3260 us; the launch traced here: 3250 us
  waiting for transfers between devices  2000 us (61%)
  matrix products  818 us (25%)
  other arithmetic  155 us (5%)
  blocking collectives  135 us (4%)
  local copies, waits for them, and re-layouts  131 us (4%)
    reduce_scatter x1, waiting for transfers between devices, local(): lax.psum_scatter(attn_total[1], ('ctx', 'wt'), scatter_dimension=0, tiled...  288 us
    reduce_scatter x1, waiting for transfers between devices, local(): lax.psum_scatter(attn_total[4], ('ctx', 'wt'), scatter_dimension=0, tiled...  277 us
    dot_general x14, matrix products, contract_rows(): lax.dot_general(left, right, (((0,), (0,)), ((), ())), preferred_element_...  222 us
    dot_general x14, matrix products, contract_last(): lax.dot_general(left, right, (((1,), (1,)), ((), ())), preferred_element_...  210 us
    reduce_scatter x1, waiting for transfers between devices, local(): lax.psum_scatter(mlp_total[0].astype(jnp.bfloat16), 'ctx', scatter_dimens...  169 us
    all_gather x1, waiting for transfers between devices, local(): lax.all_gather(w_down, 'ctx', axis=1, tiled=True)  145 us
    reduce_scatter x2, waiting for transfers between devices, local(): lax.psum_scatter(jnp.dot(hidden, down_full, preferred_element_type=jnp.fl...  139 us
    reduce_scatter x1, waiting for transfers between devices, local(): lax.psum_scatter(attn_total[2], ('ctx', 'wt'), scatter_dimension=0, tiled...  136 us
  transfers between devices with their start and end apart: 28, of which 21 were waited for; matrix products, arithmetic and copies ran while one was open for 26% of the time, Pallas kernels for 0%

commit v1 on v0

v1 whole, which is shorter than its diff:
```python
import functools
import math

import jax
import jax.numpy as jnp
from jax import lax
from jax.experimental import pallas as pl
from jax.experimental.pallas import tpu as pltpu
from jax.sharding import PartitionSpec as P

WINDOW = 2048
EPSILON = 1e-06
NEGATIVE = -1e30
LOG2E = math.log2(math.e)
LN2 = math.log(2.0)
F32 = jnp.float32
BF16 = jnp.bfloat16


def rms_scale(values, gain):
    return values * lax.rsqrt(jnp.mean(values * values, axis=-1, keepdims=True) + EPSILON) * gain


def dot(left, right, out=F32):
    return jnp.dot(left, right, preferred_element_type=out)


def contract_rows(left, right, out=F32):
    return lax.dot_general(left, right, (((0,), (0,)), ((), ())), preferred_element_type=out)


def contract_last(left, right, out=F32):
    return lax.dot_general(left, right, (((1,), (1,)), ((), ())), preferred_element_type=out)


def ring_order(count):
    return list(range(0, count, 2)) + [i for i in range(count - 1, 0, -1) if i % 2]


def ring_step(block, shift):
    count = lax.axis_size("ctx")
    order = ring_order(count)
    return lax.ppermute(
        block, "ctx", [(order[i], order[(i + shift) % count]) for i in range(count)]
    )


def ring_index(offset):
    count = lax.axis_size("ctx")
    order = ring_order(count)
    place = [order.index(i) for i in range(count)]
    here = jnp.asarray(place, jnp.int32)[lax.axis_index("ctx")]
    return jnp.asarray(order, jnp.int32)[(here + offset) % count]


def ring_gather(block):
    count = lax.axis_size("ctx")
    half = count // 2
    cut = block.shape[0] // 2 // 8 * 8
    found = jnp.zeros((count,) + block.shape, block.dtype)

    def put(found, piece, offset, row):
        start = (ring_index(offset), row) + (0,) * (block.ndim - 1)
        return lax.dynamic_update_slice(found, piece[None], start)

    found = put(found, block, 0, 0)
    ahead = behind = block
    for step in range(1, half):
        ahead = ring_step(ahead, 1)
        behind = ring_step(behind, -1)
        found = put(found, ahead, -step, 0)
        found = put(found, behind, step, 0)
    low = ring_step(ahead[:cut], 1)
    high = ring_step(behind[cut:], -1)
    found = put(found, low, half, 0)
    found = put(found, high, half, cut)
    return found


def ring_scatter(terms):
    count = terms.shape[0]
    half = count // 2
    cut = terms.shape[1] // 2 // 8 * 8

    def own(offset):
        return lax.dynamic_index_in_dim(terms, ring_index(offset), 0, keepdims=False)

    def add(first, second):
        return (first.astype(F32) + second.astype(F32)).astype(BF16)

    far = own(half)
    ahead = ring_step(far[:cut], 1)
    behind = ring_step(far[cut:], -1)
    if half == 1:
        return own(0).astype(F32) + jnp.concatenate([ahead, behind], axis=0).astype(F32)
    for step in range(half - 1, 0, -1):
        up, down = own(step), own(-step)
        if step == half - 1:
            up = jnp.concatenate([add(up[:cut], ahead), up[cut:]], axis=0)
            down = jnp.concatenate([down[:cut], add(down[cut:], behind)], axis=0)
        else:
            up, down = add(up, ahead), add(down, behind)
        ahead = ring_step(up, 1)
        behind = ring_step(down, -1)
    return own(0).astype(F32) + ahead.astype(F32) + behind.astype(F32)


def wt_swap(block, bit):
    count = lax.axis_size("wt")
    return lax.ppermute(block, "wt", [(i, i ^ bit) for i in range(count)])


def core_swap(block):
    return wt_swap(block, 1)


def x_swap(block):
    return wt_swap(block, 2)


def gather_everywhere(block):
    here = lax.axis_index("wt")
    rows, width = block.shape
    mine = ring_gather(block)
    far = x_swap(mine)
    found = jnp.zeros((mine.shape[0], 4, rows, width), block.dtype)
    for piece, bit in ((mine, 0), (far, 2), (core_swap(mine), 1), (core_swap(far), 3)):
        found = lax.dynamic_update_slice(found, piece[:, None], (0, here ^ bit, 0, 0))
    return found.reshape(-1, width)


def scatter_everywhere(terms):
    here = lax.axis_index("wt")
    count = lax.axis_size("ctx")
    rows = terms.shape[0] // (4 * count)
    split = terms.reshape(count, 2, 2, rows, terms.shape[1])
    x_here, core_here = here // 2, here % 2
    kept = lax.dynamic_index_in_dim(split, core_here, 2, keepdims=False)
    sent = lax.dynamic_index_in_dim(split, 1 - core_here, 2, keepdims=False)
    both = (kept.astype(F32) + core_swap(sent).astype(F32)).astype(BF16)
    kept = lax.dynamic_index_in_dim(both, x_here, 1, keepdims=False)
    sent = lax.dynamic_index_in_dim(both, 1 - x_here, 1, keepdims=False)
    return ring_scatter((kept.astype(F32) + x_swap(sent).astype(F32)).astype(BF16))


def gather_wt(block):
    chip = jnp.concatenate([block, x_swap(block)], axis=0)
    return jnp.concatenate([chip, core_swap(chip)], axis=0)


def scatter_wt(terms):
    rows = terms.shape[0] // 4
    other = core_swap(terms[2 * rows :])
    far = (terms[rows : 2 * rows].astype(F32) + other[rows:].astype(F32)).astype(BF16)
    near = terms[:rows].astype(F32) + other[:rows].astype(F32)
    return near + x_swap(far).astype(F32)


def rotate(values, cosine, sine):
    half = values.shape[-1] // 2
    first, second = values[:, :half], values[:, half:]
    return jnp.concatenate(
        [first * cosine - second * sine, second * cosine + first * sine], axis=-1
    )


def visible(start, keys, low, high):
    index = start + lax.broadcasted_iota(jnp.int32, (keys, low.shape[1]), 0)
    return (index >= low) & (index <= high)


def attend_kernel(
    spans, q_ref, kv_ref, low_ref, high_ref, cos_ref, sin_ref,
    out_ref, qrot_ref, lse_ref, vt_ref, *, heads, size, keys,
):
    rows = q_ref.shape[0]
    scale = size ** -0.5 * LOG2E

    @pl.when(pl.program_id(0) == 0)
    def _():
        vt_ref[...] = kv_ref[:, size:].T

    turned = []
    for head in range(heads):
        part = rotate(q_ref[:, head * size : (head + 1) * size], cos_ref[...], sin_ref[...])
        part = (part * scale).astype(BF16)
        qrot_ref[:, head * size : (head + 1) * size] = part
        turned.append(part.T)
    qt = jnp.concatenate(turned, axis=1)
    low, high = low_ref[...], high_ref[...]

    def step(block, carry, masked):
        top, total, acc = carry
        start = pl.multiple_of(block * keys, keys)
        scores = dot(kv_ref[pl.ds(start, keys), :size], qt)
        if masked:
            scores = jnp.where(visible(start, keys, low, high), scores, NEGATIVE)
        new_top = jnp.maximum(top, jnp.max(scores, axis=0, keepdims=True))
        probs = jnp.exp2(scores - new_top)
        fade = jnp.exp2(top - new_top)
        total = total * fade + jnp.sum(probs, axis=0, keepdims=True)
        acc = acc * fade + dot(vt_ref[:, pl.ds(start, keys)], probs.astype(BF16))
        return new_top, total, acc

    carry = (
        jnp.full((1, heads * rows), NEGATIVE, F32),
        jnp.zeros((1, heads * rows), F32),
        jnp.zeros((size, heads * rows), F32),
    )
    carry = lax.fori_loop(spans[0], spans[1], functools.partial(step, masked=True), carry)
    carry = lax.fori_loop(spans[2], spans[3], functools.partial(step, masked=False), carry)
    carry = lax.fori_loop(spans[4], spans[5], functools.partial(step, masked=True), carry)
    top, total, acc = carry
    acc = acc * (1.0 / total)
    lse_ref[0] = top + jnp.log2(total)
    for head in range(heads):
        out_ref[:, head * size : (head + 1) * size] = (
            acc[:, head * rows : (head + 1) * rows].astype(BF16).T
        )


def attend_back_kernel(
    spans, q_ref, kv_ref, low_ref, high_ref, cos_ref, sin_ref, out_ref, grad_ref, lse_ref,
    dq_ref, dkv_ref, kt_ref, dk_ref, dv_ref, *, heads, size, keys,
):
    rows = q_ref.shape[0]

    @pl.when(pl.program_id(0) == 0)
    def _():
        kt_ref[...] = kv_ref[:, :size].T
        dk_ref[...] = jnp.zeros_like(dk_ref)
        dv_ref[...] = jnp.zeros_like(dv_ref)

    parts = [slice(head * size, (head + 1) * size) for head in range(heads)]
    q = jnp.concatenate([q_ref[:, part] for part in parts], axis=0)
    grad = jnp.concatenate([grad_ref[:, part] for part in parts], axis=0)
    out_t = jnp.concatenate([out_ref[:, part].T for part in parts], axis=1)
    qt, grad_t = q.T, grad.T
    delta = jnp.sum(grad_t.astype(F32) * out_t.astype(F32), axis=0, keepdims=True)
    low, high, lse = low_ref[...], high_ref[...], lse_ref[0]

    def step(block, dq, masked):
        start = pl.multiple_of(block * keys, keys)
        here = pl.ds(start, keys)
        scores = dot(kv_ref[here, :size], qt)
        if masked:
            scores = jnp.where(visible(start, keys, low, high), scores, NEGATIVE)
        probs = jnp.exp2(scores - lse)
        probs_grad = dot(kv_ref[here, size:], grad_t)
        score_grad = (probs * (probs_grad - delta)).astype(BF16)
        dv_ref[here, :] += dot(probs.astype(BF16), grad)
        dk_ref[here, :] += dot(score_grad, q)
        return dq + dot(kt_ref[:, here], score_grad)

    dq = jnp.zeros((size, heads * rows), F32)
    dq = lax.fori_loop(spans[0], spans[1], functools.partial(step, masked=True), dq)
    dq = lax.fori_loop(spans[2], spans[3], functools.partial(step, masked=False), dq)
    dq = lax.fori_loop(spans[4], spans[5], functools.partial(step, masked=True), dq)
    for head, part in enumerate(parts):
        turned = rotate(dq[:, head * rows : (head + 1) * rows].T, cos_ref[...], -sin_ref[...])
        dq_ref[:, part] = (turned * size ** -0.5).astype(BF16)

    @pl.when(pl.program_id(0) == pl.num_programs(0) - 1)
    def _():
        dkv_ref[:, :size] = (dk_ref[...] * LN2).astype(BF16)
        dkv_ref[:, size:] = dv_ref[...].astype(BF16)


def attention_calls(rows, width, size, total, keys):
    heads = 2 if (width // size) % 2 == 0 else 1
    groups = width // size // heads
    span = heads * size
    head_block = pl.BlockSpec((rows, span), lambda g, s: (0, g))

    def whole(*shape):
        return pl.BlockSpec(shape, lambda g, s: (0,) * len(shape))

    lse_block = pl.BlockSpec((1, 1, heads * rows), lambda g, s: (g, 0, 0))
    shared = [
        head_block, whole(total, 2 * size), whole(1, heads * rows), whole(1, heads * rows),
        whole(rows, size // 2), whole(rows, size // 2),
    ]
    lse_shape = jax.ShapeDtypeStruct((groups, 1, heads * rows), F32)
    row_shape = jax.ShapeDtypeStruct((rows, width), BF16)
    params = pltpu.CompilerParams(vmem_limit_bytes=48 * 2**20)
    work = rows * width * min(total, WINDOW) * 2
    sizes = dict(heads=heads, size=size, keys=keys)
    forward = pl.pallas_call(
        functools.partial(attend_kernel, **sizes),
        out_shape=(row_shape, row_shape, lse_shape),
        grid_spec=pltpu.PrefetchScalarGridSpec(
            num_scalar_prefetch=1, grid=(groups,), in_specs=shared,
            out_specs=(head_block, head_block, lse_block),
            scratch_shapes=[pltpu.VMEM((size, total), BF16)],
        ),
        compiler_params=params,
        cost_estimate=pl.CostEstimate(
            flops=2 * work, bytes_accessed=rows * width * 8, transcendentals=work // size // 2
        ),
    )
    backward = pl.pallas_call(
        functools.partial(attend_back_kernel, **sizes),
        out_shape=(row_shape, jax.ShapeDtypeStruct((total, 2 * size), BF16)),
        grid_spec=pltpu.PrefetchScalarGridSpec(
            num_scalar_prefetch=1, grid=(groups,),
            in_specs=shared + [head_block, head_block, lse_block],
            out_specs=(head_block, whole(total, 2 * size)),
            scratch_shapes=[
                pltpu.VMEM((size, total), BF16),
                pltpu.VMEM((total, size), F32),
                pltpu.VMEM((total, size), F32),
            ],
        ),
        compiler_params=params,
        cost_estimate=pl.CostEstimate(
            flops=5 * work, bytes_accessed=rows * width * 10, transcendentals=work // size // 2
        ),
    )
    return forward, backward, heads


def pad_rows(array, rows):
    return jnp.pad(array, ((0, rows - array.shape[0]), (0, 0)))


def local(
    tokens, segment_ids, cotangent, gain_attn, w_query, w_key, w_value, w_out, gain_mlp,
    w_gate, w_up, w_down,
):
    micros, _, rows, width = tokens.shape
    size = w_key.shape[1]
    count = lax.axis_size("ctx")
    total = rows * count
    first = lax.axis_index("ctx") * rows
    padded = -(-rows // 128) * 128
    keys = min(384, total)
    forward, backward, heads = attention_calls(padded, w_query.shape[1], size, total, keys)

    ids = segment_ids[:, 0]
    ids_all = lax.all_gather(ids, "ctx", axis=1, tiled=True)

    gains = jnp.stack([gain_attn, gain_mlp], axis=1)
    narrow = jnp.concatenate([w_key, w_value, jnp.pad(gains, ((0, 0), (0, 126)))], axis=1)
    narrow = gather_everywhere(narrow)
    w_kv = narrow[:, : 2 * size]
    gain_first = narrow[:, 2 * size].astype(F32)
    gain_second = narrow[:, 2 * size + 1].astype(F32)
    query_full = gather_everywhere(w_query)
    out_full = gather_everywhere(w_out.T)

    index = first + jnp.arange(rows, dtype=jnp.int32)
    begins = jnp.sum(
        (ids_all[:, None, :] < ids[:, :, None]).astype(jnp.int32), axis=-1, dtype=jnp.int32
    )
    position = (index[None] - begins).astype(F32)
    half = size // 2
    freqs = 10000.0 ** (-jnp.arange(half, dtype=F32) / half)
    angles = position[:, :, None] * freqs
    cosine, sine = jnp.cos(angles), jnp.sin(angles)
    lowest = jnp.maximum(begins, index[None] - (WINDOW - 1))

    inputs = tokens[:, 0].astype(F32)
    normed = rms_scale(inputs, gain_first).astype(BF16).reshape(micros * rows, width)
    kv = dot(normed, w_kv, BF16).reshape(micros, rows, 2 * size)
    queries = dot(normed, query_full).reshape(micros, rows, -1)

    saved = []
    middles = []
    mlp_rows = []
    for m in range(micros):
        key_rot = rotate(kv[m, :, :size].astype(F32), cosine[m], sine[m]).astype(BF16)
        kv_all = ring_gather(jnp.concatenate([key_rot, kv[m, :, size:]], axis=1))
        kv_all = kv_all.reshape(total, 2 * size)
        full_from = (jnp.max(lowest[m]) + keys - 1) // keys
        full_to = (first + 1) // keys
        last = (first + rows - 1) // keys + 1
        spans = jnp.stack([
            jnp.min(lowest[m]) // keys, jnp.minimum(full_from, last),
            full_from, full_to,
            jnp.maximum(full_from, full_to), last,
        ]).astype(jnp.int32)

        def lanes(values):
            return jnp.tile(jnp.pad(values, (0, padded - rows))[None], (1, heads))

        shared = (
            kv_all, lanes(lowest[m]), lanes(index),
            pad_rows(cosine[m], padded), pad_rows(sine[m], padded),
        )
        attended, query_rot, lse = forward(spans, pad_rows(queries[m], padded), *shared)
        saved.append((spans, query_rot, shared, attended, lse))
        middle = inputs[m] + contract_last(attended[:rows], out_full)
        middles.append(middle)
        mlp_rows.append(rms_scale(middle, gain_second).astype(BF16))

    normed_all = gather_wt(jnp.concatenate(mlp_rows, axis=0))
    cot_all = gather_wt(cotangent.reshape(micros * rows, width))
    hidden_cols = w_gate.shape[1]
    gate_full = ring_gather(w_gate).reshape(width, hidden_cols)
    up_full = ring_gather(w_up).reshape(width, hidden_cols)
    down_full = ring_gather(w_down.T).reshape(width, hidden_cols)

    gate_rows = dot(normed_all, gate_full)
    up_rows = dot(normed_all, up_full)
    hidden = (jax.nn.gelu(gate_rows) * up_rows).astype(BF16)

    def scatter_weight(left, right):
        return ring_scatter(contract_rows(left, right, BF16).reshape(count, -1, hidden_cols))

    grad_down = scatter_weight(cot_all, hidden).T
    hidden_grad = dot(cot_all, down_full)
    gelu_gate, gelu_back = jax.vjp(jax.nn.gelu, gate_rows)
    gate_grad = gelu_back(hidden_grad * up_rows)[0].astype(BF16)
    up_grad = (hidden_grad * gelu_gate).astype(BF16)
    mlp_in_grad = scatter_wt(
        (contract_last(gate_grad, gate_full) + contract_last(up_grad, up_full)).astype(BF16)
    ).reshape(micros, rows, width)
    grad_gate = scatter_weight(normed_all, gate_grad)
    grad_up = scatter_weight(normed_all, up_grad)
    mlp_out = scatter_wt(contract_last(hidden, down_full, BF16)).reshape(micros, rows, width)
    output = jnp.stack(middles) + mlp_out

    middle_grads, query_grads, key_value_grads, branch_grads, gain_two = [], [], [], [], []
    for m in range(micros):
        spans, query_rot, shared, attended, lse = saved[m]
        norm_back = jax.vjp(rms_scale, middles[m], gain_second)[1]
        middle_part, gain_part = norm_back(mlp_in_grad[m])
        gain_two.append(gain_part)
        middle_grad = middle_part + cotangent[m, 0].astype(F32)
        middle_grads.append(middle_grad)
        branch_grad = middle_grad.astype(BF16)
        branch_grads.append(branch_grad)
        attended_grad = dot(branch_grad, out_full, BF16)
        query_grad, kv_term = backward(
            spans, query_rot, *shared, attended, pad_rows(attended_grad, padded), lse
        )
        query_grads.append(query_grad[:rows])
        kv_own = ring_scatter(kv_term.reshape(count, rows, 2 * size))
        key_own = rotate(kv_own[:, :size], cosine[m], -sine[m])
        key_value_grads.append(jnp.concatenate([key_own, kv_own[:, size:]], axis=1).astype(BF16))

    query_grad = jnp.concatenate(query_grads, axis=0)
    kv_grad = jnp.concatenate(key_value_grads, axis=0)
    attended = jnp.concatenate([entry[3][:rows] for entry in saved], axis=0)
    grad_out = scatter_everywhere(
        contract_rows(jnp.concatenate(branch_grads, axis=0), attended, BF16)
    ).T
    grad_query = scatter_everywhere(contract_rows(normed, query_grad, BF16))

    attn_in_grad = contract_last(query_grad, query_full) + contract_last(kv_grad, w_kv)
    norm_back = jax.vjp(rms_scale, inputs, gain_first)[1]
    input_part, gain_one = norm_back(attn_in_grad.reshape(micros, rows, width))
    grad_tokens = jnp.stack(middle_grads) + input_part

    gain_cols = jnp.stack([gain_one, sum(gain_two)], axis=1).astype(BF16)
    narrow_grad = scatter_everywhere(
        jnp.concatenate(
            [contract_rows(normed, kv_grad, BF16), jnp.pad(gain_cols, ((0, 0), (0, 126)))], axis=1
        )
    )
    return (
        output[:, None],
        grad_tokens[:, None],
        narrow_grad[:, 2 * size],
        grad_query,
        narrow_grad[:, :size],
        narrow_grad[:, size : 2 * size],
        grad_out,
        narrow_grad[:, 2 * size + 1],
        grad_gate,
        grad_up,
        grad_down,
    )


def solution(mesh):
    rows = P(None, "wt", "ctx", None)
    everywhere = P(("ctx", "wt"))
    tall = P(("ctx", "wt"), None)
    wide = P(None, ("ctx", "wt"))
    square = P("ctx", "wt")
    return jax.shard_map(
        local,
        mesh=mesh,
        in_specs=(
            rows, P(None, "wt", "ctx"), rows, everywhere, tall, tall, tall, wide, everywhere,
            square, square, P("wt", "ctx"),
        ),
        out_specs=(
            rows, rows, everywhere, tall, tall, tall, wide, everywhere, square, square,
            P("wt", "ctx"),
        ),
        check_vma=False,
    )
```

time: 3260 us -> 2100 us (0.64)
  waiting for transfers between devices: 2000 us -> 760 us
  starting transfers between devices: 1.71 us -> 321 us
  matrix products: 818 us -> 507 us
  blocking collectives: 135 us -> 26.4 us
  local copies, waits for them, and re-layouts: 131 us -> 228 us
  Pallas kernels: 0 us -> 57.1 us
    reduce_scatter x10 -> x0, waiting for transfers between devices: 1240 us -> none  [the longest x1 288 us: local(): lax.psum_scatter(attn_total[1], ('ctx', 'wt'), scatter_dimension=0, tiled...]
    ppermute x0 -> x151, waiting for transfers between devices: none -> 760 us  [the longest x128 543 us: ring_step(): lax.ppermute(block, 'ctx', [(order[i], order[(i + shift) % count]) for i...]
    all_gather x15 -> x0, waiting for transfers between devices: 747 us -> none  [the longest x1 145 us: local(): lax.all_gather(w_down, 'ctx', axis=1, tiled=True)]
    ppermute x0 -> x151, starting transfers between devices: none -> 321 us  [the longest x128 296 us: ring_step(): lax.ppermute(block, 'ctx', [(order[i], order[(i + shift) % count]) for i...]
    dot_general x24 -> x7, matrix products: 347 us -> 189 us  [dot(): return jnp.dot(left, right, preferred_element_type=out)]
    unnamed x2 -> x0, blocking collectives: 82.6 us -> none
    dot_general x14 -> x6, matrix products: 222 us -> 150 us  [contract_rows(): lax.dot_general(left, right, (((0,), (0,)), ((), ())), preferred_element_...]
    pallas_call x0 -> x4, Pallas kernels: none -> 57.1 us  [the longest x2 33.3 us: local(): backward(spans, query_rot, *shared, attended, pad_rows(attended_grad, pad...]
  transfers between devices with their start and end apart: 28 -> 151, of which waited for: 21 -> 67; matrix products, arithmetic and copies ran while one was open for 26% -> 33% of each run, Pallas kernels for 0% -> 3%
where the time goes in v1:
time: 2100 us; the launch traced here: 2090 us
  waiting for transfers between devices  760 us (36%)
  matrix products  507 us (24%)
  starting transfers between devices  321 us (15%)
  local copies, waits for them, and re-layouts  228 us (11%)
  other arithmetic  156 us (7%)
  Pallas kernels  57.1 us (3%)
  between operations  30 us (1%)
  blocking collectives  26.4 us (1%)
    ppermute x128, waiting for transfers between devices, ring_step(): lax.ppermute(block, 'ctx', [(order[i], order[(i + shift) % count]) for i...  543 us
    ppermute x128, starting transfers between devices, ring_step(): lax.ppermute(block, 'ctx', [(order[i], order[(i + shift) % count]) for i...  296 us
    ppermute x23, waiting for transfers between devices, wt_swap(): return lax.ppermute(block, 'wt', [(i, i ^ bit) for i in range(count)])  217 us
    dot_general x7, matrix products, dot(): return jnp.dot(left, right, preferred_element_type=out)  189 us
    dot_general x7, matrix products, contract_last(): lax.dot_general(left, right, (((1,), (1,)), ((), ())), preferred_element_...  168 us
    dot_general x6, matrix products, contract_rows(): lax.dot_general(left, right, (((0,), (0,)), ((), ())), preferred_element_...  150 us
    dynamic_update_slice x67, local copies, waits for them, and re-layouts, put(): return lax.dynamic_update_slice(found, piece[None], start)  73.6 us
  transfers between devices with their start and end apart: 151, of which 67 were waited for; matrix products, arithmetic and copies ran while one was open for 33% of the time, Pallas kernels for 3%

profile of v1, /device:TPU:0, one launch (start us, length us, event | category | flops | bytes accessed | tf_op | source)
XLA Modules:
  0.0 2085.8 jit_solution(8732640562813718744)
XLA Ops:
  29.8 26.4 %all-gather = s32[2,1,3072]{2,1,0:T(1,128)S(1)} all-gather(s32[2,1,384]{2,1,0:T(1,128)} %param.285), channel_id=2, replica_groups=mesh['ctx'=8,'wt'=4] {'ctx'}, dimensions={2}, use_global_device_ids=true | all-gather | bytes 27648 | tf_op jit(solution)/shard_map/all_gather | solution.py:340
  145.1 42.8 %collective-permute-done.13 = bf16[80,2560]{1,0:T(8,128)(2,1)S(1)} collective-permute-done((bf16[80,2560]{1,0:T(8,128)(2,1)}, bf16[80,2560]{1,0:T(8,128)(2,1)S(1)}, u32[]{:S(2)}, u32[]{:S(2)}) %collective-permute-start.13) | collective-permute-done | bytes 409632 | tf_op jit(solution)/shard_map/ppermute | solution.py:43
  233.8 22.6 %collective-permute-done.16 = bf16[80,2560]{1,0:T(8,128)(2,1)S(1)} collective-permute-done((bf16[80,2560]{1,0:T(8,128)(2,1)S(1)}, bf16[80,2560]{1,0:T(8,128)(2,1)S(1)}, u32[]{:S(2)}, u32[]{:S(2)}) %collective-permute-start.16) | collective-permute-done | bytes 409632 | tf_op jit(solution)/shard_map/ppermute | solution.py:43
  366.6 18.6 collective-permute-done.69
  444.4 25.5 %collective-permute-done.19 = bf16[8,80,2560]{2,1,0:T(8,128)(2,1)} collective-permute-done((bf16[8,80,2560]{2,1,0:T(8,128)(2,1)}, bf16[8,80,2560]{2,1,0:T(8,128)(2,1)}, u32[]{:S(2)}, u32[]{:S(2)}) %collective-permute-start.19) | collective-permute-done | bytes 3276832 | tf_op jit(solution)/shard_map/ppermute | solution.py:110
  479.2 49.9 %collective-permute-done.38 = bf16[8,80,2560]{2,1,0:T(8,128)(2,1)} collective-permute-done((bf16[8,80,2560]{2,1,0:T(8,128)(2,1)}, bf16[8,80,2560]{2,1,0:T(8,128)(2,1)}, u32[]{:S(2)}, u32[]{:S(2)}) %collective-permute-start.38) | collective-permute-done | bytes 3276832 | tf_op jit(solution)/shard_map/ppermute | solution.py:110
  625.5 18.2 collective-permute-start.56
  677.4 17.5 collective-permute-start.74
  705.6 29.7 %collective-permute-done.49 = bf16[768,2560]{1,0:T(8,128)(2,1)S(1)} collective-permute-done((bf16[768,2560]{1,0:T(8,128)(2,1)S(1)}, bf16[768,2560]{1,0:T(8,128)(2,1)S(1)}, u32[]{:S(2)}, u32[]{:S(2)}) %collective-permute-start.49) | collective-permute-done | bytes 3932192 | tf_op jit(solution)/shard_map/ppermute | solution.py:110
  781.8 43.0 %fusion.23 = f32[3072,1920]{1,0:T(8,128)} fusion(bf16[2560,1920]{1,0:T(8,128)(2,1)} %bitcast.148, bf16[1536,2560]{1,0:T(8,128)(2,1)} %collective-permute-done.78, bf16[768,2560]{1,0:T(8,128)(2,1)} %collective-permute-done.77, bf16[768,2560]{1,0:T(8,128)(2,1)} %bitcast.150), kind=kOutput, calls=%fused_computation.53 | convolution fusion | flops 30246174720 | bytes 49152000 | tf_op jit(solution)/shard_map/dot_general | solution.py:25
  824.8 46.2 %fusion.123 = f32[3072,1920]{1,0:T(8,128)} fusion(bf16[2560,1920]{1,0:T(8,128)(2,1)} %bitcast.137, bf16[1536,2560]{1,0:T(8,128)(2,1)} %collective-permute-done.50, bf16[768,2560]{1,0:T(8,128)(2,1)} %copy-done.34, bf16[384,2560]{1,0:T(8,128)(2,1)S(1)} %get-tuple-element.149, bf16[384,2560]{1,0:T(8,128)(2,1)S(1)} %get-tuple-element.148), kind=kOutput, calls=%fused_computation.438 | convolution fusion | flops 30261903360 | bytes 49152000 | tf_op jit(solution)/shard_map/dot_general | solution.py:25
  871.0 65.3 %fusion.6 = (bf16[3072,1920]{1,0:T(8,128)(2,1)}, bf16[3072,1920]{1,0:T(8,128)(2,1)}, bf16[3072,1920]{1,0:T(8,128)(2,1)}) fusion(f32[3072,1920]{1,0:T(8,128)} %fusion.23, f32[3072,1920]{1,0:T(8,128)} %fusion.123, bf16[2560,1920]{1,0:T(8,128)(2,1)} %bitcast.127, bf16[1536,2560]{1,0:T(8,128)(2,1)} %collective-permute-done.50, bf16[768,2560]{1,0:T(8,128)(2,1)} %copy-done.34, ...), kind=kOutput, calls=%fused_computation.9 | convolution fusion | flops 30415257600 | bytes 108134400 | tf_op jit(solution)/shard_map/dot_general | solution.py:25
  936.3 39.6 %fusion.129 = bf16[3072,2560]{1,0:T(8,128)(2,1)} fusion(bf16[3072,1920]{1,0:T(8,128)(2,1)} %get-tuple-element.49, bf16[2560,1920]{1,0:T(8,128)(2,1)} %bitcast.148), kind=kOutput, calls=%fused_computation.444 | convolution fusion | flops 30198988800 | bytes 37355520 | tf_op jit(solution)/shard_map/dot_general | solution.py:33
  975.9 39.3 %fusion.22 = bf16[2560,1920]{1,0:T(8,128)(2,1)S(1)} fusion(bf16[3072,1920]{1,0:T(8,128)(2,1)} %get-tuple-element.49, bf16[1536,2560]{1,0:T(8,128)(2,1)} %collective-permute-done.78, bf16[768,2560]{1,0:T(8,128)(2,1)} %collective-permute-done.77, bf16[768,2560]{1,0:T(8,128)(2,1)} %bitcast.150), kind=kOutput, calls=%fused_computation.52 | convolution fusion | flops 30246174720 | bytes 37355520 | tf_op jit(solution)/shard_map/dot_general | solution.py:29
  1020.7 41.2 %fusion.130 = f32[3072,2560]{1,0:T(8,128)} fusion(bf16[3072,1920]{1,0:T(8,128)(2,1)} %get-tuple-element.48, bf16[2560,1920]{1,0:T(8,128)(2,1)} %bitcast.137), kind=kOutput, calls=%fused_computation.445 | convolution fusion | flops 30198988800 | bytes 53084160 | tf_op jit(solution)/shard_map/dot_general | solution.py:33
  1061.9 39.1 %fusion.121 = bf16[2560,1920]{1,0:T(8,128)(2,1)S(1)} fusion(bf16[3072,1920]{1,0:T(8,128)(2,1)} %get-tuple-element.48, bf16[1536,2560]{1,0:T(8,128)(2,1)} %collective-permute-done.50, bf16[768,2560]{1,0:T(8,128)(2,1)} %copy-done.34, bf16[384,2560]{1,0:T(8,128)(2,1)S(1)} %copy-done.18, bf16[384,2560]{1,0:T(8,128)(2,1)S(1)} %copy-done.16), kind=kOutput, calls=%fused_computation.436 | convolution fusion | flops 30261903360 | bytes 37355520 | tf_op jit(solution)/shard_map/dot_general | solution.py:29
  1108.7 42.8 %add_convert_fusion = bf16[3072,2560]{1,0:T(8,128)(2,1)} fusion(f32[3072,2560]{1,0:T(8,128)} %fusion.130, bf16[3072,1920]{1,0:T(8,128)(2,1)} %get-tuple-element.47, bf16[2560,1920]{1,0:T(8,128)(2,1)} %bitcast.127), kind=kOutput, calls=%fused_computation.2 | convolution fusion | flops 30214717440 | bytes 68812800 | tf_op jit(solution)/shard_map/dot_general | solution.py:33
  1158.5 40.4 %fusion.122 = bf16[2560,1920]{1,0:T(8,128)(2,1)} fusion(bf16[3072,1920]{1,0:T(8,128)(2,1)} %get-tuple-element.47, bf16[1536,2560]{1,0:T(8,128)(2,1)} %collective-permute-done.50, bf16[768,2560]{1,0:T(8,128)(2,1)} %copy-done.34, bf16[384,2560]{1,0:T(8,128)(2,1)S(1)} %copy-done.18, bf16[384,2560]{1,0:T(8,128)(2,1)S(1)} %copy-done.16), kind=kOutput, calls=%fused_computation.437 | convolution fusion | flops 30261903360 | bytes 37355520 | tf_op jit(solution)/shard_map/dot_general | solution.py:29
  1229.0 24.1 %collective-permute-done.148 = bf16[320,1920]{1,0:T(8,128)(2,1)S(1)} collective-permute-done((bf16[320,1920]{1,0:T(8,128)(2,1)S(1)}, bf16[320,1920]{1,0:T(8,128)(2,1)S(1)}, u32[]{:S(2)}, u32[]{:S(2)}) %collective-permute-start.148) | collective-permute-done | bytes 1228832 | tf_op jit(solution)/shard_map/ppermute | solution.py:43
  1257.3 21.6 %collective-permute-done.140 = bf16[320,1920]{1,0:T(8,128)(2,1)} collective-permute-done((bf16[320,1920]{1,0:T(8,128)(2,1)S(1)}, bf16[320,1920]{1,0:T(8,128)(2,1)}, u32[]{:S(2)}, u32[]{:S(2)}) %collective-permute-start.140) | collective-permute-done | bytes 1228832 | tf_op jit(solution)/shard_map/ppermute | solution.py:43
  1281.4 22.8 %collective-permute-done.128 = bf16[320,1920]{1,0:T(8,128)(2,1)S(1)} collective-permute-done((bf16[320,1920]{1,0:T(8,128)(2,1)S(1)}, bf16[320,1920]{1,0:T(8,128)(2,1)S(1)}, u32[]{:S(2)}, u32[]{:S(2)}) %collective-permute-start.128) | collective-permute-done | bytes 1228832 | tf_op jit(solution)/shard_map/ppermute | solution.py:43
  1306.1 24.6 %collective-permute-done.145 = bf16[320,1920]{1,0:T(8,128)(2,1)} collective-permute-done((bf16[320,1920]{1,0:T(8,128)(2,1)}, bf16[320,1920]{1,0:T(8,128)(2,1)}, u32[]{:S(2)}, u32[]{:S(2)}) %collective-permute-start.145) | collective-permute-done | bytes 1228832 | tf_op jit(solution)/shard_map/ppermute | solution.py:43
  1336.1 20.9 %collective-permute-done.137 = bf16[320,1920]{1,0:T(8,128)(2,1)} collective-permute-done((bf16[320,1920]{1,0:T(8,128)(2,1)S(1)}, bf16[320,1920]{1,0:T(8,128)(2,1)}, u32[]{:S(2)}, u32[]{:S(2)}) %collective-permute-start.137) | collective-permute-done | bytes 1228832 | tf_op jit(solution)/shard_map/ppermute | solution.py:43
  1362.3 21.1 %collective-permute-done.129 = bf16[320,1920]{1,0:T(8,128)(2,1)} collective-permute-done((bf16[320,1920]{1,0:T(8,128)(2,1)S(1)}, bf16[320,1920]{1,0:T(8,128)(2,1)}, u32[]{:S(2)}, u32[]{:S(2)}) %collective-permute-start.129) | collective-permute-done | bytes 1228832 | tf_op jit(solution)/shard_map/ppermute | solution.py:43
  1390.9 18.7 collective-permute-done.146
  1444.5 21.6 %collective-permute-done.150 = bf16[320,1920]{1,0:T(8,128)(2,1)} collective-permute-done((bf16[320,1920]{1,0:T(8,128)(2,1)}, bf16[320,1920]{1,0:T(8,128)(2,1)}, u32[]{:S(2)}, u32[]{:S(2)}) %collective-permute-start.150) | collective-permute-done | bytes 1228832 | tf_op jit(solution)/shard_map/ppermute | solution.py:43
  1472.1 20.4 collective-permute-done.142
  1496.4 21.7 %collective-permute-done.134 = bf16[320,1920]{1,0:T(8,128)(2,1)} collective-permute-done((bf16[320,1920]{1,0:T(8,128)(2,1)}, bf16[320,1920]{1,0:T(8,128)(2,1)}, u32[]{:S(2)}, u32[]{:S(2)}) %collective-permute-start.134) | collective-permute-done | bytes 1228832 | tf_op jit(solution)/shard_map/ppermute | solution.py:43
  1626.4 19.4 collective-permute-start.89
  1750.6 19.7 fusion.12
  1904.9 45.7 %collective-permute-done.118 = bf16[8,80,2560]{2,1,0:T(8,128)(2,1)S(1)} collective-permute-done((bf16[8,80,2560]{2,1,0:T(8,128)(2,1)}, bf16[8,80,2560]{2,1,0:T(8,128)(2,1)S(1)}, u32[]{:S(2)}, u32[]{:S(2)}) %collective-permute-start.118) | collective-permute-done | bytes 3276832 | tf_op jit(solution)/shard_map/ppermute | solution.py:110
  1960.0 56.7 %collective-permute-done.108 = bf16[8,80,2560]{2,1,0:T(8,128)(2,1)S(1)} collective-permute-done((bf16[8,80,2560]{2,1,0:T(8,128)(2,1)S(1)}, bf16[8,80,2560]{2,1,0:T(8,128)(2,1)S(1)}, u32[]{:S(2)}, u32[]{:S(2)}) %collective-permute-start.108) | collective-permute-done | bytes 3276832 | tf_op jit(solution)/shard_map/ppermute | solution.py:110
  (727 shorter events, 1048.6 us)
Async XLA Ops:
  2.9 99.9 %collective-permute-start = (bf16[80,640]{1,0:T(8,128)(2,1)}, bf16[80,640]{1,0:T(8,128)(2,1)S(1)}, u32[]{:S(2)}, u32[]{:S(2)}) collective-permute-start(bf16[80,640]{1,0:T(8,128)(2,1)} %fusion.107), channel_id=1, source_target_pairs={{0,8},{8,16},{16,24},{24,28},{28,20},{20,12},{12,4},{4,0},{1,9},{9... | collective-permute-start | bytes 307208 | tf_op jit(solution)/shard_map/ppermute | solution.py:43
  5.9 97.2 %collective-permute-start.1 = (bf16[80,640]{1,0:T(8,128)(2,1)}, bf16[80,640]{1,0:T(8,128)(2,1)S(1)}, u32[]{:S(2)}, u32[]{:S(2)}) collective-permute-start(bf16[80,640]{1,0:T(8,128)(2,1)} %fusion.107), channel_id=1, source_target_pairs={{0,4},{8,0},{16,8},{24,16},{28,24},{20,28},{12,20},{4,12},{1,5},{9... | collective-permute-start | bytes 307208 | tf_op jit(solution)/shard_map/ppermute | solution.py:43
  5.9 129.4 %collective-permute-start.11 = (bf16[80,2560]{1,0:T(8,128)(2,1)}, bf16[80,2560]{1,0:T(8,128)(2,1)}, u32[]{:S(2)}, u32[]{:S(2)}) collective-permute-start(bf16[80,2560]{1,0:T(8,128)(2,1)} %param.288), channel_id=1, source_target_pairs={{0,8},{8,16},{16,24},{24,28},{28,20},{20,12},{12,4},{4,0},{1,9},{9... | collective-permute-start | bytes 1228808 | tf_op jit(solution)/shard_map/ppermute | solution.py:43
  7.9 129.5 %collective-permute-start.12 = (bf16[80,2560]{1,0:T(8,128)(2,1)}, bf16[80,2560]{1,0:T(8,128)(2,1)}, u32[]{:S(2)}, u32[]{:S(2)}) collective-permute-start(bf16[80,2560]{1,0:T(8,128)(2,1)} %param.288), channel_id=1, source_target_pairs={{0,4},{8,0},{16,8},{24,16},{28,24},{20,28},{12,20},{4,12},{1,5},{9... | collective-permute-start | bytes 1228808 | tf_op jit(solution)/shard_map/ppermute | solution.py:43
  8.0 133.1 %collective-permute-start.30 = (bf16[80,2560]{1,0:T(8,128)(2,1)}, bf16[80,2560]{1,0:T(8,128)(2,1)}, u32[]{:S(2)}, u32[]{:S(2)}) collective-permute-start(bf16[80,2560]{1,0:T(8,128)(2,1)} %bitcast.770), channel_id=1, source_target_pairs={{0,8},{8,16},{16,24},{24,28},{28,20},{20,12},{12,4},{4,0},{1,9},{9... | collective-permute-start | bytes 1228808 | tf_op jit(solution)/shard_map/ppermute | solution.py:43
  133.1 96.5 %collective-permute-start.59 = (bf16[320,1920]{1,0:T(8,128)(2,1)S(1)}, bf16[320,1920]{1,0:T(8,128)(2,1)}, u32[]{:S(2)}, u32[]{:S(2)}) collective-permute-start(bf16[320,1920]{1,0:T(8,128)(2,1)S(1)} %copy-done.41), channel_id=1, source_target_pairs={{0,8},{8,16},{16,24},{24,28},{28,20},{20,12},{12,4},{4,0},{1,9},{9... | collective-permute-start | bytes 3686408 | tf_op jit(solution)/shard_map/ppermute | solution.py:43
  135.4 123.5 %collective-permute-start.60 = (bf16[320,1920]{1,0:T(8,128)(2,1)S(1)}, bf16[320,1920]{1,0:T(8,128)(2,1)S(1)}, u32[]{:S(2)}, u32[]{:S(2)}) collective-permute-start(bf16[320,1920]{1,0:T(8,128)(2,1)S(1)} %copy-done.41), channel_id=1, source_target_pairs={{0,4},{8,0},{16,8},{24,16},{28,24},{20,28},{12,20},{4,12},{1,5},{9... | collective-permute-start | bytes 3686408 | tf_op jit(solution)/shard_map/ppermute | solution.py:43
  137.5 124.1 %collective-permute-start.67 = (bf16[320,1920]{1,0:T(8,128)(2,1)S(1)}, bf16[320,1920]{1,0:T(8,128)(2,1)S(1)}, u32[]{:S(2)}, u32[]{:S(2)}) collective-permute-start(bf16[320,1920]{1,0:T(8,128)(2,1)S(1)} %bitcast.768), channel_id=1, source_target_pairs={{0,8},{8,16},{16,24},{24,28},{28,20},{20,12},{12,4},{4,0},{1,9},{9... | collective-permute-start | bytes 3686408 | tf_op jit(solution)/shard_map/ppermute | solution.py:43
  141.0 75.6 %collective-permute-start.8 = (bf16[8,80,640]{2,1,0:T(8,128)(2,1)S(1)}, bf16[8,80,640]{2,1,0:T(8,128)(2,1)}, u32[]{:S(2)}, u32[]{:S(2)}) collective-permute-start(bf16[8,80,640]{2,1,0:T(8,128)(2,1)S(1)} %bitcast_dynamic-update-slice_fusion.82), channel_id=1, source_target_pairs={{0,2},{1,3},{2,0},{3,1},{4,6},{5,7},{6,4},{7,5},{8,10},{9,11},{10,... | collective-permute-start | bytes 2457608 | tf_op jit(solution)/shard_map/ppermute | solution.py:110
  258.9 178.4 %collective-permute-start.77 = (bf16[768,2560]{1,0:T(8,128)(2,1)}, bf16[768,2560]{1,0:T(8,128)(2,1)}, u32[]{:S(2)}, u32[]{:S(2)}) collective-permute-start(bf16[768,2560]{1,0:T(8,128)(2,1)} %bitcast.150), channel_id=1, source_target_pairs={{0,2},{1,3},{2,0},{3,1},{4,6},{5,7},{6,4},{7,5},{8,10},{9,11},{10,... | collective-permute-start | bytes 11796488 | tf_op jit(solution)/shard_map/ppermute | solution.py:110
  421.5 107.6 %collective-permute-start.38 = (bf16[8,80,2560]{2,1,0:T(8,128)(2,1)}, bf16[8,80,2560]{2,1,0:T(8,128)(2,1)}, u32[]{:S(2)}, u32[]{:S(2)}) collective-permute-start(bf16[8,80,2560]{2,1,0:T(8,128)(2,1)} %bitcast_dynamic-update-slice_fusion.67), channel_id=1, source_target_pairs={{0,2},{1,3},{2,0},{3,1},{4,6},{5,7},{6,4},{7,5},{8,10},{9,11},{10,... | collective-permute-start | bytes 9830408 | tf_op jit(solution)/shard_map/ppermute | solution.py:110
  435.5 178.3 %collective-permute-start.53 = (bf16[320,1920]{1,0:T(8,128)(2,1)}, bf16[320,1920]{1,0:T(8,128)(2,1)}, u32[]{:S(2)}, u32[]{:S(2)}) collective-permute-start(bf16[320,1920]{1,0:T(8,128)(2,1)} %collective-permute-done.51), channel_id=1, source_target_pairs={{0,8},{8,16},{16,24},{24,28},{28,20},{20,12},{12,4},{4,0},{1,9},{9... | collective-permute-start | bytes 3686408 | tf_op jit(solution)/shard_map/ppermute | solution.py:43
  437.3 96.1 %collective-permute-start.39 = (bf16[8,80,2560]{2,1,0:T(8,128)(2,1)}, bf16[8,80,2560]{2,1,0:T(8,128)(2,1)}, u32[]{:S(2)}, u32[]{:S(2)}) collective-permute-start(bf16[8,80,2560]{2,1,0:T(8,128)(2,1)} %bitcast_dynamic-update-slice_fusion.67), channel_id=1, source_target_pairs={{0,1},{1,0},{2,3},{3,2},{4,5},{5,4},{6,7},{7,6},{8,9},{9,8},{10,11... | collective-permute-start | bytes 9830408 | tf_op jit(solution)/shard_map/ppermute | solution.py:110
  473.7 151.8 %collective-permute-start.54 = (bf16[320,1920]{1,0:T(8,128)(2,1)}, bf16[320,1920]{1,0:T(8,128)(2,1)}, u32[]{:S(2)}, u32[]{:S(2)}) collective-permute-start(bf16[320,1920]{1,0:T(8,128)(2,1)} %collective-permute-done.52), channel_id=1, source_target_pairs={{0,4},{8,0},{16,8},{24,16},{28,24},{20,28},{12,20},{4,12},{1,5},{9... | collective-permute-start | bytes 3686408 | tf_op jit(solution)/shard_map/ppermute | solution.py:43
  529.1 96.4 %collective-permute-start.63 = (bf16[320,1920]{1,0:T(8,128)(2,1)}, bf16[320,1920]{1,0:T(8,128)(2,1)}, u32[]{:S(2)}, u32[]{:S(2)}) collective-permute-start(bf16[320,1920]{1,0:T(8,128)(2,1)} %collective-permute-done.61), channel_id=1, source_target_pairs={{0,8},{8,16},{16,24},{24,28},{28,20},{20,12},{12,4},{4,0},{1,9},{9... | collective-permute-start | bytes 3686408 | tf_op jit(solution)/shard_map/ppermute | solution.py:43
  533.4 110.2 %collective-permute-start.71 = (bf16[320,1920]{1,0:T(8,128)(2,1)}, bf16[320,1920]{1,0:T(8,128)(2,1)}, u32[]{:S(2)}, u32[]{:S(2)}) collective-permute-start(bf16[320,1920]{1,0:T(8,128)(2,1)} %collective-permute-done.69), channel_id=1, source_target_pairs={{0,8},{8,16},{16,24},{24,28},{28,20},{20,12},{12,4},{4,0},{1,9},{9... | collective-permute-start | bytes 3686408 | tf_op jit(solution)/shard_map/ppermute | solution.py:43
  643.7 138.2 %collective-permute-start.78 = (bf16[1536,2560]{1,0:T(8,128)(2,1)}, bf16[1536,2560]{1,0:T(8,128)(2,1)}, u32[]{:S(2)}, u32[]{:S(2)}) collective-permute-start(bf16[1536,2560]{1,0:T(8,128)(2,1)} %pad_maximum_fusion.3), channel_id=1, source_target_pairs={{0,1},{1,0},{2,3},{3,2},{4,5},{5,4},{6,7},{7,6},{8,9},{9,8},{10,11... | collective-permute-start | bytes 23592968 | tf_op jit(solution)/shard_map/ppermute | solution.py:110
  643.9 91.4 %collective-permute-start.49 = (bf16[768,2560]{1,0:T(8,128)(2,1)S(1)}, bf16[768,2560]{1,0:T(8,128)(2,1)S(1)}, u32[]{:S(2)}, u32[]{:S(2)}) collective-permute-start(bf16[768,2560]{1,0:T(8,128)(2,1)S(1)} %pad_maximum_fusion.6), channel_id=1, source_target_pairs={{0,2},{1,3},{2,0},{3,1},{4,6},{5,7},{6,4},{7,5},{8,10},{9,11},{10,... | collective-permute-start | bytes 11796488 | tf_op jit(solution)/shard_map/ppermute | solution.py:110
  658.0 79.3 %collective-permute-start.65 = (bf16[160,1920]{1,0:T(8,128)(2,1)S(1)}, bf16[160,1920]{1,0:T(8,128)(2,1)S(1)}, u32[]{:S(2)}, u32[]{:S(2)}) collective-permute-start(bf16[160,1920]{1,0:T(8,128)(2,1)S(1)} %slice.639), channel_id=1, source_target_pairs={{0,8},{8,16},{16,24},{24,28},{28,20},{20,12},{12,4},{4,0},{1,9},{9... | collective-permute-start | bytes 1843208 | tf_op jit(solution)/shard_map/ppermute | solution.py:43
  677.4 92.9 %collective-permute-start.74 = (bf16[160,1920]{1,0:T(8,128)(2,1)S(1)}, bf16[160,1920]{1,0:T(8,128)(2,1)S(1)}, u32[]{:S(2)}, u32[]{:S(2)}) collective-permute-start(bf16[160,1920]{1,0:T(8,128)(2,1)S(1)} %slice.642), channel_id=1, source_target_pairs={{0,4},{8,0},{16,8},{24,16},{28,24},{20,28},{12,20},{4,12},{1,5},{9... | collective-permute-start | bytes 1843208 | tf_op jit(solution)/shard_map/ppermute | solution.py:43
  737.3 87.6 %collective-permute-start.50 = (bf16[1536,2560]{1,0:T(8,128)(2,1)S(1)}, bf16[1536,2560]{1,0:T(8,128)(2,1)}, u32[]{:S(2)}, u32[]{:S(2)}) collective-permute-start(bf16[1536,2560]{1,0:T(8,128)(2,1)S(1)} %pad_maximum_fusion.2), channel_id=1, source_target_pairs={{0,1},{1,0},{2,3},{3,2},{4,5},{5,4},{6,7},{7,6},{8,9},{9,8},{10,11... | collective-permute-start | bytes 23592968 | tf_op jit(solution)/shard_map/ppermute | solution.py:110
  1016.8 191.2 %collective-permute-start.143 = (bf16[160,1920]{1,0:T(8,128)(2,1)}, bf16[160,1920]{1,0:T(8,128)(2,1)}, u32[]{:S(2)}, u32[]{:S(2)}) collective-permute-start(bf16[160,1920]{1,0:T(8,128)(2,1)} %get-tuple-element.62), channel_id=1, source_target_pairs={{0,8},{8,16},{16,24},{24,28},{28,20},{20,12},{12,4},{4,0},{1,9},{9... | collective-permute-start | bytes 1843208 | tf_op jit(solution)/shard_map/ppermute | solution.py:43
  1020.6 189.5 %collective-permute-start.147 = (bf16[160,1920]{1,0:T(8,128)(2,1)}, bf16[160,1920]{1,0:T(8,128)(2,1)}, u32[]{:S(2)}, u32[]{:S(2)}) collective-permute-start(bf16[160,1920]{1,0:T(8,128)(2,1)} %get-tuple-element.64), channel_id=1, source_target_pairs={{0,4},{8,0},{16,8},{24,16},{28,24},{20,28},{12,20},{4,12},{1,5},{9... | collective-permute-start | bytes 1843208 | tf_op jit(solution)/shard_map/ppermute | solution.py:43
  1105.9 107.0 %collective-permute-start.135 = (bf16[160,1920]{1,0:T(8,128)(2,1)}, bf16[160,1920]{1,0:T(8,128)(2,1)}, u32[]{:S(2)}, u32[]{:S(2)}) collective-permute-start(bf16[160,1920]{1,0:T(8,128)(2,1)} %get-tuple-element.70), channel_id=1, source_target_pairs={{0,8},{8,16},{16,24},{24,28},{28,20},{20,12},{12,4},{4,0},{1,9},{9... | collective-permute-start | bytes 1843208 | tf_op jit(solution)/shard_map/ppermute | solution.py:43
  1108.7 106.3 %collective-permute-start.139 = (bf16[160,1920]{1,0:T(8,128)(2,1)}, bf16[160,1920]{1,0:T(8,128)(2,1)}, u32[]{:S(2)}, u32[]{:S(2)}) collective-permute-start(bf16[160,1920]{1,0:T(8,128)(2,1)} %get-tuple-element.72), channel_id=1, source_target_pairs={{0,4},{8,0},{16,8},{24,16},{28,24},{20,28},{12,20},{4,12},{1,5},{9... | collective-permute-start | bytes 1843208 | tf_op jit(solution)/shard_map/ppermute | solution.py:43
  1158.5 253.1 %collective-permute-start.79 = (bf16[1536,2560]{1,0:T(8,128)(2,1)}, bf16[1536,2560]{1,0:T(8,128)(2,1)}, u32[]{:S(2)}, u32[]{:S(2)}) collective-permute-start(bf16[1536,2560]{1,0:T(8,128)(2,1)} %slice.649), channel_id=1, source_target_pairs={{0,1},{1,0},{2,3},{3,2},{4,5},{5,4},{6,7},{7,6},{8,9},{9,8},{10,11... | collective-permute-start | bytes 23592968 | tf_op jit(solution)/shard_map/ppermute | solution.py:110
  1253.1 268.8 %collective-permute-start.75 = (bf16[1536,2560]{1,0:T(8,128)(2,1)}, bf16[1536,2560]{1,0:T(8,128)(2,1)}, u32[]{:S(2)}, u32[]{:S(2)}) collective-permute-start(bf16[1536,2560]{1,0:T(8,128)(2,1)} %slice.644), channel_id=1, source_target_pairs={{0,1},{1,0},{2,3},{3,2},{4,5},{5,4},{6,7},{7,6},{8,9},{9,8},{10,11... | collective-permute-start | bytes 23592968 | tf_op jit(solution)/shard_map/ppermute | solution.py:110
  1419.8 110.2 %collective-permute-start.80 = (bf16[768,2560]{1,0:T(8,128)(2,1)}, bf16[768,2560]{1,0:T(8,128)(2,1)}, u32[]{:S(2)}, u32[]{:S(2)}) collective-permute-start(bf16[768,2560]{1,0:T(8,128)(2,1)} %add_convert_fusion.1), channel_id=1, source_target_pairs={{0,2},{1,3},{2,0},{3,1},{4,6},{5,7},{6,4},{7,5},{8,10},{9,11},{10,... | collective-permute-start | bytes 11796488 | tf_op jit(solution)/shard_map/ppermute | solution.py:110
  1528.2 280.3 %collective-permute-start.76 = (bf16[768,2560]{1,0:T(8,128)(2,1)}, bf16[768,2560]{1,0:T(8,128)(2,1)}, u32[]{:S(2)}, u32[]{:S(2)}) collective-permute-start(bf16[768,2560]{1,0:T(8,128)(2,1)} %add_convert_fusion.2), channel_id=1, source_target_pairs={{0,2},{1,3},{2,0},{3,1},{4,6},{5,7},{6,4},{7,5},{8,10},{9,11},{10,... | collective-permute-start | bytes 11796488 | tf_op jit(solution)/shard_map/ppermute | solution.py:110
  1736.0 127.2 %collective-permute-start.117 = (bf16[8,2,80,2560]{3,2,0,1:T(8,128)(2,1)}, bf16[8,2,80,2560]{3,2,0,1:T(8,128)(2,1)}, u32[]{:S(2)}, u32[]{:S(2)}) collective-permute-start(bf16[8,2,80,2560]{3,2,0,1:T(8,128)(2,1)} %bitcast.749), channel_id=1, source_target_pairs={{0,1},{1,0},{2,3},{3,2},{4,5},{5,4},{6,7},{7,6},{8,9},{9,8},{10,11... | collective-permute-start | bytes 19660808 | tf_op jit(solution)/shard_map/ppermute | solution.py:110
  1893.1 123.6 %collective-permute-start.108 = (bf16[8,80,2560]{2,1,0:T(8,128)(2,1)S(1)}, bf16[8,80,2560]{2,1,0:T(8,128)(2,1)S(1)}, u32[]{:S(2)}, u32[]{:S(2)}) collective-permute-start(bf16[8,80,2560]{2,1,0:T(8,128)(2,1)S(1)} %dynamic-slice_bitcast_fusion.2), channel_id=1, source_target_pairs={{0,2},{1,3},{2,0},{3,1},{4,6},{5,7},{6,4},{7,5},{8,10},{9,11},{10,... | collective-permute-start | bytes 9830408 | tf_op jit(solution)/shard_map/ppermute | solution.py:110
  1958.4 85.5 %collective-permute-start.124 = (bf16[80,2560]{1,0:T(8,128)(2,1)S(1)}, bf16[80,2560]{1,0:T(8,128)(2,1)S(1)}, u32[]{:S(2)}, u32[]{:S(2)}) collective-permute-start(bf16[80,2560]{1,0:T(8,128)(2,1)S(1)} %pad_maximum_fusion.17), channel_id=1, source_target_pairs={{0,4},{8,0},{16,8},{24,16},{28,24},{20,28},{12,20},{4,12},{1,5},{9... | collective-permute-start | bytes 1228808 | tf_op jit(solution)/shard_map/ppermute | solution.py:43
  (207 other events, 6222.2 us)

commit v2 on v1

v2 whole, which is shorter than its diff:
```python
import functools
import math

import jax
import jax.numpy as jnp
from jax import lax
from jax.experimental import pallas as pl
from jax.experimental.pallas import tpu as pltpu
from jax.sharding import PartitionSpec as P

WINDOW = 2048
EPSILON = 1e-06
NEGATIVE = -1e30
LOG2E = math.log2(math.e)
LN2 = math.log(2.0)
F32 = jnp.float32
BF16 = jnp.bfloat16
SHORT = pl.CostEstimate(flops=1024, bytes_accessed=1024, transcendentals=0)


def rms_scale(values, gain):
    return values * lax.rsqrt(jnp.mean(values * values, axis=-1, keepdims=True) + EPSILON) * gain


def dot(left, right, out=F32):
    return jnp.dot(left, right, preferred_element_type=out)


def contract_rows(left, right, out=F32):
    return lax.dot_general(left, right, (((0,), (0,)), ((), ())), preferred_element_type=out)


def contract_last(left, right, out=F32):
    return lax.dot_general(left, right, (((1,), (1,)), ((), ())), preferred_element_type=out)


class Plan:
    def __init__(self):
        self.now = ()

    def hold(self, value):
        if not self.now:
            return value
        return lax.optimization_barrier((value,) + self.now)[0]

    def run(self, function, first, *rest):
        out = function(self.hold(first), *rest)
        self.now = tuple(jax.tree.leaves(out))
        return out

    def start(self, generator):
        return Transfer(self, generator)

    def step(self, *transfers):
        for transfer in transfers:
            transfer.step()


class Transfer:
    def __init__(self, plan, generator):
        self.plan, self.generator = plan, generator
        self.ended, self.value, self.passed = False, None, []
        self.launch(None)

    def launch(self, arrived):
        try:
            wanted = self.generator.send(arrived)
            while not isinstance(wanted, list):
                self.passed.append(wanted)
                wanted = next(self.generator)
        except StopIteration as stop:
            self.ended, self.value = True, stop.value
            return
        held = [self.plan.hold(operand) for operand, _, _ in wanted]
        self.flying = [
            lax.ppermute(operand, axis, pairs) for operand, (_, axis, pairs) in zip(held, wanted)
        ]
        self.plan.now = self.plan.now + tuple(operand for operand, _, _ in wanted)

    def step(self):
        if not self.ended:
            arrived = self.flying
            self.plan.now = self.plan.now + tuple(arrived)
            self.launch(arrived)

    def end(self):
        while not self.ended:
            self.step()
        return self.value


class Whole:
    def __init__(self, plan, function, operand):
        self.plan, self.value = plan, function(plan.hold(operand))

    def end(self):
        self.plan.now = self.plan.now + (self.value,)
        return self.value


def ctx_gather(block):
    return lax.all_gather(block, "ctx", axis=0, tiled=True)


def ctx_scatter(terms):
    return lax.psum_scatter(terms, "ctx", scatter_dimension=0, tiled=True)


def ring_order(count):
    return list(range(0, count, 2)) + [i for i in range(count - 1, 0, -1) if i % 2]


def ring(block, shift):
    count = lax.axis_size("ctx")
    order = ring_order(count)
    return block, "ctx", [(order[i], order[(i + shift) % count]) for i in range(count)]


def wt_swap(block, bit):
    return block, "wt", [(i, i ^ bit) for i in range(lax.axis_size("wt"))]


def core_swap(block):
    return wt_swap(block, 1)


def x_swap(block):
    return wt_swap(block, 2)


def ring_index(offset):
    count = lax.axis_size("ctx")
    here = lax.axis_index("ctx")
    place = jnp.where(here % 2 == 0, here // 2, count - 1 - here // 2)
    place = (place + offset + count) % count
    return jnp.where(place < count // 2, 2 * place, 2 * (count - 1 - place) + 1)


def half_rows(rows):
    return rows // 2 // 16 * 16 if rows >= 32 else rows // 2


def ring_blocks(block):
    half = lax.axis_size("ctx") // 2
    cut = half_rows(block.shape[0])
    ahead = behind = block
    for step in range(1, half):
        ahead, behind = yield [ring(ahead, 1), ring(behind, -1)], None
        yield None, [(-step, 0, ahead), (step, 0, behind)]
    low, high = yield [ring(ahead[:cut], 1), ring(behind[cut:], -1)], None
    yield None, [(half, 0, low), (half, cut, high)]


def put(found, piece, offset, row):
    start = (ring_index(offset), row) + (0,) * (piece.ndim - 1)
    return lax.dynamic_update_slice(found, piece[None], start)


def begin_kernel(place, block_ref, out_ref):
    del place
    out_ref[0] = block_ref[...]


def begin(block, count):
    shape = block.shape
    return pl.pallas_call(
        begin_kernel,
        out_shape=jax.ShapeDtypeStruct((count,) + shape, block.dtype),
        grid_spec=pltpu.PrefetchScalarGridSpec(
            num_scalar_prefetch=1,
            grid=(1,),
            in_specs=[pl.BlockSpec(shape, lambda i, place: (0, 0))],
            out_specs=pl.BlockSpec((1,) + shape, lambda i, place: (place[0], 0, 0)),
        ),
        cost_estimate=pl.CostEstimate(
            flops=0, bytes_accessed=4 * math.prod(shape), transcendentals=0
        ),
    )(lax.axis_index("ctx").reshape(1), block)


def ring_gather(block):
    found = begin(block, lax.axis_size("ctx"))
    blocks = ring_blocks(block)
    wanted, _ = next(blocks)
    while wanted is not None:
        arrived = yield wanted
        _, pieces = blocks.send(arrived)
        for offset, row, piece in pieces:
            found = put(found, piece, offset, row)
        wanted, _ = next(blocks, (None, None))
    return found


def ring_scatter(terms):
    half = terms.shape[0] // 2
    cut = half_rows(terms.shape[1])

    def own(offset):
        return lax.dynamic_index_in_dim(terms, ring_index(offset), 0, keepdims=False)

    far = own(half)
    ahead, behind = yield [ring(far[:cut], 1), ring(far[cut:], -1)]
    if half == 1:
        return own(0).astype(F32) + jnp.concatenate([ahead, behind], axis=0).astype(F32)
    for step in range(half - 1, 0, -1):
        up, down = own(step), own(-step)
        if step == half - 1:
            up = jnp.concatenate([add(up[:cut], ahead), up[cut:]], axis=0)
            down = jnp.concatenate([down[:cut], add(down[cut:], behind)], axis=0)
        else:
            up, down = add(up, ahead), add(down, behind)
        ahead, behind = yield [ring(up, 1), ring(down, -1)]
    return own(0).astype(F32) + ahead.astype(F32) + behind.astype(F32)


def add(first, second):
    return (first.astype(F32) + second.astype(F32)).astype(BF16)


def gather_everywhere(block):
    here = lax.axis_index("wt")
    width = block.shape[1]
    mine = begin(block, lax.axis_size("ctx"))
    far = None
    blocks = ring_blocks(block)
    crossing = [(0, 0, block)]
    wanted, _ = next(blocks)
    while wanted is not None or crossing:
        turns = wanted or []
        arrived = yield turns + [x_swap(piece) for _, _, piece in crossing]
        for (offset, row, _), piece in zip(crossing, arrived[len(turns) :]):
            far = begin(piece, mine.shape[0]) if far is None else put(far, piece, offset, row)
        crossing = []
        if wanted is not None:
            _, crossing = blocks.send(arrived[: len(turns)])
            for offset, row, piece in crossing:
                mine = put(mine, piece, offset, row)
            wanted, _ = next(blocks, (None, None))
    near, last = yield [core_swap(mine), core_swap(far)]
    return interleave(here, mine, near, far, last).reshape(-1, width)


def interleave_kernel(here, *refs):
    *pieces, out_ref = refs
    for bit, piece in enumerate(pieces):
        out_ref[0, here[0] ^ bit] = piece[0]


def interleave(here, *pieces):
    count, rows, width = pieces[0].shape
    return pl.pallas_call(
        interleave_kernel,
        out_shape=jax.ShapeDtypeStruct((count, 4, rows, width), pieces[0].dtype),
        grid_spec=pltpu.PrefetchScalarGridSpec(
            num_scalar_prefetch=1,
            grid=(count,),
            in_specs=[pl.BlockSpec((1, rows, width), lambda i, here: (i, 0, 0))] * 4,
            out_specs=pl.BlockSpec((1, 4, rows, width), lambda i, here: (i, 0, 0, 0)),
        ),
        cost_estimate=SHORT,
    )(here.reshape(1), *pieces)


def scatter_everywhere(terms):
    here = lax.axis_index("wt")
    count = lax.axis_size("ctx")
    rows = terms.shape[0] // (4 * count)
    split = terms.reshape(count, 2, 2, rows, terms.shape[1])
    x_here, core_here = here // 2, here % 2
    sent = lax.dynamic_index_in_dim(split, 1 - core_here, 2, keepdims=False)
    (came,) = yield [core_swap(sent)]
    both = add(lax.dynamic_index_in_dim(split, core_here, 2, keepdims=False), came)
    sent = lax.dynamic_index_in_dim(both, 1 - x_here, 1, keepdims=False)
    (came,) = yield [x_swap(sent)]
    kept = add(lax.dynamic_index_in_dim(both, x_here, 1, keepdims=False), came)
    return (yield from ring_scatter(kept))


def once(permute):
    (came,) = yield [permute]
    return came


def rows_there(block):
    (far,) = yield [x_swap(block)]
    (last,) = yield [core_swap(far)]
    return [far, last]


def scatter_here(terms):
    rows = terms.shape[0] // 2
    (near,) = yield [core_swap(terms[rows:])]
    return terms[:rows].astype(F32) + near.astype(F32)


def scatter_there(terms, parts):
    rows = terms.shape[0] // 2
    (last,) = yield [core_swap(terms[rows:])]
    far = add(terms[:rows], last)
    came = []
    for part in jnp.split(far, parts):
        came += yield [x_swap(part)]
        yield came[-1]
    return jnp.concatenate(came, axis=0)


def rotate(values, cosine, sine):
    half = values.shape[-1] // 2
    first, second = values[:, :half], values[:, half:]
    return jnp.concatenate(
        [first * cosine - second * sine, second * cosine + first * sine], axis=-1
    )


def visible(start, keys, low, high):
    index = start + lax.broadcasted_iota(jnp.int32, (keys, low.shape[1]), 0)
    return (index >= low) & (index <= high)


def key_parts(keys):
    return [slice(0, keys)]


def attend_kernel(
    spans, q_ref, kv_ref, low_ref, high_ref, cos_ref, sin_ref,
    out_ref, qrot_ref, lse_ref, vt_ref, *, heads, size, keys,
):
    rows = q_ref.shape[0]
    scale = size ** -0.5 * LOG2E

    @pl.when(pl.program_id(0) == 0)
    def _():
        for block in range(kv_ref.shape[0]):
            vt_ref[block] = kv_ref[block, :, size:].T

    turned = []
    for head in range(heads):
        part = rotate(q_ref[:, head * size : (head + 1) * size], cos_ref[...], sin_ref[...])
        part = (part * scale).astype(BF16)
        qrot_ref[:, head * size : (head + 1) * size] = part
        turned.append(part.T)
    qt = jnp.concatenate(turned, axis=1)
    low, high = low_ref[...], high_ref[...]
    parts = key_parts(keys)

    def step(block, carry, masked):
        top, total, acc = carry
        scores = []
        for part in parts:
            piece = dot(kv_ref[block, part, :size], qt)
            if masked:
                seen = visible(block * keys + part.start, part.stop - part.start, low, high)
                piece = jnp.where(seen, piece, NEGATIVE)
            scores.append(piece)
        new_top = top
        for piece in scores:
            new_top = jnp.maximum(new_top, jnp.max(piece, axis=0, keepdims=True))
        fade = jnp.exp2(top - new_top)
        total = total * fade
        acc = acc * fade
        for part, piece in zip(parts, scores):
            probs = jnp.exp2(piece - new_top)
            total = total + jnp.sum(probs, axis=0, keepdims=True)
            acc = acc + dot(vt_ref[block, :, part], probs.astype(BF16))
        return new_top, total, acc

    carry = (
        jnp.full((1, heads * rows), NEGATIVE, F32),
        jnp.zeros((1, heads * rows), F32),
        jnp.zeros((size, heads * rows), F32),
    )
    carry = lax.fori_loop(spans[0], spans[1], functools.partial(step, masked=True), carry)
    carry = lax.fori_loop(spans[2], spans[3], functools.partial(step, masked=False), carry)
    carry = lax.fori_loop(spans[4], spans[5], functools.partial(step, masked=True), carry)
    top, total, acc = carry
    acc = acc * (1.0 / total)
    lse_ref[0] = top + jnp.log2(total)
    for head in range(heads):
        out_ref[:, head * size : (head + 1) * size] = (
            acc[:, head * rows : (head + 1) * rows].astype(BF16).T
        )


def attend_back_kernel(
    spans, q_ref, kv_ref, low_ref, high_ref, cos_ref, sin_ref, out_ref, grad_ref, lse_ref,
    dq_ref, dkv_ref, kt_ref, dk_ref, dv_ref, *, heads, size, keys,
):
    rows = q_ref.shape[0]

    @pl.when(pl.program_id(0) == 0)
    def _():
        for block in range(kv_ref.shape[0]):
            kt_ref[block] = kv_ref[block, :, :size].T
        dk_ref[...] = jnp.zeros_like(dk_ref)
        dv_ref[...] = jnp.zeros_like(dv_ref)

    parts = [slice(head * size, (head + 1) * size) for head in range(heads)]
    q = jnp.concatenate([q_ref[:, part] for part in parts], axis=0)
    grad = jnp.concatenate([grad_ref[:, part] for part in parts], axis=0)
    out_t = jnp.concatenate([out_ref[:, part].T for part in parts], axis=1)
    qt, grad_t = q.T, grad.T
    delta = jnp.sum(grad_t.astype(F32) * out_t.astype(F32), axis=0, keepdims=True)
    low, high, lse = low_ref[...], high_ref[...], lse_ref[0]

    def step(block, dq, masked):
        for part in key_parts(keys):
            scores = dot(kv_ref[block, part, :size], qt)
            if masked:
                seen = visible(block * keys + part.start, part.stop - part.start, low, high)
                scores = jnp.where(seen, scores, NEGATIVE)
            probs = jnp.exp2(scores - lse)
            probs_grad = dot(kv_ref[block, part, size:], grad_t)
            score_grad = (probs * (probs_grad - delta)).astype(BF16)
            dv_ref[block, part] += dot(probs.astype(BF16), grad)
            dk_ref[block, part] += dot(score_grad, q)
            dq = dq + dot(kt_ref[block, :, part], score_grad)
        return dq

    dq = jnp.zeros((size, heads * rows), F32)
    dq = lax.fori_loop(spans[0], spans[1], functools.partial(step, masked=True), dq)
    dq = lax.fori_loop(spans[2], spans[3], functools.partial(step, masked=False), dq)
    dq = lax.fori_loop(spans[4], spans[5], functools.partial(step, masked=True), dq)
    for head, part in enumerate(parts):
        turned = rotate(dq[:, head * rows : (head + 1) * rows].T, cos_ref[...], -sin_ref[...])
        dq_ref[:, part] = (turned * size ** -0.5).astype(BF16)

    @pl.when(pl.program_id(0) == pl.num_programs(0) - 1)
    def _():
        for block in range(dkv_ref.shape[0]):
            dkv_ref[block, :, :size] = (dk_ref[block] * LN2).astype(BF16)
            dkv_ref[block, :, size:] = dv_ref[block].astype(BF16)


def attention_calls(rows, width, size, count, keys, micro):
    heads = 2 if (width // size) % 2 == 0 else 1
    groups = width // size // heads
    span = heads * size
    head_block = pl.BlockSpec((rows, span), lambda g, s: (0, g))

    def whole(*shape):
        return pl.BlockSpec(shape, lambda g, s: (0,) * len(shape))

    lse_block = pl.BlockSpec((1, 1, heads * rows), lambda g, s: (g, 0, 0))
    shared = [
        head_block,
        pl.BlockSpec((count, keys, 2 * size), lambda g, s: (0, micro, 0)),
        whole(1, heads * rows), whole(1, heads * rows),
        whole(rows, size // 2), whole(rows, size // 2),
    ]
    lse_shape = jax.ShapeDtypeStruct((groups, 1, heads * rows), F32)
    row_shape = jax.ShapeDtypeStruct((rows, width), BF16)
    params = pltpu.CompilerParams(vmem_limit_bytes=48 * 2**20)
    work = rows * width * min(count * keys, WINDOW) * 2
    sizes = dict(heads=heads, size=size, keys=keys)
    forward = pl.pallas_call(
        functools.partial(attend_kernel, **sizes),
        out_shape=(row_shape, row_shape, lse_shape),
        grid_spec=pltpu.PrefetchScalarGridSpec(
            num_scalar_prefetch=1, grid=(groups,), in_specs=shared,
            out_specs=(head_block, head_block, lse_block),
            scratch_shapes=[pltpu.VMEM((count, size, keys), BF16)],
        ),
        compiler_params=params,
        cost_estimate=SHORT,
    )
    backward = pl.pallas_call(
        functools.partial(attend_back_kernel, **sizes),
        out_shape=(row_shape, jax.ShapeDtypeStruct((count, keys, 2 * size), BF16)),
        grid_spec=pltpu.PrefetchScalarGridSpec(
            num_scalar_prefetch=1, grid=(groups,),
            in_specs=shared + [head_block, head_block, lse_block],
            out_specs=(head_block, whole(count, keys, 2 * size)),
            scratch_shapes=[
                pltpu.VMEM((count, size, keys), BF16),
                pltpu.VMEM((count, keys, size), F32),
                pltpu.VMEM((count, keys, size), F32),
            ],
        ),
        compiler_params=params,
        cost_estimate=SHORT,
    )
    return forward, backward, heads


def pad_rows(array, rows):
    return jnp.pad(array, ((0, rows - array.shape[0]), (0, 0)))


def weight_kernel(a_here, a_there, b_here, b_there, out_ref):
    out_ref[...] = (
        contract_rows(a_here[...], b_here[...]) + contract_rows(a_there[...], b_there[...])
    ).astype(BF16)


def weight_grad(left, right):
    rows, width = left[0].shape
    cols = right[0].shape[1]
    tile = 256 if width % 256 == 0 else 128

    def column(array):
        return pl.BlockSpec((rows, tile), lambda i: (0, i))

    def fixed(array):
        return pl.BlockSpec(array.shape, lambda i: (0, 0), pipeline_mode=pl.Buffered(1))

    return pl.pallas_call(
        weight_kernel,
        out_shape=jax.ShapeDtypeStruct((width, cols), BF16),
        grid=(width // tile,),
        in_specs=[column(a) for a in left] + [fixed(a) for a in right],
        out_specs=pl.BlockSpec((tile, cols), lambda i: (i, 0)),
        compiler_params=pltpu.CompilerParams(vmem_limit_bytes=48 * 2**20),
        cost_estimate=pl.CostEstimate(
            flops=4 * rows * width * cols,
            bytes_accessed=4 * rows * (width + cols) + 2 * width * cols,
            transcendentals=0,
        ),
    )(*left, *right)


def local(
    tokens, segment_ids, cotangent, gain_attn, w_query, w_key, w_value, w_out, gain_mlp,
    w_gate, w_up, w_down,
):
    micros, _, rows, width = tokens.shape
    size = w_key.shape[1]
    query_width = w_query.shape[1]
    hidden_cols = w_gate.shape[1]
    count = lax.axis_size("ctx")
    first = lax.axis_index("ctx") * rows
    padded = -(-rows // 128) * 128
    calls = [
        attention_calls(padded, query_width, size, count, rows, m) for m in range(micros)
    ]
    heads = calls[0][2]
    plan = Plan()

    ids = segment_ids[:, 0]
    slots = w_key.shape[0]
    id_cols = -(-micros * rows // slots)
    id_flat = jnp.pad(ids.reshape(-1), (0, id_cols * slots - micros * rows)).astype(BF16)
    beside = jnp.concatenate(
        [jnp.stack([gain_attn, gain_mlp], axis=1), id_flat.reshape(slots, id_cols)], axis=1
    )
    beside = jnp.pad(beside, ((0, 0), (0, -beside.shape[1] % 128)))
    everyone = ("ctx", "wt")
    narrow_in = Whole(
        plan, lambda block: lax.all_gather(block, everyone, axis=0, tiled=True),
        jnp.concatenate([w_key, w_value, beside], axis=1),
    )
    query_in = plan.start(gather_everywhere(w_query))
    plan.step(query_in)
    plan.step(query_in)
    narrow_full = narrow_in.end()
    narrow_ring = lax.dynamic_index_in_dim(
        narrow_full.reshape(count, 4, slots, -1), lax.axis_index("wt"), 1, keepdims=False
    )
    w_kv = narrow_full[:, : 2 * size]
    gain_first = narrow_full[:, 2 * size].astype(F32)
    gain_second = narrow_full[:, 2 * size + 1].astype(F32)
    ids_all = narrow_ring[:, :, 2 * size + 2 : 2 * size + 2 + id_cols].reshape(count, -1)
    ids_all = ids_all[:, : micros * rows].reshape(count, micros, rows)
    ids_all = ids_all.transpose(1, 0, 2).reshape(micros, count * rows).astype(jnp.int32)

    index = first + jnp.arange(rows, dtype=jnp.int32)
    half = size // 2

    def tables(index):
        freqs = 10000.0 ** (-jnp.arange(half, dtype=F32) / half)
        angles = index.astype(F32)[:, None] * freqs
        return jnp.cos(angles), jnp.sin(angles)

    cosine, sine = tables(index)
    begins = jnp.sum(
        (ids_all[:, None, :] < ids[:, :, None]).astype(jnp.int32), axis=-1, dtype=jnp.int32
    )
    lowest = jnp.maximum(begins, index[None] - (WINDOW - 1))

    def project_kv(rows_in, gain, weights, cosine, sine):
        normed = rms_scale(rows_in[:, 0].astype(F32), gain).astype(BF16)
        normed = normed.reshape(micros * rows, width)
        both = dot(normed, weights)
        keys = both[:, :size].astype(BF16).astype(F32)
        twice = [jnp.concatenate([t] * micros, axis=0) for t in (cosine, sine)]
        return normed, jnp.concatenate([rotate(keys, *twice), both[:, size:]], axis=1).astype(BF16)

    normed, turned = plan.run(project_kv, tokens, gain_first, w_kv, cosine, sine)
    kv_in = Whole(plan, ctx_gather, turned)
    plan.step(query_in)
    plan.step(query_in)
    out_in = plan.start(gather_everywhere(plan.hold(w_out).T))
    plan.step(query_in)
    plan.step(out_in)
    query_full = query_in.end()
    cot = plan.hold(cotangent).reshape(micros * rows, width)
    cot_near, cot_far = plan.start(once(core_swap(cot))), plan.start(rows_there(cot))
    queries = plan.run(lambda a, b: dot(a, b).reshape(micros, rows, -1), normed, query_full)
    plan.step(out_in)
    kv_all = kv_in.end().reshape(count, micros * rows, 2 * size)
    gate_in = Whole(plan, ctx_gather, w_gate)
    plan.step(out_in)

    saved = []
    for m in range(micros):
        full_from = (jnp.max(lowest[m]) + rows - 1) // rows
        full_to = (first + 1) // rows
        last = (first + rows - 1) // rows + 1
        spans = jnp.stack([
            jnp.min(lowest[m]) // rows, jnp.minimum(full_from, last),
            full_from, full_to,
            jnp.maximum(full_from, full_to), last,
        ]).astype(jnp.int32)

        def lanes(values):
            return jnp.tile(jnp.pad(values, (0, padded - rows))[None], (1, heads))

        shared = (
            kv_all, lanes(lowest[m]), lanes(index),
            pad_rows(cosine, padded), pad_rows(sine, padded),
        )
        attended, query_rot, lse = plan.run(
            lambda q, s, *rest: calls[m][0](s, q, *rest),
            pad_rows(queries[m], padded), spans, *shared,
        )
        saved.append((spans, query_rot, shared, attended, lse))
        plan.step(out_in)

    attended = jnp.concatenate([entry[3][:rows] for entry in saved], axis=0)
    plan.step(cot_near, cot_far)
    out_full = out_in.end()

    def join(attended, tokens, weights, gain):
        middle = tokens.reshape(micros * rows, width).astype(F32) + contract_last(attended, weights)
        return middle, rms_scale(middle, gain).astype(BF16)

    middle, low = plan.run(join, attended, tokens, out_full, gain_second)
    near_in, far_in = plan.start(once(core_swap(low))), plan.start(rows_there(low))

    cot_rows = [
        jnp.concatenate([cot, cot_near.end()], axis=0), jnp.concatenate(cot_far.end(), axis=0)
    ]
    gate_full = gate_in.end()
    up_in = Whole(plan, ctx_gather, w_up)
    normed_rows = [
        jnp.concatenate([low, near_in.end()], axis=0), jnp.concatenate(far_in.end(), axis=0)
    ]
    gate_rows = [plan.run(dot, rows_in, gate_full) for rows_in in normed_rows]
    up_full = up_in.end()
    down_in = Whole(plan, ctx_gather, w_down.T)

    def make_hidden(rows_in, weights, gate):
        up = dot(rows_in, weights)
        return up, (jax.nn.gelu(gate) * up).astype(BF16)

    up_rows, hidden = [], []
    for side in range(2):
        up, both = plan.run(make_hidden, normed_rows[side], up_full, gate_rows[side])
        up_rows.append(up)
        hidden.append(both)

    def weight_sum(left, right):
        terms = plan.run(lambda a, *rest: weight_grad((a, left[1]), right), left[0])
        return Whole(plan, ctx_scatter, terms)

    down_out = weight_sum(cot_rows, hidden)
    down_full = down_in.end()

    def both_halves(function, parts, between=None):
        there = plan.start(scatter_there(function(1), parts))
        if between is not None:
            between()
        here = plan.start(scatter_here(function(0)))
        plan.step(there)
        return here, there

    mlp_here, mlp_there = both_halves(
        lambda side: plan.run(lambda a, b: contract_last(a, b, BF16), hidden[side], down_full), 1
    )

    def hidden_back(cot, weights, gate, up):
        hidden_grad = dot(cot, weights)
        gelu_gate, gelu_back = jax.vjp(jax.nn.gelu, gate)
        gate_grad = gelu_back(hidden_grad * up)[0].astype(BF16)
        return gate_grad, (hidden_grad * gelu_gate).astype(BF16)

    gate_grad, up_grad = [None, None], [None, None]
    for side in range(2):
        gate_grad[side], up_grad[side] = plan.run(
            hidden_back, cot_rows[side], down_full, gate_rows[side], up_rows[side]
        )
    mlp_own = mlp_here.end()
    gate_out = weight_sum(normed_rows, gate_grad)
    mlp_came = mlp_there.end()

    def rows_back(side):
        part = plan.run(contract_last, gate_grad[side], gate_full)
        return plan.run(
            lambda a, b, c: (contract_last(a, b) + c).astype(BF16), up_grad[side], up_full, part
        )

    back_here, back_there = both_halves(rows_back, micros, down_out.end)
    up_terms = plan.run(
        lambda a, *rest: weight_grad((a, normed_rows[1]), up_grad), normed_rows[0]
    )
    up_out = plan.start(ring_scatter(up_terms.reshape(count, -1, hidden_cols)))

    middle_grads, branch_grads, attended_grads, gain_two = [], [], [], []
    query_grads, kv_out = [], []
    back_own = back_here.end()

    def join_back(came, own, middle, gain, cot):
        incoming = own + came.astype(F32)
        middle_part, gain_part = jax.vjp(rms_scale, middle, gain)[1](incoming)
        middle_grad = middle_part + cot.astype(F32)
        return middle_grad, middle_grad.astype(BF16), gain_part

    def before_attention(m):
        here = slice(m * rows, (m + 1) * rows)
        middle_grad, branch_grad, gain_part = plan.run(
            join_back, back_there.passed[m], back_own[here], middle[here], gain_second, cot[here]
        )
        middle_grads.append(middle_grad)
        branch_grads.append(branch_grad)
        gain_two.append(gain_part)
        attended_grads.append(plan.run(lambda a, b: dot(a, b, BF16), branch_grad, out_full))

    def through_attention(m):
        spans, query_rot, shared, attended, lse = saved[m]
        query_grad, kv_term = plan.run(
            lambda g, s, q, shared, out, lse: calls[m][1](s, q, *shared, out, g, lse),
            pad_rows(attended_grads[m], padded), spans, query_rot, shared, attended, lse,
        )
        query_grads.append(query_grad[:rows])
        kv_out.append(plan.start(ring_scatter(kv_term)))

    plan.step(back_there)
    plan.step(up_out)
    before_attention(0)
    through_attention(0)
    gate_out.end()
    plan.step(up_out)
    plan.step(back_there)
    before_attention(1)
    plan.step(kv_out[0])
    plan.step(up_out)
    out_out = plan.start(scatter_everywhere(
        plan.run(
            lambda a, b: contract_rows(a, b, BF16), jnp.concatenate(branch_grads, axis=0), attended
        )
    ))
    plan.step(kv_out[0])
    plan.step(out_out)
    through_attention(1)
    plan.step(kv_out[0])
    plan.step(up_out)
    query_grad = jnp.concatenate(query_grads, axis=0)
    query_out = plan.start(scatter_everywhere(
        plan.run(lambda a, b: contract_rows(a, b, BF16), normed, query_grad)
    ))
    plan.step(kv_out[0])
    plan.step(kv_out[1])
    plan.step(query_out)
    plan.step(out_out)
    part = plan.run(contract_last, query_grad, query_full)
    plan.step(kv_out[1])

    def finish_output(came, own, middle):
        return (middle + own + came.astype(F32)).reshape(micros, rows, width)

    output = plan.run(finish_output, mlp_came, mlp_own, middle)
    plan.step(kv_out[1])
    plan.step(out_out)
    kv_own = jnp.concatenate([t.end() for t in kv_out], axis=0)
    twice = [jnp.concatenate([t] * micros, axis=0) for t in (cosine, sine)]
    key_own = rotate(kv_own[:, :size], twice[0], -twice[1])
    kv_grad = jnp.concatenate([key_own, kv_own[:, size:]], axis=1).astype(BF16)

    def narrow_back(kv_grad, normed):
        return contract_rows(normed, kv_grad, BF16)

    def inputs_back(kv_grad, part, weights, tokens, gain, middle_grads):
        attn_in_grad = part + contract_last(kv_grad, weights)
        norm_back = jax.vjp(rms_scale, tokens[:, 0].astype(F32), gain)[1]
        input_part, gain_one = norm_back(attn_in_grad.reshape(micros, rows, width))
        return jnp.stack(middle_grads) + input_part, gain_one

    kv_terms = plan.run(narrow_back, kv_grad, normed)
    grad_tokens, gain_one = plan.run(
        inputs_back, kv_grad, part, w_kv, tokens, gain_first, middle_grads
    )
    gain_cols = jnp.stack([gain_one, sum(gain_two)], axis=1).astype(BF16)
    narrow_out = plan.start(scatter_everywhere(
        jnp.concatenate([kv_terms, jnp.pad(gain_cols, ((0, 0), (0, 126)))], axis=1)
    ))
    for _ in range(count):
        plan.step(narrow_out, out_out, query_out)
    narrow_grad = narrow_out.end()
    return (
        output[:, None],
        grad_tokens[:, None],
        narrow_grad[:, 2 * size],
        query_out.end(),
        narrow_grad[:, :size],
        narrow_grad[:, size : 2 * size],
        out_out.end().T,
        narrow_grad[:, 2 * size + 1],
        gate_out.value.astype(F32),
        up_out.end(),
        down_out.value.T.astype(F32),
    )


def solution(mesh):
    rows = P(None, "wt", "ctx", None)
    everywhere = P(("ctx", "wt"))
    tall = P(("ctx", "wt"), None)
    wide = P(None, ("ctx", "wt"))
    square = P("ctx", "wt")
    return jax.shard_map(
        local,
        mesh=mesh,
        in_specs=(
            rows, P(None, "wt", "ctx"), rows, everywhere, tall, tall, tall, wide, everywhere,
            square, square, P("wt", "ctx"),
        ),
        out_specs=(
            rows, rows, everywhere, tall, tall, tall, wide, everywhere, square, square,
            P("wt", "ctx"),
        ),
        check_vma=False,
    )
```

time: 2100 us -> 1670 us (0.80)
  waiting for transfers between devices: 760 us -> 565 us
  Pallas kernels: 57.1 us -> 204 us
  starting transfers between devices: 321 us -> 196 us
  matrix products: 507 us -> 395 us
  local copies, waits for them, and re-layouts: 228 us -> 132 us
  blocking collectives: 26.4 us -> 0 us
    ppermute x151 -> x105, waiting for transfers between devices: 760 us -> 495 us  [launch(): lax.ppermute(operand, axis, pairs)]
    pallas_call x4 -> x13, Pallas kernels: 57.1 us -> 204 us  [the longest x3 117 us: weight_grad(): pl.pallas_call(weight_kernel, out_shape=jax.ShapeDtypeStruct((width, cols...]
    ppermute x151 -> x105, starting transfers between devices: 321 us -> 196 us  [launch(): lax.ppermute(operand, axis, pairs)]
    dot_general x6 -> x3, matrix products: 150 us -> 28.4 us  [contract_rows(): lax.dot_general(left, right, (((0,), (0,)), ((), ())), preferred_element_...]
    all_gather x0 -> x5, waiting for transfers between devices: none -> 70.4 us  [the longest x4 59.5 us: ctx_gather(): return lax.all_gather(block, 'ctx', axis=0, tiled=True)]
    dynamic_update_slice x67 -> x32, local copies, waits for them, and re-layouts: 73.6 us -> 20.1 us  [put(): return lax.dynamic_update_slice(found, piece[None], start)]
    another operation x11 -> x3, local copies, waits for them, and re-layouts: 35.3 us -> 0.19 us  [the longest x2 0.17 us: local(): jnp.stack([jnp.min(lowest[m]) // rows, jnp.minimum(full_from, last), full...]
    dynamic_update_slice x12 -> x0, local copies, waits for them, and re-layouts: 31.9 us -> none  [gather_everywhere(): lax.dynamic_update_slice(found, piece[:, None], (0, here ^ bit, 0, 0))]
  transfers between devices with their start and end apart: 151 -> 112, of which waited for: 67 -> 59; matrix products, arithmetic and copies ran while one was open for 33% -> 32% of each run, Pallas kernels for 3% -> 12%
where the time goes in v2:
time: 1670 us
  waiting for transfers between devices  565 us (34%)
  matrix products  395 us (24%)
  Pallas kernels  204 us (12%)
  starting transfers between devices  196 us (12%)
  other arithmetic  151 us (9%)
  local copies, waits for them, and re-layouts  132 us (8%)
  between operations  21.1 us (1%)
    ppermute x105, waiting for transfers between devices, launch(): lax.ppermute(operand, axis, pairs)  495 us
    dot_general x10, matrix products, dot(): return jnp.dot(left, right, preferred_element_type=out)  197 us
    ppermute x105, starting transfers between devices, launch(): lax.ppermute(operand, axis, pairs)  196 us
    dot_general x9, matrix products, contract_last(): lax.dot_general(left, right, (((1,), (1,)), ((), ())), preferred_element_...  170 us
    pallas_call x3, Pallas kernels, weight_grad(): pl.pallas_call(weight_kernel, out_shape=jax.ShapeDtypeStruct((width, cols...  117 us
    all_gather x4, waiting for transfers between devices, ctx_gather(): return lax.all_gather(block, 'ctx', axis=0, tiled=True)  59.5 us
    convert_element_type x29, other arithmetic, add(): return (first.astype(F32) + second.astype(F32)).astype(BF16)  56.8 us
    unnamed x164, local copies, waits for them, and re-layouts  36.7 us
  transfers between devices with their start and end apart: 112, of which 59 were waited for; matrix products, arithmetic and copies ran while one was open for 32% of the time, Pallas kernels for 12%

profile of v2, /device:TPU:0, one launch (start us, length us, event | category | flops | bytes accessed | tf_op | source)
XLA Modules:
  0.0 1665.0 jit_solution(6794003674284363951)
XLA Ops:
  164.4 23.4 %collective-permute-done.23 = bf16[80,2560]{1,0:T(8,128)(2,1)S(1)} collective-permute-done((bf16[80,2560]{1,0:T(8,128)(2,1)S(1)}, bf16[80,2560]{1,0:T(8,128)(2,1)S(1)}, u32[]{:S(2)}, u32[]{:S(2)}) %collective-permute-start.23) | collective-permute-done | bytes 409632 | tf_op jit(solution)/shard_map/ppermute | solution.py:76
  200.3 16.4 fusion.117
  230.6 24.7 %collective-permute-done.27 = bf16[80,2560]{1,0:T(8,128)(2,1)S(1)} collective-permute-done((bf16[80,2560]{1,0:T(8,128)(2,1)S(1)}, bf16[80,2560]{1,0:T(8,128)(2,1)S(1)}, u32[]{:S(2)}, u32[]{:S(2)}) %collective-permute-start.27) | collective-permute-done | bytes 409632 | tf_op jit(solution)/shard_map/ppermute | solution.py:76
  276.7 63.8 %collective-permute-done.32 = bf16[80,2560]{1,0:T(8,128)(2,1)S(1)} collective-permute-done((bf16[80,2560]{1,0:T(8,128)(2,1)S(1)}, bf16[80,2560]{1,0:T(8,128)(2,1)S(1)}, u32[]{:S(2)}, u32[]{:S(2)}) %collective-permute-start.32) | collective-permute-done | bytes 409632 | tf_op jit(solution)/shard_map/ppermute | solution.py:76
  385.8 15.9 multiply_reduce_fusion
  408.0 85.7 %collective-permute-done.42 = bf16[768,2560]{1,0:T(8,128)(2,1)} collective-permute-done((bf16[768,2560]{1,0:T(8,128)(2,1)}, bf16[768,2560]{1,0:T(8,128)(2,1)}, u32[]{:S(2)}, u32[]{:S(2)}) %collective-permute-start.42) | collective-permute-done | bytes 3932192 | tf_op jit(solution)/shard_map/ppermute | solution.py:76
  510.9 20.6 %fusion.118 = f32[1536,1920]{1,0:T(8,128)} fusion(bf16[1536,2560]{1,0:T(8,128)(2,1)S(1)} %copy-done.27, bf16[2560,1920]{1,0:T(8,128)(2,1)} %all-gather.10.cloned.1.call-done), kind=kOutput, calls=%fused_computation.351 | convolution fusion | flops 15099494400 | bytes 29491200 | tf_op jit(solution)/shard_map/dot_general | solution.py:26
  531.5 19.1 %fusion.119 = f32[1536,1920]{1,0:T(8,128)} fusion(bf16[1536,2560]{1,0:T(8,128)(2,1)S(1)} %copy-done.37, bf16[2560,1920]{1,0:T(8,128)(2,1)S(1)} %bitcast.503), kind=kOutput, calls=%fused_computation.352 | convolution fusion | flops 15099494400 | bytes 29491200 | tf_op jit(solution)/shard_map/dot_general | solution.py:26
  550.7 22.9 %all-gather.12.cloned.1.call-done = bf16[2560,1920]{1,0:T(8,128)(2,1)} async-done(((bf16[320,1920]{1,0:T(8,128)(2,1)}), bf16[2560,1920]{1,0:T(8,128)(2,1)}) %all-gather.12.cloned.1.call-update) | async-done | bytes 9830416 | tf_op jit(solution)/shard_map/all_gather | solution.py:102
  589.8 24.7 %multiply_convert_fusion.3 = (bf16[1536,1920]{1,0:T(8,128)(2,1)S(1)}, f32[1536,1920]{1,0:T(8,128)}) fusion(f32[1536,1920]{1,0:T(8,128)} %fusion.118, bf16[1536,2560]{1,0:T(8,128)(2,1)} %pad_maximum_fusion.a_here, bf16[2560,1920]{1,0:T(8,128)(2,1)} %all-gather.12.cloned.1.call-done), kind=kOutput, calls=%fused_computation.29 | convolution fusion | flops 15128985600 | bytes 47185920 | tf_op jit(solution)/shard_map/dot_general | solution.py:26
  614.4 28.3 %multiply_convert_fusion.2 = (bf16[1536,1920]{1,0:T(8,128)(2,1)}, f32[1536,1920]{1,0:T(8,128)}) fusion(f32[1536,1920]{1,0:T(8,128)} %fusion.119, bf16[1536,2560]{1,0:T(8,128)(2,1)} %constant_dynamic-update-slice_fusion.2.a_there, bf16[2560,1920]{1,0:T(8,128)(2,1)} %all-gather.12.cloned.1.call-done), kind=kOutput, calls=%fused_computation.28 | convolution fusion | flops 15128985600 | bytes 47185920 | tf_op jit(solution)/shard_map/dot_general | solution.py:26
  642.7 39.0 %shard_map.211 = bf16[2560,1920]{1,0:T(8,128)(2,1)} custom-call(bf16[1536,2560]{1,0:T(8,128)(2,1)} %pad_maximum_fusion.1.a_here, bf16[1536,2560]{1,0:T(8,128)(2,1)} %constant_dynamic-update-slice_fusion.4.a_there, bf16[1536,1920]{1,0:T(8,128)(2,1)S(1)} %get-tuple-element.206.b_here, bf16[1536,1920]{1,0:T(8,128)(2,1)} %get-tuple-element.205.b_there), custom_call_target="tpu_custom_call" | custom-call | flops 30198988800 | bytes 37355520 | tf_op jit(solution)/shard_map/pallas_call | solution.py:506
  681.8 36.6 %all-gather.14.cloned.1.call-done = bf16[2560,1920]{1,0:T(8,128)(2,1)} async-done(((bf16[320,1920]{1,0:T(8,128)(2,1)}), bf16[2560,1920]{1,0:T(8,128)(2,1)}) %all-gather.14.cloned.1.call-update) | async-done | bytes 9830416 | tf_op jit(solution)/shard_map/all_gather | solution.py:102
  718.3 20.9 %fusion.120 = bf16[1536,2560]{1,0:T(8,128)(2,1)S(1)} fusion(bf16[1536,1920]{1,0:T(8,128)(2,1)} %get-tuple-element.205.b_there, bf16[2560,1920]{1,0:T(8,128)(2,1)} %all-gather.14.cloned.1.call-done), kind=kOutput, calls=%fused_computation.353 | convolution fusion | flops 15099494400 | bytes 23592960 | tf_op jit(solution)/shard_map/dot_general | solution.py:34
  747.3 20.8 %fusion.121 = bf16[1536,2560]{1,0:T(8,128)(2,1)S(1)} fusion(bf16[1536,1920]{1,0:T(8,128)(2,1)} %copy-done.11, bf16[2560,1920]{1,0:T(8,128)(2,1)} %all-gather.14.cloned.1.call-done), kind=kOutput, calls=%fused_computation.354 | convolution fusion | flops 15099494400 | bytes 23592960 | tf_op jit(solution)/shard_map/dot_general | solution.py:34
  782.1 33.2 %multiply_convert_fusion.1 = (bf16[1536,1920]{1,0:T(8,128)(2,1)}, bf16[1536,1920]{1,0:T(8,128)(2,1)S(1)}) fusion(f32[1536,1920]{1,0:T(8,128)} %fusion.118, f32[1536,1920]{1,0:T(8,128)} %get-tuple-element.439, bf16[1536,2560]{1,0:T(8,128)(2,1)} %pad_maximum_fusion.1.a_here, bf16[2560,1920]{1,0:T(8,128)(2,1)} %all-gather.14.cloned.1.call-done), kind=kOutput, calls=%fused_computation.27 | convolution fusion | flops 15170273280 | bytes 53084160 | tf_op jit(solution)/shard_map/dot_general | solution.py:26
  815.3 36.0 %multiply_convert_fusion = (bf16[1536,1920]{1,0:T(8,128)(2,1)}, bf16[1536,1920]{1,0:T(8,128)(2,1)}) fusion(f32[1536,1920]{1,0:T(8,128)} %fusion.119, f32[1536,1920]{1,0:T(8,128)} %get-tuple-element.441, bf16[1536,2560]{1,0:T(8,128)(2,1)} %constant_dynamic-update-slice_fusion.4.a_there, bf16[2560,1920]{1,0:T(8,128)(2,1)} %all-gather.14.cloned.1.call-done), kind=kOutput, calls=%fused_computation.26 | convolution fusion | flops 15170273280 | bytes 53084160 | tf_op jit(solution)/shard_map/dot_general | solution.py:26
  851.3 39.4 %shard_map.212 = bf16[2560,1920]{1,0:T(8,128)(2,1)} custom-call(bf16[1536,2560]{1,0:T(8,128)(2,1)} %pad_maximum_fusion.a_here, bf16[1536,2560]{1,0:T(8,128)(2,1)} %constant_dynamic-update-slice_fusion.2.a_there, bf16[1536,1920]{1,0:T(8,128)(2,1)S(1)} %get-tuple-element.216.b_here, bf16[1536,1920]{1,0:T(8,128)(2,1)} %get-tuple-element.213.b_there), custom_call_target="tpu_custom_call" | custom-call | flops 30198988800 | bytes 37355520 | tf_op jit(solution)/shard_map/pallas_call | solution.py:506
  890.7 22.5 %fusion.122 = f32[1536,2560]{1,0:T(8,128)} fusion(bf16[1536,1920]{1,0:T(8,128)(2,1)} %get-tuple-element.213.b_there, bf16[2560,1920]{1,0:T(8,128)(2,1)} %all-gather.10.cloned.1.call-done), kind=kOutput, calls=%fused_computation.355 | convolution fusion | flops 15099494400 | bytes 31457280 | tf_op jit(solution)/shard_map/dot_general | solution.py:34
  913.2 24.3 %add_convert_fusion.1 = bf16[1536,2560]{1,0:T(8,128)(2,1)} fusion(f32[1536,2560]{1,0:T(8,128)} %fusion.122, bf16[1536,1920]{1,0:T(8,128)(2,1)} %get-tuple-element.214.b_there, bf16[2560,1920]{1,0:T(8,128)(2,1)} %all-gather.12.cloned.1.call-done), kind=kOutput, calls=%fused_computation.5 | convolution fusion | flops 15107358720 | bytes 39321600 | tf_op jit(solution)/shard_map/dot_general | solution.py:34
  942.0 22.8 %fusion.123 = f32[1536,2560]{1,0:T(8,128)} fusion(bf16[1536,1920]{1,0:T(8,128)(2,1)} %copy-done.12, bf16[2560,1920]{1,0:T(8,128)(2,1)} %all-gather.10.cloned.1.call-done), kind=kOutput, calls=%fused_computation.356 | convolution fusion | flops 15099494400 | bytes 31457280 | tf_op jit(solution)/shard_map/dot_general | solution.py:34
  964.8 24.6 %add_convert_fusion = bf16[1536,2560]{1,0:T(8,128)(2,1)} fusion(f32[1536,2560]{1,0:T(8,128)} %fusion.123, bf16[1536,1920]{1,0:T(8,128)(2,1)} %get-tuple-element.217.b_here, bf16[2560,1920]{1,0:T(8,128)(2,1)} %all-gather.12.cloned.1.call-done), kind=kOutput, calls=%fused_computation.4 | convolution fusion | flops 15107358720 | bytes 39321600 | tf_op jit(solution)/shard_map/dot_general | solution.py:34
  1001.8 39.0 %shard_map.213 = bf16[2560,1920]{1,0:T(8,128)(2,1)} custom-call(bf16[1536,2560]{1,0:T(8,128)(2,1)} %pad_maximum_fusion.a_here, bf16[1536,2560]{1,0:T(8,128)(2,1)} %constant_dynamic-update-slice_fusion.2.a_there, bf16[1536,1920]{1,0:T(8,128)(2,1)S(1)} %bitcast.451, bf16[1536,1920]{1,0:T(8,128)(2,1)} %get-tuple-element.214.b_there), custom_call_target="tpu_custom_call" | custom-call | flops 30198988800 | bytes 37355520 | tf_op jit(solution)/shard_map/pallas_call | solution.py:506
  1049.6 19.6 %collective-permute-done.50 = bf16[160,1920]{1,0:T(8,128)(2,1)S(1)} collective-permute-done((bf16[160,1920]{1,0:T(8,128)(2,1)S(1)}, bf16[160,1920]{1,0:T(8,128)(2,1)S(1)}, u32[]{:S(2)}, u32[]{:S(2)}) %collective-permute-start.50) | collective-permute-done | bytes 614432 | tf_op jit(solution)/shard_map/ppermute | solution.py:76
  1095.3 16.4 shard_map.214
  1113.7 14.4 collective-permute-start.55
  1131.3 13.1 collective-permute-done.56
  1265.6 17.1 %shard_map.215 = (bf16[384,2560]{1,0:T(8,128)(2,1)S(1)}, bf16[8,384,512]{2,1,0:T(8,128)(2,1)}) custom-call(s32[6]{0:T(128)S(1)} %copy-done.8, bf16[384,2560]{1,0:T(8,128)(2,1)S(1)} %get-tuple-element.184.q_ref, bf16[8,768,512]{2,1,0:T(8,128)(2,1)} %bitcast.463, s32[1,768]{1,0:T(1,128)S(1)} %bitcast.447, s32[1,768]{1,0:T(1,128)S(1)} %bitcast.445, ...), custom_call_target="tpu_custom_call" | custom-call | flops 1024 | bytes 1024 | tf_op jit(solution)/shard_map/pallas_call | solution.py:730
  1348.0 13.6 collective-permute-done.67
  1376.3 14.4 collective-permute-done.71
  1409.7 15.5 fusion.128
  1534.3 57.9 %collective-permute-done.81 = bf16[8,80,640]{2,1,0:T(8,128)(2,1)S(1)} collective-permute-done((bf16[8,80,640]{2,1,0:T(8,128)(2,1)S(1)}, bf16[8,80,640]{2,1,0:T(8,128)(2,1)S(1)}, u32[]{:S(2)}, u32[]{:S(2)}) %collective-permute-start.81) | collective-permute-done | bytes 819232 | tf_op jit(solution)/shard_map/ppermute | solution.py:76
  (579 shorter events, 757.3 us)
Async XLA Ops:
  7.2 70.9 %all-gather.6.cloned.1.call-start = ((), (), s32[]{:S(2)}) async-start(), calls=%async_computation.2 | async-start | bytes 3379200 | tf_op jit(solution)/shard_map/all_gather | solution.py:548
  15.5 201.2 %all-gather.8.cloned.1.call-start = ((), (), s32[]{:S(2)}) async-start(), calls=%async_computation.3 | async-start | bytes 7077888 | tf_op jit(solution)/shard_map/all_gather | solution.py:102
  95.4 310.6 %all-gather.10.cloned.1.call-start = ((), (), s32[]{:S(2)}) async-start(), calls=%async_computation.4 | async-start | bytes 11059200 | tf_op jit(solution)/shard_map/all_gather | solution.py:102
  133.8 54.9 %collective-permute-start.20 = (bf16[8,80,2560]{2,1,0:T(8,128)(2,1)}, bf16[8,80,2560]{2,1,0:T(8,128)(2,1)}, u32[]{:S(2)}, u32[]{:S(2)}) collective-permute-start(bf16[8,80,2560]{2,1,0:T(8,128)(2,1)} %bitcast_dynamic-update-slice_fusion.27.refs_0_), channel_id=1, source_target_pairs={{0,1},{1,0},{2,3},{3,2},{4,5},{5,4},{6,7},{7,6},{8,9},{9,8},{10,11... | collective-permute-start | bytes 9830408 | tf_op jit(solution)/shard_map/ppermute | solution.py:76
  134.5 54.1 %collective-permute-start.21 = (bf16[8,80,2560]{2,1,0:T(8,128)(2,1)}, bf16[8,80,2560]{2,1,0:T(8,128)(2,1)}, u32[]{:S(2)}, u32[]{:S(2)}) collective-permute-start(bf16[8,80,2560]{2,1,0:T(8,128)(2,1)} %bitcast_dynamic-update-slice_fusion.26.refs_2_), channel_id=1, source_target_pairs={{0,1},{1,0},{2,3},{3,2},{4,5},{5,4},{6,7},{7,6},{8,9},{9,8},{10,11... | collective-permute-start | bytes 9830408 | tf_op jit(solution)/shard_map/ppermute | solution.py:76
  143.9 72.8 %collective-permute-start.24 = (bf16[80,2560]{1,0:T(8,128)(2,1)S(1)}, bf16[80,2560]{1,0:T(8,128)(2,1)S(1)}, u32[]{:S(2)}, u32[]{:S(2)}) collective-permute-start(bf16[80,2560]{1,0:T(8,128)(2,1)S(1)} %collective-permute-done.17), channel_id=1, source_target_pairs={{0,2},{1,3},{2,0},{3,1},{4,6},{5,7},{6,4},{7,5},{8,10},{9,11},{10,... | collective-permute-start | bytes 1228808 | tf_op jit(solution)/shard_map/ppermute | solution.py:76
  145.2 42.7 %collective-permute-start.23 = (bf16[80,2560]{1,0:T(8,128)(2,1)S(1)}, bf16[80,2560]{1,0:T(8,128)(2,1)S(1)}, u32[]{:S(2)}, u32[]{:S(2)}) collective-permute-start(bf16[80,2560]{1,0:T(8,128)(2,1)S(1)} %collective-permute-done.18), channel_id=1, source_target_pairs={{0,4},{8,0},{16,8},{24,16},{28,24},{20,28},{12,20},{4,12},{1,5},{9... | collective-permute-start | bytes 1228808 | tf_op jit(solution)/shard_map/ppermute | solution.py:76
  162.8 53.9 %collective-permute-start.25 = (bf16[80,2560]{1,0:T(8,128)(2,1)S(1)}, bf16[80,2560]{1,0:T(8,128)(2,1)S(1)}, u32[]{:S(2)}, u32[]{:S(2)}) collective-permute-start(bf16[80,2560]{1,0:T(8,128)(2,1)S(1)} %collective-permute-done.18), channel_id=1, source_target_pairs={{0,2},{1,3},{2,0},{3,1},{4,6},{5,7},{6,4},{7,5},{8,10},{9,11},{10,... | collective-permute-start | bytes 1228808 | tf_op jit(solution)/shard_map/ppermute | solution.py:76
  216.7 356.9 %all-gather.12.cloned.1.call-start = ((), (), s32[]{:S(2)}) async-start(), calls=%async_computation.5 | async-start | bytes 11059200 | tf_op jit(solution)/shard_map/all_gather | solution.py:102
  229.6 132.0 %collective-permute-start.36 = (bf16[768,2560]{1,0:T(8,128)(2,1)S(1)}, bf16[768,2560]{1,0:T(8,128)(2,1)}, u32[]{:S(2)}, u32[]{:S(2)}) collective-permute-start(bf16[768,2560]{1,0:T(8,128)(2,1)S(1)} %bitcast.472), channel_id=1, source_target_pairs={{0,1},{1,0},{2,3},{3,2},{4,5},{5,4},{6,7},{7,6},{8,9},{9,8},{10,11... | collective-permute-start | bytes 11796488 | tf_op jit(solution)/shard_map/ppermute | solution.py:76
  229.7 131.9 %collective-permute-start.37 = (bf16[768,2560]{1,0:T(8,128)(2,1)S(1)}, bf16[768,2560]{1,0:T(8,128)(2,1)}, u32[]{:S(2)}, u32[]{:S(2)}) collective-permute-start(bf16[768,2560]{1,0:T(8,128)(2,1)S(1)} %bitcast.473), channel_id=1, source_target_pairs={{0,2},{1,3},{2,0},{3,1},{4,6},{5,7},{6,4},{7,5},{8,10},{9,11},{10,... | collective-permute-start | bytes 11796488 | tf_op jit(solution)/shard_map/ppermute | solution.py:76
  258.3 82.1 %collective-permute-start.32 = (bf16[80,2560]{1,0:T(8,128)(2,1)S(1)}, bf16[80,2560]{1,0:T(8,128)(2,1)S(1)}, u32[]{:S(2)}, u32[]{:S(2)}) collective-permute-start(bf16[80,2560]{1,0:T(8,128)(2,1)S(1)} %collective-permute-done.26), channel_id=1, source_target_pairs={{0,2},{1,3},{2,0},{3,1},{4,6},{5,7},{6,4},{7,5},{8,10},{9,11},{10,... | collective-permute-start | bytes 1228808 | tf_op jit(solution)/shard_map/ppermute | solution.py:76
  275.2 70.6 %collective-permute-start.33 = (bf16[80,2560]{1,0:T(8,128)(2,1)S(1)}, bf16[80,2560]{1,0:T(8,128)(2,1)S(1)}, u32[]{:S(2)}, u32[]{:S(2)}) collective-permute-start(bf16[80,2560]{1,0:T(8,128)(2,1)S(1)} %collective-permute-done.27), channel_id=1, source_target_pairs={{0,2},{1,3},{2,0},{3,1},{4,6},{5,7},{6,4},{7,5},{8,10},{9,11},{10,... | collective-permute-start | bytes 1228808 | tf_op jit(solution)/shard_map/ppermute | solution.py:76
  363.6 42.4 %collective-permute-start.41 = (bf16[768,2560]{1,0:T(8,128)(2,1)}, bf16[768,2560]{1,0:T(8,128)(2,1)}, u32[]{:S(2)}, u32[]{:S(2)}) collective-permute-start(bf16[768,2560]{1,0:T(8,128)(2,1)} %collective-permute-done.37), channel_id=1, source_target_pairs={{0,1},{1,0},{2,3},{3,2},{4,5},{5,4},{6,7},{7,6},{8,9},{9,8},{10,11... | collective-permute-start | bytes 11796488 | tf_op jit(solution)/shard_map/ppermute | solution.py:76
  406.0 312.3 %all-gather.14.cloned.1.call-start = ((), (), s32[]{:S(2)}) async-start(), calls=%async_computation.6 | async-start | bytes 11059200 | tf_op jit(solution)/shard_map/all_gather | solution.py:102
  406.1 87.6 %collective-permute-start.42 = (bf16[768,2560]{1,0:T(8,128)(2,1)}, bf16[768,2560]{1,0:T(8,128)(2,1)}, u32[]{:S(2)}, u32[]{:S(2)}) collective-permute-start(bf16[768,2560]{1,0:T(8,128)(2,1)} %multiply_convert_fusion.4), channel_id=1, source_target_pairs={{0,2},{1,3},{2,0},{3,1},{4,6},{5,7},{6,4},{7,5},{8,10},{9,11},{10,... | collective-permute-start | bytes 11796488 | tf_op jit(solution)/shard_map/ppermute | solution.py:76
  407.9 85.8 %collective-permute-start.40 = (bf16[768,2560]{1,0:T(8,128)(2,1)}, bf16[768,2560]{1,0:T(8,128)(2,1)}, u32[]{:S(2)}, u32[]{:S(2)}) collective-permute-start(bf16[768,2560]{1,0:T(8,128)(2,1)} %multiply_convert_fusion.4), channel_id=1, source_target_pairs={{0,1},{1,0},{2,3},{3,2},{4,5},{5,4},{6,7},{7,6},{8,9},{9,8},{10,11... | collective-permute-start | bytes 11796488 | tf_op jit(solution)/shard_map/ppermute | solution.py:76
  573.6 368.3 %reduce-scatter.3.cloned.1.call-start = ((), (), s32[]{:S(2)}) async-start(), calls=%async_computation.7 | async-start | bytes 11059200 | tf_op jit(solution)/shard_map/reduce_scatter | solution.py:106
  681.7 468.3 %reduce-scatter.5.cloned.1.call-start = ((), (), s32[]{:S(2)}) async-start(), calls=%async_computation.8 | async-start | bytes 11059200 | tf_op jit(solution)/shard_map/reduce_scatter | solution.py:106
  774.1 77.2 %collective-permute-start.44 = (bf16[768,2560]{1,0:T(8,128)(2,1)}, bf16[768,2560]{1,0:T(8,128)(2,1)}, u32[]{:S(2)}, u32[]{:S(2)}) collective-permute-start(bf16[768,2560]{1,0:T(8,128)(2,1)} %slice.437), channel_id=1, source_target_pairs={{0,1},{1,0},{2,3},{3,2},{4,5},{5,4},{6,7},{7,6},{8,9},{9,8},{10,11... | collective-permute-start | bytes 11796488 | tf_op jit(solution)/shard_map/ppermute | solution.py:76
  780.6 110.1 %collective-permute-start.46 = (bf16[768,2560]{1,0:T(8,128)(2,1)}, bf16[768,2560]{1,0:T(8,128)(2,1)}, u32[]{:S(2)}, u32[]{:S(2)}) collective-permute-start(bf16[768,2560]{1,0:T(8,128)(2,1)} %add_convert_fusion.3), channel_id=1, source_target_pairs={{0,2},{1,3},{2,0},{3,1},{4,6},{5,7},{6,4},{7,5},{8,10},{9,11},{10,... | collective-permute-start | bytes 11796488 | tf_op jit(solution)/shard_map/ppermute | solution.py:76
  941.9 52.4 %collective-permute-start.48 = (bf16[768,2560]{1,0:T(8,128)(2,1)}, bf16[768,2560]{1,0:T(8,128)(2,1)}, u32[]{:S(2)}, u32[]{:S(2)}) collective-permute-start(bf16[768,2560]{1,0:T(8,128)(2,1)} %slice.439), channel_id=1, source_target_pairs={{0,1},{1,0},{2,3},{3,2},{4,5},{5,4},{6,7},{7,6},{8,9},{9,8},{10,11... | collective-permute-start | bytes 11796488 | tf_op jit(solution)/shard_map/ppermute | solution.py:76
  993.9 50.7 %collective-permute-start.47 = (bf16[768,2560]{1,0:T(8,128)(2,1)}, bf16[768,2560]{1,0:T(8,128)(2,1)}, u32[]{:S(2)}, u32[]{:S(2)}) collective-permute-start(bf16[768,2560]{1,0:T(8,128)(2,1)} %slice.441), channel_id=1, source_target_pairs={{0,1},{1,0},{2,3},{3,2},{4,5},{5,4},{6,7},{7,6},{8,9},{9,8},{10,11... | collective-permute-start | bytes 11796488 | tf_op jit(solution)/shard_map/ppermute | solution.py:76
  1001.0 73.9 %collective-permute-start.49 = (bf16[384,2560]{1,0:T(8,128)(2,1)}, bf16[384,2560]{1,0:T(8,128)(2,1)S(1)}, u32[]{:S(2)}, u32[]{:S(2)}) collective-permute-start(bf16[384,2560]{1,0:T(8,128)(2,1)} %get-tuple-element.220), channel_id=1, source_target_pairs={{0,2},{1,3},{2,0},{3,1},{4,6},{5,7},{6,4},{7,5},{8,10},{9,11},{10,... | collective-permute-start | bytes 5898248 | tf_op jit(solution)/shard_map/ppermute | solution.py:76
  1080.0 70.0 %collective-permute-start.52 = (bf16[384,2560]{1,0:T(8,128)(2,1)}, bf16[384,2560]{1,0:T(8,128)(2,1)}, u32[]{:S(2)}, u32[]{:S(2)}) collective-permute-start(bf16[384,2560]{1,0:T(8,128)(2,1)} %get-tuple-element.227), channel_id=1, source_target_pairs={{0,2},{1,3},{2,0},{3,1},{4,6},{5,7},{6,4},{7,5},{8,10},{9,11},{10,... | collective-permute-start | bytes 5898248 | tf_op jit(solution)/shard_map/ppermute | solution.py:76
  1081.4 64.1 %collective-permute-start.53 = (bf16[320,1920]{1,0:T(8,128)(2,1)}, bf16[320,1920]{1,0:T(8,128)(2,1)}, u32[]{:S(2)}, u32[]{:S(2)}) collective-permute-start(bf16[320,1920]{1,0:T(8,128)(2,1)} %pad_maximum_fusion.4), channel_id=1, source_target_pairs={{0,8},{8,16},{16,24},{24,28},{28,20},{20,12},{12,4},{4,0},{1,9},{9... | collective-permute-start | bytes 3686408 | tf_op jit(solution)/shard_map/ppermute | solution.py:76
  1083.3 62.3 %collective-permute-start.54 = (bf16[320,1920]{1,0:T(8,128)(2,1)}, bf16[320,1920]{1,0:T(8,128)(2,1)}, u32[]{:S(2)}, u32[]{:S(2)}) collective-permute-start(bf16[320,1920]{1,0:T(8,128)(2,1)} %pad_maximum_fusion.5), channel_id=1, source_target_pairs={{0,4},{8,0},{16,8},{24,16},{28,24},{20,28},{12,20},{4,12},{1,5},{9... | collective-permute-start | bytes 3686408 | tf_op jit(solution)/shard_map/ppermute | solution.py:76
  1242.1 42.2 %collective-permute-start.64 = (bf16[320,1920]{1,0:T(8,128)(2,1)}, bf16[320,1920]{1,0:T(8,128)(2,1)}, u32[]{:S(2)}, u32[]{:S(2)}) collective-permute-start(bf16[320,1920]{1,0:T(8,128)(2,1)} %get-tuple-element.247), channel_id=1, source_target_pairs={{0,8},{8,16},{16,24},{24,28},{28,20},{20,12},{12,4},{4,0},{1,9},{9... | collective-permute-start | bytes 3686408 | tf_op jit(solution)/shard_map/ppermute | solution.py:76
  1309.1 87.0 %collective-permute-start.70 = (bf16[8,2,80,2560]{3,2,0,1:T(8,128)(2,1)}, bf16[8,2,80,2560]{3,2,0,1:T(8,128)(2,1)}, u32[]{:S(2)}, u32[]{:S(2)}) collective-permute-start(bf16[8,2,80,2560]{3,2,0,1:T(8,128)(2,1)} %bitcast.439), channel_id=1, source_target_pairs={{0,1},{1,0},{2,3},{3,2},{4,5},{5,4},{6,7},{7,6},{8,9},{9,8},{10,11... | collective-permute-start | bytes 19660808 | tf_op jit(solution)/shard_map/ppermute | solution.py:76
  1309.2 81.5 %collective-permute-start.71 = (bf16[8,80,2560]{2,1,0:T(8,128)(2,1)}, bf16[8,80,2560]{2,1,0:T(8,128)(2,1)}, u32[]{:S(2)}, u32[]{:S(2)}) collective-permute-start(bf16[8,80,2560]{2,1,0:T(8,128)(2,1)} %dynamic-slice_bitcast_fusion.1), channel_id=1, source_target_pairs={{0,2},{1,3},{2,0},{3,1},{4,6},{5,7},{6,4},{7,5},{8,10},{9,11},{10,... | collective-permute-start | bytes 9830408 | tf_op jit(solution)/shard_map/ppermute | solution.py:76
  1501.1 91.3 %collective-permute-start.84 = (bf16[8,80,2560]{2,1,0:T(8,128)(2,1)}, bf16[8,80,2560]{2,1,0:T(8,128)(2,1)S(1)}, u32[]{:S(2)}, u32[]{:S(2)}) collective-permute-start(bf16[8,80,2560]{2,1,0:T(8,128)(2,1)} %dynamic-slice_bitcast_fusion), channel_id=1, source_target_pairs={{0,2},{1,3},{2,0},{3,1},{4,6},{5,7},{6,4},{7,5},{8,10},{9,11},{10,... | collective-permute-start | bytes 9830408 | tf_op jit(solution)/shard_map/ppermute | solution.py:76
  1519.9 72.2 %collective-permute-start.81 = (bf16[8,80,640]{2,1,0:T(8,128)(2,1)S(1)}, bf16[8,80,640]{2,1,0:T(8,128)(2,1)S(1)}, u32[]{:S(2)}, u32[]{:S(2)}) collective-permute-start(bf16[8,80,640]{2,1,0:T(8,128)(2,1)S(1)} %dynamic-slice_bitcast_fusion.3), channel_id=1, source_target_pairs={{0,2},{1,3},{2,0},{3,1},{4,6},{5,7},{6,4},{7,5},{8,10},{9,11},{10,... | collective-permute-start | bytes 2457608 | tf_op jit(solution)/shard_map/ppermute | solution.py:76
  (156 other events, 3238.6 us)
Sparse Core Ops, SparseCore 0:
  15.6 62.4 all-gather.5
  95.5 111.2 all-gather.7
  216.8 151.9 all-gather.9
  406.1 167.4 all-gather.11
  575.6 142.6 all-gather.13
  721.8 167.0 reduce-scatter.2
  892.6 177.8 reduce-scatter.4

commit v3 on v2

--- a/solution.py
+++ b/solution.py
@@ -15,7 +15,6 @@
 LN2 = math.log(2.0)
 F32 = jnp.float32
 BF16 = jnp.bfloat16
-SHORT = pl.CostEstimate(flops=1024, bytes_accessed=1024, transcendentals=0)
 
 
 def rms_scale(values, gain):
@@ -237,7 +236,7 @@
                 mine = put(mine, piece, offset, row)
             wanted, _ = next(blocks, (None, None))
     near, last = yield [core_swap(mine), core_swap(far)]
-    return interleave(here, mine, near, far, last).reshape(-1, width)
+    return interleave(here, mine, near, far, last).reshape(-1, width), mine
 
 
 def interleave_kernel(here, *refs):
@@ -257,7 +256,9 @@
             in_specs=[pl.BlockSpec((1, rows, width), lambda i, here: (i, 0, 0))] * 4,
             out_specs=pl.BlockSpec((1, 4, rows, width), lambda i, here: (i, 0, 0, 0)),
         ),
-        cost_estimate=SHORT,
+        cost_estimate=pl.CostEstimate(
+            flops=0, bytes_accessed=16 * count * rows * width, transcendentals=0
+        ),
     )(here.reshape(1), *pieces)
 
 
@@ -317,10 +318,6 @@
     return (index >= low) & (index <= high)
 
 
-def key_parts(keys):
-    return [slice(0, keys)]
-
-
 def attend_kernel(
     spans, q_ref, kv_ref, low_ref, high_ref, cos_ref, sin_ref,
     out_ref, qrot_ref, lse_ref, vt_ref, *, heads, size, keys,
@@ -341,27 +338,17 @@
         turned.append(part.T)
     qt = jnp.concatenate(turned, axis=1)
     low, high = low_ref[...], high_ref[...]
-    parts = key_parts(keys)
 
     def step(block, carry, masked):
         top, total, acc = carry
-        scores = []
-        for part in parts:
-            piece = dot(kv_ref[block, part, :size], qt)
-            if masked:
-                seen = visible(block * keys + part.start, part.stop - part.start, low, high)
-                piece = jnp.where(seen, piece, NEGATIVE)
-            scores.append(piece)
-        new_top = top
-        for piece in scores:
-            new_top = jnp.maximum(new_top, jnp.max(piece, axis=0, keepdims=True))
+        scores = dot(kv_ref[block, :, :size], qt)
+        if masked:
+            scores = jnp.where(visible(block * keys, keys, low, high), scores, NEGATIVE)
+        new_top = jnp.maximum(top, jnp.max(scores, axis=0, keepdims=True))
+        probs = jnp.exp2(scores - new_top)
         fade = jnp.exp2(top - new_top)
-        total = total * fade
-        acc = acc * fade
-        for part, piece in zip(parts, scores):
-            probs = jnp.exp2(piece - new_top)
-            total = total + jnp.sum(probs, axis=0, keepdims=True)
-            acc = acc + dot(vt_ref[block, :, part], probs.astype(BF16))
+        total = total * fade + jnp.sum(probs, axis=0, keepdims=True)
+        acc = acc * fade + dot(vt_ref[block], probs.astype(BF16))
         return new_top, total, acc
 
     carry = (
@@ -403,18 +390,15 @@
     low, high, lse = low_ref[...], high_ref[...], lse_ref[0]
 
     def step(block, dq, masked):
-        for part in key_parts(keys):
-            scores = dot(kv_ref[block, part, :size], qt)
-            if masked:
-                seen = visible(block * keys + part.start, part.stop - part.start, low, high)
-                scores = jnp.where(seen, scores, NEGATIVE)
-            probs = jnp.exp2(scores - lse)
-            probs_grad = dot(kv_ref[block, part, size:], grad_t)
-            score_grad = (probs * (probs_grad - delta)).astype(BF16)
-            dv_ref[block, part] += dot(probs.astype(BF16), grad)
-            dk_ref[block, part] += dot(score_grad, q)
-            dq = dq + dot(kt_ref[block, :, part], score_grad)
-        return dq
+        scores = dot(kv_ref[block, :, :size], qt)
+        if masked:
+            scores = jnp.where(visible(block * keys, keys, low, high), scores, NEGATIVE)
+        probs = jnp.exp2(scores - lse)
+        probs_grad = dot(kv_ref[block, :, size:], grad_t)
+        score_grad = (probs * (probs_grad - delta)).astype(BF16)
+        dv_ref[block] += dot(probs.astype(BF16), grad)
+        dk_ref[block] += dot(score_grad, q)
+        return dq + dot(kt_ref[block], score_grad)
 
     dq = jnp.zeros((size, heads * rows), F32)
     dq = lax.fori_loop(spans[0], spans[1], functools.partial(step, masked=True), dq)
@@ -461,7 +445,9 @@
             scratch_shapes=[pltpu.VMEM((count, size, keys), BF16)],
         ),
         compiler_params=params,
-        cost_estimate=SHORT,
+        cost_estimate=pl.CostEstimate(
+            flops=2 * work, bytes_accessed=rows * width * 8, transcendentals=work // size // 2
+        ),
     )
     backward = pl.pallas_call(
         functools.partial(attend_back_kernel, **sizes),
@@ -477,7 +463,9 @@
             ],
         ),
         compiler_params=params,
-        cost_estimate=SHORT,
+        cost_estimate=pl.CostEstimate(
+            flops=5 * work, bytes_accessed=rows * width * 10, transcendentals=work // size // 2
+        ),
     )
     return forward, backward, heads
 
@@ -543,18 +531,16 @@
         [jnp.stack([gain_attn, gain_mlp], axis=1), id_flat.reshape(slots, id_cols)], axis=1
     )
     beside = jnp.pad(beside, ((0, 0), (0, -beside.shape[1] % 128)))
-    everyone = ("ctx", "wt")
-    narrow_in = Whole(
-        plan, lambda block: lax.all_gather(block, everyone, axis=0, tiled=True),
-        jnp.concatenate([w_key, w_value, beside], axis=1),
-    )
+    narrow_in = plan.start(gather_everywhere(jnp.concatenate([w_key, w_value, beside], axis=1)))
     query_in = plan.start(gather_everywhere(w_query))
+    gate_in = Whole(plan, ctx_gather, w_gate)
+    for _ in range(3):
+        plan.step(narrow_in)
     plan.step(query_in)
+    plan.step(narrow_in)
+    plan.step(narrow_in)
     plan.step(query_in)
-    narrow_full = narrow_in.end()
-    narrow_ring = lax.dynamic_index_in_dim(
-        narrow_full.reshape(count, 4, slots, -1), lax.axis_index("wt"), 1, keepdims=False
-    )
+    narrow_full, narrow_ring = narrow_in.end()
     w_kv = narrow_full[:, : 2 * size]
     gain_first = narrow_full[:, 2 * size].astype(F32)
     gain_second = narrow_full[:, 2 * size + 1].astype(F32)
@@ -585,22 +571,25 @@
         return normed, jnp.concatenate([rotate(keys, *twice), both[:, size:]], axis=1).astype(BF16)
 
     normed, turned = plan.run(project_kv, tokens, gain_first, w_kv, cosine, sine)
-    kv_in = Whole(plan, ctx_gather, turned)
+    kv_in = plan.start(ring_gather(turned))
     plan.step(query_in)
+    plan.step(kv_in)
     plan.step(query_in)
     out_in = plan.start(gather_everywhere(plan.hold(w_out).T))
+    plan.step(kv_in)
     plan.step(query_in)
-    plan.step(out_in)
-    query_full = query_in.end()
     cot = plan.hold(cotangent).reshape(micros * rows, width)
     cot_near, cot_far = plan.start(once(core_swap(cot))), plan.start(rows_there(cot))
+    plan.step(out_in)
+    query_full, _ = query_in.end()
+    gate_full = gate_in.end()
     queries = plan.run(lambda a, b: dot(a, b).reshape(micros, rows, -1), normed, query_full)
+    plan.step(kv_in)
     plan.step(out_in)
-    kv_all = kv_in.end().reshape(count, micros * rows, 2 * size)
-    gate_in = Whole(plan, ctx_gather, w_gate)
-    plan.step(out_in)
 
     saved = []
+    kv_all = kv_in.end()
+    up_in = Whole(plan, ctx_gather, w_up)
     for m in range(micros):
         full_from = (jnp.max(lowest[m]) + rows - 1) // rows
         full_to = (first + 1) // rows
@@ -626,8 +615,7 @@
         plan.step(out_in)
 
     attended = jnp.concatenate([entry[3][:rows] for entry in saved], axis=0)
-    plan.step(cot_near, cot_far)
-    out_full = out_in.end()
+    out_full, _ = out_in.end()
 
     def join(attended, tokens, weights, gain):
         middle = tokens.reshape(micros * rows, width).astype(F32) + contract_last(attended, weights)
@@ -636,15 +624,10 @@
     middle, low = plan.run(join, attended, tokens, out_full, gain_second)
     near_in, far_in = plan.start(once(core_swap(low))), plan.start(rows_there(low))
 
-    cot_rows = [
-        jnp.concatenate([cot, cot_near.end()], axis=0), jnp.concatenate(cot_far.end(), axis=0)
-    ]
-    gate_full = gate_in.end()
-    up_in = Whole(plan, ctx_gather, w_up)
-    normed_rows = [
-        jnp.concatenate([low, near_in.end()], axis=0), jnp.concatenate(far_in.end(), axis=0)
-    ]
-    gate_rows = [plan.run(dot, rows_in, gate_full) for rows_in in normed_rows]
+    plan.step(cot_near)
+    normed_rows = [jnp.concatenate([low, near_in.end()], axis=0)]
+    gate_rows = [plan.run(dot, normed_rows[0], gate_full)]
+    cot_rows = [jnp.concatenate([cot, cot_near.end()], axis=0)]
     up_full = up_in.end()
     down_in = Whole(plan, ctx_gather, w_down.T)
 
@@ -653,10 +636,19 @@
         return up, (jax.nn.gelu(gate) * up).astype(BF16)
 
     up_rows, hidden = [], []
-    for side in range(2):
+
+    def hidden_half(side):
         up, both = plan.run(make_hidden, normed_rows[side], up_full, gate_rows[side])
         up_rows.append(up)
         hidden.append(both)
+
+    hidden_half(0)
+    plan.step(far_in)
+    normed_rows.append(jnp.concatenate(far_in.end(), axis=0))
+    gate_rows.append(plan.run(dot, normed_rows[1], gate_full))
+    hidden_half(1)
+    plan.step(cot_far)
+    cot_rows.append(jnp.concatenate(cot_far.end(), axis=0))
 
     def weight_sum(left, right):
         terms = plan.run(lambda a, *rest: weight_grad((a, left[1]), right), left[0])
@@ -699,10 +691,7 @@
         )
 
     back_here, back_there = both_halves(rows_back, micros, down_out.end)
-    up_terms = plan.run(
-        lambda a, *rest: weight_grad((a, normed_rows[1]), up_grad), normed_rows[0]
-    )
-    up_out = plan.start(ring_scatter(up_terms.reshape(count, -1, hidden_cols)))
+    up_out = weight_sum(normed_rows, up_grad)
 
     middle_grads, branch_grads, attended_grads, gain_two = [], [], [], []
     query_grads, kv_out = [], []
@@ -734,34 +723,29 @@
         kv_out.append(plan.start(ring_scatter(kv_term)))
 
     plan.step(back_there)
-    plan.step(up_out)
     before_attention(0)
     through_attention(0)
     gate_out.end()
-    plan.step(up_out)
     plan.step(back_there)
     before_attention(1)
     plan.step(kv_out[0])
-    plan.step(up_out)
     out_out = plan.start(scatter_everywhere(
         plan.run(
             lambda a, b: contract_rows(a, b, BF16), jnp.concatenate(branch_grads, axis=0), attended
         )
     ))
     plan.step(kv_out[0])
+    through_attention(1)
     plan.step(out_out)
-    through_attention(1)
     plan.step(kv_out[0])
-    plan.step(up_out)
     query_grad = jnp.concatenate(query_grads, axis=0)
     query_out = plan.start(scatter_everywhere(
         plan.run(lambda a, b: contract_rows(a, b, BF16), normed, query_grad)
     ))
     plan.step(kv_out[0])
     plan.step(kv_out[1])
+    part = plan.run(contract_last, query_grad, query_full)
     plan.step(query_out)
-    plan.step(out_out)
-    part = plan.run(contract_last, query_grad, query_full)
     plan.step(kv_out[1])
 
     def finish_output(came, own, middle):
@@ -805,7 +789,7 @@
         out_out.end().T,
         narrow_grad[:, 2 * size + 1],
         gate_out.value.astype(F32),
-        up_out.end(),
+        up_out.end().astype(F32),
         down_out.value.T.astype(F32),
     )
 

time: 1670 us -> 1580 us (0.946)
  waiting for transfers between devices: 565 us -> 407 us
  local copies, waits for them, and re-layouts: 132 us -> 170 us
    ppermute x105 -> x124, waiting for transfers between devices: 495 us -> 370 us  [launch(): lax.ppermute(operand, axis, pairs)]
    dynamic_update_slice x32 -> x56, local copies, waits for them, and re-layouts: 20.1 us -> 55.7 us  [put(): return lax.dynamic_update_slice(found, piece[None], start)]
    all_gather x4 -> x3, waiting for transfers between devices: 59.5 us -> 37 us  [ctx_gather(): return lax.all_gather(block, 'ctx', axis=0, tiled=True)]
    convert_element_type x29 -> x26, other arithmetic: 56.8 us -> 50.6 us  [add(): return (first.astype(F32) + second.astype(F32)).astype(BF16)]
    ppermute x105 -> x124, starting transfers between devices: 196 us -> 198 us  [launch(): lax.ppermute(operand, axis, pairs)]
    unnamed x164 -> x163, local copies, waits for them, and re-layouts: 36.7 us -> 36.8 us
  transfers between devices with their start and end apart: 112 -> 130, of which waited for: 59 -> 53; matrix products, arithmetic and copies ran while one was open for 32% -> 38% of each run, Pallas kernels for 12% -> 14%
where the time goes in v3:
time: 1580 us; the launch traced here: 1570 us
  waiting for transfers between devices  407 us (26%)
  matrix products  403 us (26%)
  Pallas kernels  216 us (14%)
  starting transfers between devices  199 us (13%)
  local copies, waits for them, and re-layouts  170 us (11%)
  other arithmetic  152 us (10%)
  between operations  21.1 us (1%)
    ppermute x124, waiting for transfers between devices, launch(): lax.ppermute(operand, axis, pairs)  370 us
    dot_general x10, matrix products, dot(): return jnp.dot(left, right, preferred_element_type=out)  203 us
    ppermute x124, starting transfers between devices, launch(): lax.ppermute(operand, axis, pairs)  198 us
    dot_general x9, matrix products, contract_last(): lax.dot_general(left, right, (((1,), (1,)), ((), ())), preferred_element_...  170 us
    pallas_call x3, Pallas kernels, weight_grad(): pl.pallas_call(weight_kernel, out_shape=jax.ShapeDtypeStruct((width, cols...  118 us
    dynamic_update_slice x56, local copies, waits for them, and re-layouts, put(): return lax.dynamic_update_slice(found, piece[None], start)  55.7 us
    convert_element_type x26, other arithmetic, add(): return (first.astype(F32) + second.astype(F32)).astype(BF16)  50.6 us
    all_gather x3, waiting for transfers between devices, ctx_gather(): return lax.all_gather(block, 'ctx', axis=0, tiled=True)  37 us
  transfers between devices with their start and end apart: 130, of which 53 were waited for; matrix products, arithmetic and copies ran while one was open for 38% of the time, Pallas kernels for 14%

profile of v3, /device:TPU:0, one launch (start us, length us, event | category | flops | bytes accessed | tf_op | source)
XLA Modules:
  0.0 1568.8 jit_solution(5937976286325120210)
XLA Ops:
  52.2 22.3 %collective-permute-done.12 = bf16[48,640]{1,0:T(8,128)(2,1)S(1)} collective-permute-done((bf16[48,640]{1,0:T(8,128)(2,1)S(1)}, bf16[48,640]{1,0:T(8,128)(2,1)S(1)}, u32[]{:S(2)}, u32[]{:S(2)}) %collective-permute-start.12) | collective-permute-done | bytes 61472 | tf_op jit(solution)/shard_map/ppermute | solution.py:75
  176.9 25.7 %collective-permute-done.33 = bf16[48,2560]{1,0:T(8,128)(2,1)S(1)} collective-permute-done((bf16[48,2560]{1,0:T(8,128)(2,1)S(1)}, bf16[48,2560]{1,0:T(8,128)(2,1)S(1)}, u32[]{:S(2)}, u32[]{:S(2)}) %collective-permute-start.33) | collective-permute-done | bytes 245792 | tf_op jit(solution)/shard_map/ppermute | solution.py:75
  292.1 14.5 fusion.114
  407.5 15.5 multiply_reduce_fusion
  441.4 23.2 %fusion.115 = f32[1536,1920]{1,0:T(8,128)} fusion(bf16[1536,2560]{1,0:T(8,128)(2,1)} %pad_maximum_fusion.a_here, bf16[2560,1920]{1,0:T(8,128)(2,1)} %all-gather.4.cloned.1.call-done), kind=kOutput, calls=%fused_computation.356 | convolution fusion | flops 15099494400 | bytes 29491200 | tf_op jit(solution)/shard_map/dot_general | solution.py:25
  467.1 26.1 %multiply_convert_fusion.3 = (bf16[1536,1920]{1,0:T(8,128)(2,1)}, f32[1536,1920]{1,0:T(8,128)}) fusion(f32[1536,1920]{1,0:T(8,128)} %fusion.115, bf16[1536,2560]{1,0:T(8,128)(2,1)} %pad_maximum_fusion.a_here, bf16[2560,1920]{1,0:T(8,128)(2,1)} %all-gather.6.cloned.1.call-done), kind=kOutput, calls=%fused_computation.29 | convolution fusion | flops 15128985600 | bytes 47185920 | tf_op jit(solution)/shard_map/dot_general | solution.py:25
  493.2 22.1 %collective-permute-done.67 = bf16[768,2560]{1,0:T(8,128)(2,1)} collective-permute-done((bf16[768,2560]{1,0:T(8,128)(2,1)}, bf16[768,2560]{1,0:T(8,128)(2,1)}, u32[]{:S(2)}, u32[]{:S(2)}) %collective-permute-start.67) | collective-permute-done | bytes 3932192 | tf_op jit(solution)/shard_map/ppermute | solution.py:75
  524.8 23.0 %fusion.116 = f32[1536,1920]{1,0:T(8,128)} fusion(bf16[1536,2560]{1,0:T(8,128)(2,1)S(1)} %constant_dynamic-update-slice_fusion.2.a_there, bf16[2560,1920]{1,0:T(8,128)(2,1)} %all-gather.4.cloned.1.call-done), kind=kOutput, calls=%fused_computation.357 | convolution fusion | flops 15099494400 | bytes 29491200 | tf_op jit(solution)/shard_map/dot_general | solution.py:25
  547.7 27.7 %multiply_convert_fusion.2 = (bf16[1536,1920]{1,0:T(8,128)(2,1)}, f32[1536,1920]{1,0:T(8,128)}) fusion(f32[1536,1920]{1,0:T(8,128)} %fusion.116, bf16[1536,2560]{1,0:T(8,128)(2,1)S(1)} %constant_dynamic-update-slice_fusion.2.a_there, bf16[2560,1920]{1,0:T(8,128)(2,1)} %all-gather.6.cloned.1.call-done), kind=kOutput, calls=%fused_computation.28 | convolution fusion | flops 15128985600 | bytes 47185920 | tf_op jit(solution)/shard_map/dot_general | solution.py:25
  575.5 27.6 %collective-permute-done.69 = bf16[768,2560]{1,0:T(8,128)(2,1)} collective-permute-done((bf16[768,2560]{1,0:T(8,128)(2,1)}, bf16[768,2560]{1,0:T(8,128)(2,1)}, u32[]{:S(2)}, u32[]{:S(2)}) %collective-permute-start.69) | collective-permute-done | bytes 3932192 | tf_op jit(solution)/shard_map/ppermute | solution.py:75
  621.4 39.3 %shard_map.215 = bf16[2560,1920]{1,0:T(8,128)(2,1)} custom-call(bf16[1536,2560]{1,0:T(8,128)(2,1)} %pad_maximum_fusion.1.a_here, bf16[1536,2560]{1,0:T(8,128)(2,1)} %constant_dynamic-update-slice_fusion.4.a_there, bf16[1536,1920]{1,0:T(8,128)(2,1)S(1)} %copy-done.10, bf16[1536,1920]{1,0:T(8,128)(2,1)} %get-tuple-element.236.b_there), custom_call_target="tpu_custom_call" | custom-call | flops 30198988800 | bytes 37355520 | tf_op jit(solution)/shard_map/pallas_call | solution.py:494
  660.8 34.5 %all-gather.8.cloned.1.call-done = bf16[2560,1920]{1,0:T(8,128)(2,1)} async-done(((bf16[320,1920]{1,0:T(8,128)(2,1)}), bf16[2560,1920]{1,0:T(8,128)(2,1)}) %all-gather.8.cloned.1.call-update) | async-done | bytes 9830416 | tf_op jit(solution)/shard_map/all_gather | solution.py:101
  695.4 20.7 %fusion.117 = bf16[1536,2560]{1,0:T(8,128)(2,1)S(1)} fusion(bf16[1536,1920]{1,0:T(8,128)(2,1)} %get-tuple-element.236.b_there, bf16[2560,1920]{1,0:T(8,128)(2,1)} %all-gather.8.cloned.1.call-done), kind=kOutput, calls=%fused_computation.358 | convolution fusion | flops 15099494400 | bytes 23592960 | tf_op jit(solution)/shard_map/dot_general | solution.py:33
  724.5 20.8 %fusion.118 = bf16[1536,2560]{1,0:T(8,128)(2,1)S(1)} fusion(bf16[1536,1920]{1,0:T(8,128)(2,1)} %get-tuple-element.237.b_here, bf16[2560,1920]{1,0:T(8,128)(2,1)} %all-gather.8.cloned.1.call-done), kind=kOutput, calls=%fused_computation.359 | convolution fusion | flops 15099494400 | bytes 23592960 | tf_op jit(solution)/shard_map/dot_general | solution.py:33
  759.6 33.2 %multiply_convert_fusion.1 = (bf16[1536,1920]{1,0:T(8,128)(2,1)}, bf16[1536,1920]{1,0:T(8,128)(2,1)S(1)}) fusion(f32[1536,1920]{1,0:T(8,128)} %fusion.115, f32[1536,1920]{1,0:T(8,128)} %get-tuple-element.453, bf16[1536,2560]{1,0:T(8,128)(2,1)} %pad_maximum_fusion.1.a_here, bf16[2560,1920]{1,0:T(8,128)(2,1)} %all-gather.8.cloned.1.call-done), kind=kOutput, calls=%fused_computation.27 | convolution fusion | flops 15170273280 | bytes 53084160 | tf_op jit(solution)/shard_map/dot_general | solution.py:25
  792.8 36.0 %multiply_convert_fusion = (bf16[1536,1920]{1,0:T(8,128)(2,1)}, bf16[1536,1920]{1,0:T(8,128)(2,1)}) fusion(f32[1536,1920]{1,0:T(8,128)} %fusion.116, f32[1536,1920]{1,0:T(8,128)} %get-tuple-element.455, bf16[1536,2560]{1,0:T(8,128)(2,1)} %constant_dynamic-update-slice_fusion.4.a_there, bf16[2560,1920]{1,0:T(8,128)(2,1)} %all-gather.8.cloned.1.call-done), kind=kOutput, calls=%fused_computation.26 | convolution fusion | flops 15170273280 | bytes 53084160 | tf_op jit(solution)/shard_map/dot_general | solution.py:25
  828.8 39.2 %shard_map.216 = bf16[2560,1920]{1,0:T(8,128)(2,1)} custom-call(bf16[1536,2560]{1,0:T(8,128)(2,1)} %pad_maximum_fusion.a_here, bf16[1536,2560]{1,0:T(8,128)(2,1)} %copy-done.32, bf16[1536,1920]{1,0:T(8,128)(2,1)S(1)} %get-tuple-element.247.b_here, bf16[1536,1920]{1,0:T(8,128)(2,1)} %get-tuple-element.244.b_there), custom_call_target="tpu_custom_call" | custom-call | flops 30198988800 | bytes 37355520 | tf_op jit(solution)/shard_map/pallas_call | solution.py:494
  868.2 22.4 %fusion.119 = f32[1536,2560]{1,0:T(8,128)} fusion(bf16[1536,1920]{1,0:T(8,128)(2,1)} %get-tuple-element.244.b_there, bf16[2560,1920]{1,0:T(8,128)(2,1)} %all-gather.4.cloned.1.call-done), kind=kOutput, calls=%fused_computation.360 | convolution fusion | flops 15099494400 | bytes 31457280 | tf_op jit(solution)/shard_map/dot_general | solution.py:33
  890.6 24.3 %add_convert_fusion.1 = bf16[1536,2560]{1,0:T(8,128)(2,1)} fusion(f32[1536,2560]{1,0:T(8,128)} %fusion.119, bf16[1536,1920]{1,0:T(8,128)(2,1)} %get-tuple-element.245.b_there, bf16[2560,1920]{1,0:T(8,128)(2,1)} %all-gather.6.cloned.1.call-done), kind=kOutput, calls=%fused_computation.5 | convolution fusion | flops 15107358720 | bytes 39321600 | tf_op jit(solution)/shard_map/dot_general | solution.py:33
  919.5 22.6 %fusion.120 = f32[1536,2560]{1,0:T(8,128)} fusion(bf16[1536,1920]{1,0:T(8,128)(2,1)} %copy-done.11, bf16[2560,1920]{1,0:T(8,128)(2,1)} %all-gather.4.cloned.1.call-done), kind=kOutput, calls=%fused_computation.361 | convolution fusion | flops 15099494400 | bytes 31457280 | tf_op jit(solution)/shard_map/dot_general | solution.py:33
  942.1 24.5 %add_convert_fusion = bf16[1536,2560]{1,0:T(8,128)(2,1)} fusion(f32[1536,2560]{1,0:T(8,128)} %fusion.120, bf16[1536,1920]{1,0:T(8,128)(2,1)} %get-tuple-element.248.b_here, bf16[2560,1920]{1,0:T(8,128)(2,1)} %all-gather.6.cloned.1.call-done), kind=kOutput, calls=%fused_computation.4 | convolution fusion | flops 15107358720 | bytes 39321600 | tf_op jit(solution)/shard_map/dot_general | solution.py:33
  979.2 39.2 %shard_map.217 = bf16[2560,1920]{1,0:T(8,128)(2,1)} custom-call(bf16[1536,2560]{1,0:T(8,128)(2,1)} %pad_maximum_fusion.a_here, bf16[1536,2560]{1,0:T(8,128)(2,1)} %copy-done.32, bf16[1536,1920]{1,0:T(8,128)(2,1)S(1)} %bitcast.462, bf16[1536,1920]{1,0:T(8,128)(2,1)} %get-tuple-element.245.b_there), custom_call_target="tpu_custom_call" | custom-call | flops 30198988800 | bytes 37355520 | tf_op jit(solution)/shard_map/pallas_call | solution.py:494
  1051.8 16.6 %shard_map.218 = (bf16[384,2560]{1,0:T(8,128)(2,1)S(1)}, bf16[8,384,512]{2,1,0:T(8,128)(2,1)}) custom-call(s32[6]{0:T(128)S(1)} %copy-done.5, bf16[384,2560]{1,0:T(8,128)(2,1)S(1)} %copy-done.9, bf16[8,768,512]{2,1,0:T(8,128)(2,1)} %bitcast_dynamic-update-slice_fusion.30.kv_ref, s32[1,768]{1,0:T(1,128)S(1)} %bitcast.460, s32[1,768]{1,0:T(1,128)S(1)} %bitcast.455, ...), custom_call_target="tpu_custom_call" | custom-call | flops 20132659200 | bytes 9830400 | tf_op jit(solution)/shard_map/pallas_call | solution.py:719
  1085.2 14.3 collective-permute-done.79
  1146.4 14.5 collective-permute-start.80
  1176.0 16.8 %shard_map.219 = (bf16[384,2560]{1,0:T(8,128)(2,1)S(1)}, bf16[8,384,512]{2,1,0:T(8,128)(2,1)}) custom-call(s32[6]{0:T(128)S(1)} %stack.81.spans, bf16[384,2560]{1,0:T(8,128)(2,1)S(1)} %copy-done.7, bf16[8,768,512]{2,1,0:T(8,128)(2,1)} %bitcast_dynamic-update-slice_fusion.30.kv_ref, s32[1,768]{1,0:T(1,128)S(1)} %bitcast.458, s32[1,768]{1,0:T(1,128)S(1)} %bitcast.456, ...), custom_call_target="tpu_custom_call" | custom-call | flops 20132659200 | bytes 9830400 | tf_op jit(solution)/shard_map/pallas_call | solution.py:719
  1210.9 14.9 fusion.124
  1278.1 15.5 collective-permute-start.90
  1294.0 16.5 %fusion.125 = f32[768,2560]{1,0:T(8,128)} fusion(bf16[768,2560]{1,0:T(8,128)(2,1)} %copy-done.36, bf16[2560,2560]{1,0:T(8,128)(2,1)} %bitcast.482), kind=kOutput, calls=%fused_computation.366 | convolution fusion | flops 10066329600 | bytes 24903680 | tf_op jit(solution)/shard_map/dot_general | solution.py:33
  1326.5 14.4 collective-permute-done.96
  1437.1 15.4 collective-permute-done.103
  1452.5 14.1 collective-permute-done.104
  (638 shorter events, 810.2 us)
Async XLA Ops:
  7.2 284.9 %all-gather.4.cloned.1.call-start = ((), (), s32[]{:S(2)}) async-start(), calls=%async_computation.3 | async-start | bytes 11059200 | tf_op jit(solution)/shard_map/all_gather | solution.py:101
  15.6 69.1 %collective-permute-start.13 = (bf16[80,2560]{1,0:T(8,128)(2,1)}, bf16[80,2560]{1,0:T(8,128)(2,1)S(1)}, u32[]{:S(2)}, u32[]{:S(2)}) collective-permute-start(bf16[80,2560]{1,0:T(8,128)(2,1)} %block_ref.1), channel_id=1, source_target_pairs={{0,8},{8,16},{16,24},{24,28},{28,20},{20,12},{12,4},{4,0},{1,9},{9... | collective-permute-start | bytes 1228808 | tf_op jit(solution)/shard_map/ppermute | solution.py:75
  17.2 449.8 %all-gather.6.cloned.1.call-start = ((), (), s32[]{:S(2)}) async-start(), calls=%async_computation.4 | async-start | bytes 11059200 | tf_op jit(solution)/shard_map/all_gather | solution.py:101
  38.0 46.7 %collective-permute-start.14 = (bf16[80,2560]{1,0:T(8,128)(2,1)S(1)}, bf16[80,2560]{1,0:T(8,128)(2,1)S(1)}, u32[]{:S(2)}, u32[]{:S(2)}) collective-permute-start(bf16[80,2560]{1,0:T(8,128)(2,1)S(1)} %copy-done.48), channel_id=1, source_target_pairs={{0,4},{8,0},{16,8},{24,16},{28,24},{20,28},{12,20},{4,12},{1,5},{9... | collective-permute-start | bytes 1228808 | tf_op jit(solution)/shard_map/ppermute | solution.py:75
  44.8 40.0 %collective-permute-start.15 = (bf16[80,2560]{1,0:T(8,128)(2,1)S(1)}, bf16[80,2560]{1,0:T(8,128)(2,1)S(1)}, u32[]{:S(2)}, u32[]{:S(2)}) collective-permute-start(bf16[80,2560]{1,0:T(8,128)(2,1)S(1)} %copy-done.48), channel_id=1, source_target_pairs={{0,2},{1,3},{2,0},{3,1},{4,6},{5,7},{6,4},{7,5},{8,10},{9,11},{10,... | collective-permute-start | bytes 1228808 | tf_op jit(solution)/shard_map/ppermute | solution.py:75
  51.0 37.1 %collective-permute-start.16 = (bf16[80,640]{1,0:T(8,128)(2,1)S(1)}, bf16[80,640]{1,0:T(8,128)(2,1)S(1)}, u32[]{:S(2)}, u32[]{:S(2)}) collective-permute-start(bf16[80,640]{1,0:T(8,128)(2,1)S(1)} %collective-permute-done.7), channel_id=1, source_target_pairs={{0,2},{1,3},{2,0},{3,1},{4,6},{5,7},{6,4},{7,5},{8,10},{9,11},{10,... | collective-permute-start | bytes 307208 | tf_op jit(solution)/shard_map/ppermute | solution.py:75
  105.6 41.5 %collective-permute-start.24 = (bf16[8,80,640]{2,1,0:T(8,128)(2,1)S(1)}, bf16[8,80,640]{2,1,0:T(8,128)(2,1)S(1)}, u32[]{:S(2)}, u32[]{:S(2)}) collective-permute-start(bf16[8,80,640]{2,1,0:T(8,128)(2,1)S(1)} %copy-done.27), channel_id=1, source_target_pairs={{0,1},{1,0},{2,3},{3,2},{4,5},{5,4},{6,7},{7,6},{8,9},{9,8},{10,11... | collective-permute-start | bytes 2457608 | tf_op jit(solution)/shard_map/ppermute | solution.py:75
  106.2 40.9 %collective-permute-start.25 = (bf16[8,80,640]{2,1,0:T(8,128)(2,1)}, bf16[8,80,640]{2,1,0:T(8,128)(2,1)}, u32[]{:S(2)}, u32[]{:S(2)}) collective-permute-start(bf16[8,80,640]{2,1,0:T(8,128)(2,1)} %bitcast_dynamic-update-slice_fusion.52.refs_2_), channel_id=1, source_target_pairs={{0,1},{1,0},{2,3},{3,2},{4,5},{5,4},{6,7},{7,6},{8,9},{9,8},{10,11... | collective-permute-start | bytes 2457608 | tf_op jit(solution)/shard_map/ppermute | solution.py:75
  132.9 32.2 %collective-permute-start.29 = (bf16[80,2560]{1,0:T(8,128)(2,1)}, bf16[80,2560]{1,0:T(8,128)(2,1)}, u32[]{:S(2)}, u32[]{:S(2)}) collective-permute-start(bf16[80,2560]{1,0:T(8,128)(2,1)} %collective-permute-done.21), channel_id=1, source_target_pairs={{0,2},{1,3},{2,0},{3,1},{4,6},{5,7},{6,4},{7,5},{8,10},{9,11},{10,... | collective-permute-start | bytes 1228808 | tf_op jit(solution)/shard_map/ppermute | solution.py:75
  167.2 37.7 %collective-permute-start.30 = (bf16[768,512]{1,0:T(8,128)(2,1)S(1)}, bf16[768,512]{1,0:T(8,128)(2,1)}, u32[]{:S(2)}, u32[]{:S(2)}) collective-permute-start(bf16[768,512]{1,0:T(8,128)(2,1)S(1)} %pad_maximum_fusion.5.block_ref), channel_id=1, source_target_pairs={{0,8},{8,16},{16,24},{24,28},{28,20},{20,12},{12,4},{4,0},{1,9},{9... | collective-permute-start | bytes 2359304 | tf_op jit(solution)/shard_map/ppermute | solution.py:75
  167.3 37.6 %collective-permute-start.31 = (bf16[768,512]{1,0:T(8,128)(2,1)S(1)}, bf16[768,512]{1,0:T(8,128)(2,1)}, u32[]{:S(2)}, u32[]{:S(2)}) collective-permute-start(bf16[768,512]{1,0:T(8,128)(2,1)S(1)} %pad_maximum_fusion.5.block_ref), channel_id=1, source_target_pairs={{0,4},{8,0},{16,8},{24,16},{28,24},{20,28},{12,20},{4,12},{1,5},{9... | collective-permute-start | bytes 2359304 | tf_op jit(solution)/shard_map/ppermute | solution.py:75
  322.0 373.3 %all-gather.8.cloned.1.call-start = ((), (), s32[]{:S(2)}) async-start(), calls=%async_computation.5 | async-start | bytes 11059200 | tf_op jit(solution)/shard_map/all_gather | solution.py:101
  427.9 87.3 %collective-permute-start.67 = (bf16[768,2560]{1,0:T(8,128)(2,1)}, bf16[768,2560]{1,0:T(8,128)(2,1)}, u32[]{:S(2)}, u32[]{:S(2)}) collective-permute-start(bf16[768,2560]{1,0:T(8,128)(2,1)} %multiply_convert_fusion.4), channel_id=1, source_target_pairs={{0,2},{1,3},{2,0},{3,1},{4,6},{5,7},{6,4},{7,5},{8,10},{9,11},{10,... | collective-permute-start | bytes 11796488 | tf_op jit(solution)/shard_map/ppermute | solution.py:75
  515.3 404.2 %reduce-scatter.4.cloned.1.call-start = ((), (), s32[]{:S(2)}) async-start(), calls=%async_computation.6 | async-start | bytes 11059200 | tf_op jit(solution)/shard_map/reduce_scatter | solution.py:105
  515.3 87.7 %collective-permute-start.69 = (bf16[768,2560]{1,0:T(8,128)(2,1)}, bf16[768,2560]{1,0:T(8,128)(2,1)}, u32[]{:S(2)}, u32[]{:S(2)}) collective-permute-start(bf16[768,2560]{1,0:T(8,128)(2,1)} %bitcast.49), channel_id=1, source_target_pairs={{0,2},{1,3},{2,0},{3,1},{4,6},{5,7},{6,4},{7,5},{8,10},{9,11},{10,... | collective-permute-start | bytes 11796488 | tf_op jit(solution)/shard_map/ppermute | solution.py:75
  660.8 440.0 %reduce-scatter.6.cloned.1.call-start = ((), (), s32[]{:S(2)}) async-start(), calls=%async_computation.7 | async-start | bytes 11059200 | tf_op jit(solution)/shard_map/reduce_scatter | solution.py:105
  747.5 81.3 %collective-permute-start.71 = (bf16[768,2560]{1,0:T(8,128)(2,1)}, bf16[768,2560]{1,0:T(8,128)(2,1)}, u32[]{:S(2)}, u32[]{:S(2)}) collective-permute-start(bf16[768,2560]{1,0:T(8,128)(2,1)} %slice.415), channel_id=1, source_target_pairs={{0,1},{1,0},{2,3},{3,2},{4,5},{5,4},{6,7},{7,6},{8,9},{9,8},{10,11... | collective-permute-start | bytes 11796488 | tf_op jit(solution)/shard_map/ppermute | solution.py:75
  758.2 110.0 %collective-permute-start.73 = (bf16[768,2560]{1,0:T(8,128)(2,1)}, bf16[768,2560]{1,0:T(8,128)(2,1)}, u32[]{:S(2)}, u32[]{:S(2)}) collective-permute-start(bf16[768,2560]{1,0:T(8,128)(2,1)} %add_convert_fusion.3), channel_id=1, source_target_pairs={{0,2},{1,3},{2,0},{3,1},{4,6},{5,7},{6,4},{7,5},{8,10},{9,11},{10,... | collective-permute-start | bytes 11796488 | tf_op jit(solution)/shard_map/ppermute | solution.py:75
  868.1 637.6 %reduce-scatter.8.cloned.1.call-start = ((), (), s32[]{:S(2)}) async-start(), calls=%async_computation.8 | async-start | bytes 11059200 | tf_op jit(solution)/shard_map/reduce_scatter | solution.py:105
  919.5 52.4 %collective-permute-start.75 = (bf16[768,2560]{1,0:T(8,128)(2,1)}, bf16[768,2560]{1,0:T(8,128)(2,1)}, u32[]{:S(2)}, u32[]{:S(2)}) collective-permute-start(bf16[768,2560]{1,0:T(8,128)(2,1)} %slice.417), channel_id=1, source_target_pairs={{0,1},{1,0},{2,3},{3,2},{4,5},{5,4},{6,7},{7,6},{8,9},{9,8},{10,11... | collective-permute-start | bytes 11796488 | tf_op jit(solution)/shard_map/ppermute | solution.py:75
  971.0 52.5 %collective-permute-start.74 = (bf16[768,2560]{1,0:T(8,128)(2,1)}, bf16[768,2560]{1,0:T(8,128)(2,1)}, u32[]{:S(2)}, u32[]{:S(2)}) collective-permute-start(bf16[768,2560]{1,0:T(8,128)(2,1)} %slice.419), channel_id=1, source_target_pairs={{0,1},{1,0},{2,3},{3,2},{4,5},{5,4},{6,7},{7,6},{8,9},{9,8},{10,11... | collective-permute-start | bytes 11796488 | tf_op jit(solution)/shard_map/ppermute | solution.py:75
  978.6 45.0 %collective-permute-start.76 = (bf16[384,2560]{1,0:T(8,128)(2,1)}, bf16[384,2560]{1,0:T(8,128)(2,1)S(1)}, u32[]{:S(2)}, u32[]{:S(2)}) collective-permute-start(bf16[384,2560]{1,0:T(8,128)(2,1)} %get-tuple-element.251), channel_id=1, source_target_pairs={{0,2},{1,3},{2,0},{3,1},{4,6},{5,7},{6,4},{7,5},{8,10},{9,11},{10,... | collective-permute-start | bytes 5898248 | tf_op jit(solution)/shard_map/ppermute | solution.py:75
  1051.3 49.4 %collective-permute-start.77 = (bf16[384,2560]{1,0:T(8,128)(2,1)S(1)}, bf16[384,2560]{1,0:T(8,128)(2,1)}, u32[]{:S(2)}, u32[]{:S(2)}) collective-permute-start(bf16[384,2560]{1,0:T(8,128)(2,1)S(1)} %copy-done.33), channel_id=1, source_target_pairs={{0,2},{1,3},{2,0},{3,1},{4,6},{5,7},{6,4},{7,5},{8,10},{9,11},{10,... | collective-permute-start | bytes 5898248 | tf_op jit(solution)/shard_map/ppermute | solution.py:75
  1146.4 51.0 %collective-permute-start.82 = (bf16[8,2,80,2560]{3,2,0,1:T(8,128)(2,1)}, bf16[8,2,80,2560]{3,2,0,1:T(8,128)(2,1)}, u32[]{:S(2)}, u32[]{:S(2)}) collective-permute-start(bf16[8,2,80,2560]{3,2,0,1:T(8,128)(2,1)} %bitcast.451), channel_id=1, source_target_pairs={{0,1},{1,0},{2,3},{3,2},{4,5},{5,4},{6,7},{7,6},{8,9},{9,8},{10,11... | collective-permute-start | bytes 19660808 | tf_op jit(solution)/shard_map/ppermute | solution.py:75
  1236.8 106.7 %collective-permute-start.89 = (bf16[8,2,80,2560]{3,2,0,1:T(8,128)(2,1)}, bf16[8,2,80,2560]{3,2,0,1:T(8,128)(2,1)}, u32[]{:S(2)}, u32[]{:S(2)}) collective-permute-start(bf16[8,2,80,2560]{3,2,0,1:T(8,128)(2,1)} %bitcast.450), channel_id=1, source_target_pairs={{0,1},{1,0},{2,3},{3,2},{4,5},{5,4},{6,7},{7,6},{8,9},{9,8},{10,11... | collective-permute-start | bytes 19660808 | tf_op jit(solution)/shard_map/ppermute | solution.py:75
  1263.9 77.0 %collective-permute-start.96 = (bf16[8,80,2560]{2,1,0:T(8,128)(2,1)}, bf16[8,80,2560]{2,1,0:T(8,128)(2,1)S(1)}, u32[]{:S(2)}, u32[]{:S(2)}) collective-permute-start(bf16[8,80,2560]{2,1,0:T(8,128)(2,1)} %dynamic-slice_bitcast_fusion.1), channel_id=1, source_target_pairs={{0,2},{1,3},{2,0},{3,1},{4,6},{5,7},{6,4},{7,5},{8,10},{9,11},{10,... | collective-permute-start | bytes 9830408 | tf_op jit(solution)/shard_map/ppermute | solution.py:75
  1278.1 33.5 %collective-permute-start.90 = (bf16[384,512]{1,0:T(8,128)(2,1)S(1)}, bf16[384,512]{1,0:T(8,128)(2,1)S(1)}, u32[]{:S(2)}, u32[]{:S(2)}) collective-permute-start(bf16[384,512]{1,0:T(8,128)(2,1)S(1)} %pad_maximum_fusion.15), channel_id=1, source_target_pairs={{0,8},{8,16},{16,24},{24,28},{28,20},{20,12},{12,4},{4,0},{1,9},{9... | collective-permute-start | bytes 1179656 | tf_op jit(solution)/shard_map/ppermute | solution.py:75
  1388.5 88.7 %collective-permute-start.101 = (bf16[8,80,2560]{2,1,0:T(8,128)(2,1)}, bf16[8,80,2560]{2,1,0:T(8,128)(2,1)}, u32[]{:S(2)}, u32[]{:S(2)}) collective-permute-start(bf16[8,80,2560]{2,1,0:T(8,128)(2,1)} %dynamic-slice_bitcast_fusion), channel_id=1, source_target_pairs={{0,2},{1,3},{2,0},{3,1},{4,6},{5,7},{6,4},{7,5},{8,10},{9,11},{10,... | collective-permute-start | bytes 9830408 | tf_op jit(solution)/shard_map/ppermute | solution.py:75
  1389.1 40.9 %collective-permute-start.99 = (bf16[32,2560]{1,0:T(8,128)(2,1)}, bf16[32,2560]{1,0:T(8,128)(2,1)}, u32[]{:S(2)}, u32[]{:S(2)}) collective-permute-start(bf16[32,2560]{1,0:T(8,128)(2,1)} %get-tuple-element.291), channel_id=1, source_target_pairs={{0,8},{8,16},{16,24},{24,28},{28,20},{20,12},{12,4},{4,0},{1,9},{9... | collective-permute-start | bytes 491528 | tf_op jit(solution)/shard_map/ppermute | solution.py:75
  1391.3 39.8 %collective-permute-start.100 = (bf16[48,2560]{1,0:T(8,128)(2,1)}, bf16[48,2560]{1,0:T(8,128)(2,1)}, u32[]{:S(2)}, u32[]{:S(2)}) collective-permute-start(bf16[48,2560]{1,0:T(8,128)(2,1)} %get-tuple-element.292), channel_id=1, source_target_pairs={{0,4},{8,0},{16,8},{24,16},{28,24},{20,28},{12,20},{4,12},{1,5},{9... | collective-permute-start | bytes 737288 | tf_op jit(solution)/shard_map/ppermute | solution.py:75
  1434.1 32.5 %collective-permute-start.104 = (bf16[80,2560]{1,0:T(8,128)(2,1)S(1)}, bf16[80,2560]{1,0:T(8,128)(2,1)S(1)}, u32[]{:S(2)}, u32[]{:S(2)}) collective-permute-start(bf16[80,2560]{1,0:T(8,128)(2,1)S(1)} %pad_maximum_fusion.8), channel_id=1, source_target_pairs={{0,4},{8,0},{16,8},{24,16},{28,24},{20,28},{12,20},{4,12},{1,5},{9... | collective-permute-start | bytes 1228808 | tf_op jit(solution)/shard_map/ppermute | solution.py:75
  1436.1 40.9 %collective-permute-start.98 = (bf16[8,80,640]{2,1,0:T(8,128)(2,1)S(1)}, bf16[8,80,640]{2,1,0:T(8,128)(2,1)S(1)}, u32[]{:S(2)}, u32[]{:S(2)}) collective-permute-start(bf16[8,80,640]{2,1,0:T(8,128)(2,1)S(1)} %dynamic-slice_bitcast_fusion.3), channel_id=1, source_target_pairs={{0,2},{1,3},{2,0},{3,1},{4,6},{5,7},{6,4},{7,5},{8,10},{9,11},{10,... | collective-permute-start | bytes 2457608 | tf_op jit(solution)/shard_map/ppermute | solution.py:75
  (173 other events, 3075.2 us)
Sparse Core Ops, SparseCore 0:
  17.4 181.8 all-gather.3
  322.1 144.9 all-gather.5
  515.4 179.9 all-gather.7
  698.8 167.8 reduce-scatter.3
  870.2 168.9 reduce-scatter.5
  1236.9 243.2 reduce-scatter.7

commit v4 on v3

--- a/solution.py
+++ b/solution.py
@@ -723,9 +723,9 @@
         kv_out.append(plan.start(ring_scatter(kv_term)))
 
     plan.step(back_there)
+    gate_out.end()
     before_attention(0)
     through_attention(0)
-    gate_out.end()
     plan.step(back_there)
     before_attention(1)
     plan.step(kv_out[0])
@@ -736,6 +736,7 @@
     ))
     plan.step(kv_out[0])
     through_attention(1)
+    up_out.end()
     plan.step(out_out)
     plan.step(kv_out[0])
     query_grad = jnp.concatenate(query_grads, axis=0)

time: 1580 us -> 1560 us (0.987)
  starting transfers between devices: 199 us -> 166 us
  waiting for transfers between devices: 407 us -> 435 us
    ppermute x124, starting transfers between devices: 198 us -> 166 us  [launch(): lax.ppermute(operand, axis, pairs)]
    reduce_scatter x3, waiting for transfers between devices: 0.02 us -> 23.1 us  [ctx_scatter(): return lax.psum_scatter(terms, 'ctx', scatter_dimension=0, tiled=True)]
    unnamed x163 -> x175, local copies, waits for them, and re-layouts: 36.8 us -> 35.6 us
  transfers between devices with their start and end apart: 130 -> 130, of which waited for: 53 -> 57; matrix products, arithmetic and copies ran while one was open for 38% -> 40% of each run, Pallas kernels for 14% -> 14%
where the time goes in v4:
time: 1560 us; the launch traced here: 1550 us
  waiting for transfers between devices  435 us (28%)
  matrix products  401 us (26%)
  Pallas kernels  217 us (14%)
  local copies, waits for them, and re-layouts  169 us (11%)
  starting transfers between devices  166 us (11%)
  other arithmetic  142 us (9%)
  between operations  21.2 us (1%)
    ppermute x124, waiting for transfers between devices, launch(): lax.ppermute(operand, axis, pairs)  379 us
    dot_general x10, matrix products, dot(): return jnp.dot(left, right, preferred_element_type=out)  199 us
    dot_general x9, matrix products, contract_last(): lax.dot_general(left, right, (((1,), (1,)), ((), ())), preferred_element_...  170 us
    ppermute x124, starting transfers between devices, launch(): lax.ppermute(operand, axis, pairs)  166 us
    pallas_call x3, Pallas kernels, weight_grad(): pl.pallas_call(weight_kernel, out_shape=jax.ShapeDtypeStruct((width, cols...  118 us
    dynamic_update_slice x56, local copies, waits for them, and re-layouts, put(): return lax.dynamic_update_slice(found, piece[None], start)  55.7 us
    convert_element_type x26, other arithmetic, add(): return (first.astype(F32) + second.astype(F32)).astype(BF16)  47.5 us
    unnamed x175, local copies, waits for them, and re-layouts  35.6 us
  transfers between devices with their start and end apart: 130, of which 57 were waited for; matrix products, arithmetic and copies ran while one was open for 40% of the time, Pallas kernels for 14%

profile of v4, /device:TPU:0, one launch (start us, length us, event | category | flops | bytes accessed | tf_op | source)
XLA Modules:
  0.0 1550.4 jit_solution(17858907382326612454)
XLA Ops:
  52.2 22.3 %collective-permute-done.12 = bf16[48,640]{1,0:T(8,128)(2,1)S(1)} collective-permute-done((bf16[48,640]{1,0:T(8,128)(2,1)S(1)}, bf16[48,640]{1,0:T(8,128)(2,1)S(1)}, u32[]{:S(2)}, u32[]{:S(2)}) %collective-permute-start.12) | collective-permute-done | bytes 61472 | tf_op jit(solution)/shard_map/ppermute | solution.py:75
  176.8 25.8 %collective-permute-done.33 = bf16[48,2560]{1,0:T(8,128)(2,1)S(1)} collective-permute-done((bf16[48,2560]{1,0:T(8,128)(2,1)S(1)}, bf16[48,2560]{1,0:T(8,128)(2,1)S(1)}, u32[]{:S(2)}, u32[]{:S(2)}) %collective-permute-start.33) | collective-permute-done | bytes 245792 | tf_op jit(solution)/shard_map/ppermute | solution.py:75
  292.0 14.5 fusion.114
  407.7 15.5 multiply_reduce_fusion
  441.6 23.1 %fusion.115 = f32[1536,1920]{1,0:T(8,128)} fusion(bf16[1536,2560]{1,0:T(8,128)(2,1)} %pad_maximum_fusion.a_here, bf16[2560,1920]{1,0:T(8,128)(2,1)} %all-gather.4.cloned.1.call-done), kind=kOutput, calls=%fused_computation.356 | convolution fusion | flops 15099494400 | bytes 29491200 | tf_op jit(solution)/shard_map/dot_general | solution.py:25
  467.1 26.1 %multiply_convert_fusion.3 = (bf16[1536,1920]{1,0:T(8,128)(2,1)}, f32[1536,1920]{1,0:T(8,128)}) fusion(f32[1536,1920]{1,0:T(8,128)} %fusion.115, bf16[1536,2560]{1,0:T(8,128)(2,1)} %pad_maximum_fusion.a_here, bf16[2560,1920]{1,0:T(8,128)(2,1)} %all-gather.6.cloned.1.call-done), kind=kOutput, calls=%fused_computation.29 | convolution fusion | flops 15128985600 | bytes 47185920 | tf_op jit(solution)/shard_map/dot_general | solution.py:25
  493.2 22.3 %collective-permute-done.67 = bf16[768,2560]{1,0:T(8,128)(2,1)} collective-permute-done((bf16[768,2560]{1,0:T(8,128)(2,1)}, bf16[768,2560]{1,0:T(8,128)(2,1)}, u32[]{:S(2)}, u32[]{:S(2)}) %collective-permute-start.67) | collective-permute-done | bytes 3932192 | tf_op jit(solution)/shard_map/ppermute | solution.py:75
  525.0 23.0 %fusion.116 = f32[1536,1920]{1,0:T(8,128)} fusion(bf16[1536,2560]{1,0:T(8,128)(2,1)S(1)} %constant_dynamic-update-slice_fusion.2.a_there, bf16[2560,1920]{1,0:T(8,128)(2,1)} %all-gather.4.cloned.1.call-done), kind=kOutput, calls=%fused_computation.357 | convolution fusion | flops 15099494400 | bytes 29491200 | tf_op jit(solution)/shard_map/dot_general | solution.py:25
  548.0 27.7 %multiply_convert_fusion.2 = (bf16[1536,1920]{1,0:T(8,128)(2,1)}, f32[1536,1920]{1,0:T(8,128)}) fusion(f32[1536,1920]{1,0:T(8,128)} %fusion.116, bf16[1536,2560]{1,0:T(8,128)(2,1)S(1)} %constant_dynamic-update-slice_fusion.2.a_there, bf16[2560,1920]{1,0:T(8,128)(2,1)} %all-gather.6.cloned.1.call-done), kind=kOutput, calls=%fused_computation.28 | convolution fusion | flops 15128985600 | bytes 47185920 | tf_op jit(solution)/shard_map/dot_general | solution.py:25
  575.7 27.6 %collective-permute-done.69 = bf16[768,2560]{1,0:T(8,128)(2,1)} collective-permute-done((bf16[768,2560]{1,0:T(8,128)(2,1)}, bf16[768,2560]{1,0:T(8,128)(2,1)}, u32[]{:S(2)}, u32[]{:S(2)}) %collective-permute-start.69) | collective-permute-done | bytes 3932192 | tf_op jit(solution)/shard_map/ppermute | solution.py:75
  622.1 39.4 %shard_map.215 = bf16[2560,1920]{1,0:T(8,128)(2,1)} custom-call(bf16[1536,2560]{1,0:T(8,128)(2,1)} %pad_maximum_fusion.1.a_here, bf16[1536,2560]{1,0:T(8,128)(2,1)} %constant_dynamic-update-slice_fusion.4.a_there, bf16[1536,1920]{1,0:T(8,128)(2,1)S(1)} %copy-done.11, bf16[1536,1920]{1,0:T(8,128)(2,1)} %get-tuple-element.236.b_there), custom_call_target="tpu_custom_call" | custom-call | flops 30198988800 | bytes 37355520 | tf_op jit(solution)/shard_map/pallas_call | solution.py:494
  661.6 30.3 %all-gather.8.cloned.1.call-done = bf16[2560,1920]{1,0:T(8,128)(2,1)} async-done(((bf16[320,1920]{1,0:T(8,128)(2,1)}), bf16[2560,1920]{1,0:T(8,128)(2,1)}) %all-gather.8.cloned.1.call-update) | async-done | bytes 9830416 | tf_op jit(solution)/shard_map/all_gather | solution.py:101
  691.9 20.7 %fusion.117 = bf16[1536,2560]{1,0:T(8,128)(2,1)S(1)} fusion(bf16[1536,1920]{1,0:T(8,128)(2,1)} %get-tuple-element.236.b_there, bf16[2560,1920]{1,0:T(8,128)(2,1)} %all-gather.8.cloned.1.call-done), kind=kOutput, calls=%fused_computation.358 | convolution fusion | flops 15099494400 | bytes 23592960 | tf_op jit(solution)/shard_map/dot_general | solution.py:33
  717.0 20.7 %fusion.118 = bf16[1536,2560]{1,0:T(8,128)(2,1)S(1)} fusion(bf16[1536,1920]{1,0:T(8,128)(2,1)} %get-tuple-element.237.b_here, bf16[2560,1920]{1,0:T(8,128)(2,1)} %all-gather.8.cloned.1.call-done), kind=kOutput, calls=%fused_computation.359 | convolution fusion | flops 15099494400 | bytes 23592960 | tf_op jit(solution)/shard_map/dot_general | solution.py:33
  749.6 33.2 %multiply_convert_fusion.1 = (bf16[1536,1920]{1,0:T(8,128)(2,1)}, bf16[1536,1920]{1,0:T(8,128)(2,1)S(1)}) fusion(f32[1536,1920]{1,0:T(8,128)} %fusion.115, f32[1536,1920]{1,0:T(8,128)} %get-tuple-element.453, bf16[1536,2560]{1,0:T(8,128)(2,1)} %pad_maximum_fusion.1.a_here, bf16[2560,1920]{1,0:T(8,128)(2,1)} %all-gather.8.cloned.1.call-done), kind=kOutput, calls=%fused_computation.27 | convolution fusion | flops 15170273280 | bytes 53084160 | tf_op jit(solution)/shard_map/dot_general | solution.py:25
  782.8 35.5 %multiply_convert_fusion = (bf16[1536,1920]{1,0:T(8,128)(2,1)}, bf16[1536,1920]{1,0:T(8,128)(2,1)}) fusion(f32[1536,1920]{1,0:T(8,128)} %fusion.116, f32[1536,1920]{1,0:T(8,128)} %get-tuple-element.455, bf16[1536,2560]{1,0:T(8,128)(2,1)} %constant_dynamic-update-slice_fusion.4.a_there, bf16[2560,1920]{1,0:T(8,128)(2,1)} %all-gather.8.cloned.1.call-done), kind=kOutput, calls=%fused_computation.26 | convolution fusion | flops 15170273280 | bytes 53084160 | tf_op jit(solution)/shard_map/dot_general | solution.py:25
  818.3 39.7 %shard_map.216 = bf16[2560,1920]{1,0:T(8,128)(2,1)} custom-call(bf16[1536,2560]{1,0:T(8,128)(2,1)} %pad_maximum_fusion.a_here, bf16[1536,2560]{1,0:T(8,128)(2,1)} %copy-done.30, bf16[1536,1920]{1,0:T(8,128)(2,1)S(1)} %get-tuple-element.247.b_here, bf16[1536,1920]{1,0:T(8,128)(2,1)} %get-tuple-element.244.b_there), custom_call_target="tpu_custom_call" | custom-call | flops 30198988800 | bytes 37355520 | tf_op jit(solution)/shard_map/pallas_call | solution.py:494
  861.1 22.5 %fusion.119 = f32[1536,2560]{1,0:T(8,128)} fusion(bf16[1536,1920]{1,0:T(8,128)(2,1)} %get-tuple-element.244.b_there, bf16[2560,1920]{1,0:T(8,128)(2,1)} %all-gather.4.cloned.1.call-done), kind=kOutput, calls=%fused_computation.360 | convolution fusion | flops 15099494400 | bytes 31457280 | tf_op jit(solution)/shard_map/dot_general | solution.py:33
  883.7 24.4 %add_convert_fusion.1 = bf16[1536,2560]{1,0:T(8,128)(2,1)} fusion(f32[1536,2560]{1,0:T(8,128)} %fusion.119, bf16[1536,1920]{1,0:T(8,128)(2,1)} %get-tuple-element.245.b_there, bf16[2560,1920]{1,0:T(8,128)(2,1)} %all-gather.6.cloned.1.call-done), kind=kOutput, calls=%fused_computation.5 | convolution fusion | flops 15107358720 | bytes 39321600 | tf_op jit(solution)/shard_map/dot_general | solution.py:33
  912.7 22.8 %fusion.120 = f32[1536,2560]{1,0:T(8,128)} fusion(bf16[1536,1920]{1,0:T(8,128)(2,1)} %copy-done.10, bf16[2560,1920]{1,0:T(8,128)(2,1)} %all-gather.4.cloned.1.call-done), kind=kOutput, calls=%fused_computation.361 | convolution fusion | flops 15099494400 | bytes 31457280 | tf_op jit(solution)/shard_map/dot_general | solution.py:33
  935.4 24.6 %add_convert_fusion = bf16[1536,2560]{1,0:T(8,128)(2,1)} fusion(f32[1536,2560]{1,0:T(8,128)} %fusion.120, bf16[1536,1920]{1,0:T(8,128)(2,1)} %get-tuple-element.248.b_here, bf16[2560,1920]{1,0:T(8,128)(2,1)} %all-gather.6.cloned.1.call-done), kind=kOutput, calls=%fused_computation.4 | convolution fusion | flops 15107358720 | bytes 39321600 | tf_op jit(solution)/shard_map/dot_general | solution.py:33
  972.7 39.2 %shard_map.217 = bf16[2560,1920]{1,0:T(8,128)(2,1)} custom-call(bf16[1536,2560]{1,0:T(8,128)(2,1)} %pad_maximum_fusion.a_here, bf16[1536,2560]{1,0:T(8,128)(2,1)} %copy-done.30, bf16[1536,1920]{1,0:T(8,128)(2,1)S(1)} %bitcast.462, bf16[1536,1920]{1,0:T(8,128)(2,1)} %get-tuple-element.245.b_there), custom_call_target="tpu_custom_call" | custom-call | flops 30198988800 | bytes 37355520 | tf_op jit(solution)/shard_map/pallas_call | solution.py:494
  1056.0 16.9 %shard_map.218 = (bf16[384,2560]{1,0:T(8,128)(2,1)S(1)}, bf16[8,384,512]{2,1,0:T(8,128)(2,1)}) custom-call(s32[6]{0:T(128)S(1)} %copy-done.5, bf16[384,2560]{1,0:T(8,128)(2,1)S(1)} %copy-done.9, bf16[8,768,512]{2,1,0:T(8,128)(2,1)} %bitcast_dynamic-update-slice_fusion.30.kv_ref, s32[1,768]{1,0:T(1,128)S(1)} %bitcast.460, s32[1,768]{1,0:T(1,128)S(1)} %bitcast.455, ...), custom_call_target="tpu_custom_call" | custom-call | flops 20132659200 | bytes 9830400 | tf_op jit(solution)/shard_map/pallas_call | solution.py:719
  1149.4 14.1 collective-permute-done.80
  1167.0 16.8 %shard_map.219 = (bf16[384,2560]{1,0:T(8,128)(2,1)S(1)}, bf16[8,384,512]{2,1,0:T(8,128)(2,1)}) custom-call(s32[6]{0:T(128)S(1)} %stack.81.spans, bf16[384,2560]{1,0:T(8,128)(2,1)S(1)} %copy-done.7, bf16[8,768,512]{2,1,0:T(8,128)(2,1)} %bitcast_dynamic-update-slice_fusion.30.kv_ref, s32[1,768]{1,0:T(1,128)S(1)} %bitcast.458, s32[1,768]{1,0:T(1,128)S(1)} %bitcast.456, ...), custom_call_target="tpu_custom_call" | custom-call | flops 20132659200 | bytes 9830400 | tf_op jit(solution)/shard_map/pallas_call | solution.py:719
  1206.5 13.8 reduce-scatter.8.cloned.1.call-done
  1220.3 16.4 %fusion.124 = bf16[2560,2560]{1,0:T(8,128)(2,1)} fusion(bf16[768,2560]{1,0:T(8,128)(2,1)} %copy-done.27, bf16[768,2560]{1,0:T(8,128)(2,1)} %copy-done.34), kind=kOutput, calls=%fused_computation.365 | convolution fusion | flops 10066329600 | bytes 20971520 | tf_op jit(solution)/shard_map/dot_general | solution.py:29
  1267.3 15.1 collective-permute-done.86
  1286.8 16.9 %fusion.125 = f32[768,2560]{1,0:T(8,128)} fusion(bf16[768,2560]{1,0:T(8,128)(2,1)} %copy-done.34, bf16[2560,2560]{1,0:T(8,128)(2,1)} %bitcast.486), kind=kOutput, calls=%fused_computation.366 | convolution fusion | flops 10066329600 | bytes 24903680 | tf_op jit(solution)/shard_map/dot_general | solution.py:33
  1306.2 31.7 %collective-permute-done.96 = bf16[8,80,2560]{2,1,0:T(8,128)(2,1)S(1)} collective-permute-done((bf16[8,80,2560]{2,1,0:T(8,128)(2,1)}, bf16[8,80,2560]{2,1,0:T(8,128)(2,1)S(1)}, u32[]{:S(2)}, u32[]{:S(2)}) %collective-permute-start.96) | collective-permute-done | bytes 3276832 | tf_op jit(solution)/shard_map/ppermute | solution.py:75
  1353.8 14.7 collective-permute-start.92
  1436.7 37.9 %collective-permute-done.98 = bf16[8,80,640]{2,1,0:T(8,128)(2,1)S(1)} collective-permute-done((bf16[8,80,640]{2,1,0:T(8,128)(2,1)S(1)}, bf16[8,80,640]{2,1,0:T(8,128)(2,1)S(1)}, u32[]{:S(2)}, u32[]{:S(2)}) %collective-permute-start.98) | collective-permute-done | bytes 819232 | tf_op jit(solution)/shard_map/ppermute | solution.py:75
  (653 shorter events, 754.0 us)
Async XLA Ops:
  7.2 284.9 %all-gather.4.cloned.1.call-start = ((), (), s32[]{:S(2)}) async-start(), calls=%async_computation.3 | async-start | bytes 11059200 | tf_op jit(solution)/shard_map/all_gather | solution.py:101
  15.6 69.1 %collective-permute-start.13 = (bf16[80,2560]{1,0:T(8,128)(2,1)}, bf16[80,2560]{1,0:T(8,128)(2,1)S(1)}, u32[]{:S(2)}, u32[]{:S(2)}) collective-permute-start(bf16[80,2560]{1,0:T(8,128)(2,1)} %block_ref.1), channel_id=1, source_target_pairs={{0,8},{8,16},{16,24},{24,28},{28,20},{20,12},{12,4},{4,0},{1,9},{9... | collective-permute-start | bytes 1228808 | tf_op jit(solution)/shard_map/ppermute | solution.py:75
  17.2 449.8 %all-gather.6.cloned.1.call-start = ((), (), s32[]{:S(2)}) async-start(), calls=%async_computation.4 | async-start | bytes 11059200 | tf_op jit(solution)/shard_map/all_gather | solution.py:101
  38.0 46.7 %collective-permute-start.14 = (bf16[80,2560]{1,0:T(8,128)(2,1)S(1)}, bf16[80,2560]{1,0:T(8,128)(2,1)S(1)}, u32[]{:S(2)}, u32[]{:S(2)}) collective-permute-start(bf16[80,2560]{1,0:T(8,128)(2,1)S(1)} %copy-done.46), channel_id=1, source_target_pairs={{0,4},{8,0},{16,8},{24,16},{28,24},{20,28},{12,20},{4,12},{1,5},{9... | collective-permute-start | bytes 1228808 | tf_op jit(solution)/shard_map/ppermute | solution.py:75
  44.8 40.0 %collective-permute-start.15 = (bf16[80,2560]{1,0:T(8,128)(2,1)S(1)}, bf16[80,2560]{1,0:T(8,128)(2,1)S(1)}, u32[]{:S(2)}, u32[]{:S(2)}) collective-permute-start(bf16[80,2560]{1,0:T(8,128)(2,1)S(1)} %copy-done.46), channel_id=1, source_target_pairs={{0,2},{1,3},{2,0},{3,1},{4,6},{5,7},{6,4},{7,5},{8,10},{9,11},{10,... | collective-permute-start | bytes 1228808 | tf_op jit(solution)/shard_map/ppermute | solution.py:75
  51.0 37.1 %collective-permute-start.16 = (bf16[80,640]{1,0:T(8,128)(2,1)S(1)}, bf16[80,640]{1,0:T(8,128)(2,1)S(1)}, u32[]{:S(2)}, u32[]{:S(2)}) collective-permute-start(bf16[80,640]{1,0:T(8,128)(2,1)S(1)} %collective-permute-done.7), channel_id=1, source_target_pairs={{0,2},{1,3},{2,0},{3,1},{4,6},{5,7},{6,4},{7,5},{8,10},{9,11},{10,... | collective-permute-start | bytes 307208 | tf_op jit(solution)/shard_map/ppermute | solution.py:75
  105.6 41.5 %collective-permute-start.24 = (bf16[8,80,640]{2,1,0:T(8,128)(2,1)S(1)}, bf16[8,80,640]{2,1,0:T(8,128)(2,1)S(1)}, u32[]{:S(2)}, u32[]{:S(2)}) collective-permute-start(bf16[8,80,640]{2,1,0:T(8,128)(2,1)S(1)} %copy-done.26), channel_id=1, source_target_pairs={{0,1},{1,0},{2,3},{3,2},{4,5},{5,4},{6,7},{7,6},{8,9},{9,8},{10,11... | collective-permute-start | bytes 2457608 | tf_op jit(solution)/shard_map/ppermute | solution.py:75
  106.2 40.9 %collective-permute-start.25 = (bf16[8,80,640]{2,1,0:T(8,128)(2,1)}, bf16[8,80,640]{2,1,0:T(8,128)(2,1)}, u32[]{:S(2)}, u32[]{:S(2)}) collective-permute-start(bf16[8,80,640]{2,1,0:T(8,128)(2,1)} %bitcast_dynamic-update-slice_fusion.52.refs_2_), channel_id=1, source_target_pairs={{0,1},{1,0},{2,3},{3,2},{4,5},{5,4},{6,7},{7,6},{8,9},{9,8},{10,11... | collective-permute-start | bytes 2457608 | tf_op jit(solution)/shard_map/ppermute | solution.py:75
  114.6 31.8 %collective-permute-start.28 = (bf16[80,2560]{1,0:T(8,128)(2,1)}, bf16[80,2560]{1,0:T(8,128)(2,1)S(1)}, u32[]{:S(2)}, u32[]{:S(2)}) collective-permute-start(bf16[80,2560]{1,0:T(8,128)(2,1)} %collective-permute-done.20), channel_id=1, source_target_pairs={{0,2},{1,3},{2,0},{3,1},{4,6},{5,7},{6,4},{7,5},{8,10},{9,11},{10,... | collective-permute-start | bytes 1228808 | tf_op jit(solution)/shard_map/ppermute | solution.py:75
  132.9 32.2 %collective-permute-start.29 = (bf16[80,2560]{1,0:T(8,128)(2,1)}, bf16[80,2560]{1,0:T(8,128)(2,1)}, u32[]{:S(2)}, u32[]{:S(2)}) collective-permute-start(bf16[80,2560]{1,0:T(8,128)(2,1)} %collective-permute-done.21), channel_id=1, source_target_pairs={{0,2},{1,3},{2,0},{3,1},{4,6},{5,7},{6,4},{7,5},{8,10},{9,11},{10,... | collective-permute-start | bytes 1228808 | tf_op jit(solution)/shard_map/ppermute | solution.py:75
  167.2 37.7 %collective-permute-start.30 = (bf16[768,512]{1,0:T(8,128)(2,1)S(1)}, bf16[768,512]{1,0:T(8,128)(2,1)}, u32[]{:S(2)}, u32[]{:S(2)}) collective-permute-start(bf16[768,512]{1,0:T(8,128)(2,1)S(1)} %pad_maximum_fusion.5.block_ref), channel_id=1, source_target_pairs={{0,8},{8,16},{16,24},{24,28},{28,20},{20,12},{12,4},{4,0},{1,9},{9... | collective-permute-start | bytes 2359304 | tf_op jit(solution)/shard_map/ppermute | solution.py:75
  167.3 37.7 %collective-permute-start.31 = (bf16[768,512]{1,0:T(8,128)(2,1)S(1)}, bf16[768,512]{1,0:T(8,128)(2,1)}, u32[]{:S(2)}, u32[]{:S(2)}) collective-permute-start(bf16[768,512]{1,0:T(8,128)(2,1)S(1)} %pad_maximum_fusion.5.block_ref), channel_id=1, source_target_pairs={{0,4},{8,0},{16,8},{24,16},{28,24},{20,28},{12,20},{4,12},{1,5},{9... | collective-permute-start | bytes 2359304 | tf_op jit(solution)/shard_map/ppermute | solution.py:75
  171.4 31.2 %collective-permute-start.33 = (bf16[48,2560]{1,0:T(8,128)(2,1)S(1)}, bf16[48,2560]{1,0:T(8,128)(2,1)S(1)}, u32[]{:S(2)}, u32[]{:S(2)}) collective-permute-start(bf16[48,2560]{1,0:T(8,128)(2,1)S(1)} %slice.404), channel_id=1, source_target_pairs={{0,4},{8,0},{16,8},{24,16},{28,24},{20,28},{12,20},{4,12},{1,5},{9... | collective-permute-start | bytes 737288 | tf_op jit(solution)/shard_map/ppermute | solution.py:75
  249.3 31.2 %collective-permute-start.43 = (bf16[8,80,2560]{2,1,0:T(8,128)(2,1)}, bf16[8,80,2560]{2,1,0:T(8,128)(2,1)}, u32[]{:S(2)}, u32[]{:S(2)}) collective-permute-start(bf16[8,80,2560]{2,1,0:T(8,128)(2,1)} %bitcast_dynamic-update-slice_fusion.35.refs_0_), channel_id=1, source_target_pairs={{0,1},{1,0},{2,3},{3,2},{4,5},{5,4},{6,7},{7,6},{8,9},{9,8},{10,11... | collective-permute-start | bytes 9830408 | tf_op jit(solution)/shard_map/ppermute | solution.py:75
  322.0 369.9 %all-gather.8.cloned.1.call-start = ((), (), s32[]{:S(2)}) async-start(), calls=%async_computation.5 | async-start | bytes 11059200 | tf_op jit(solution)/shard_map/all_gather | solution.py:101
  428.1 87.4 %collective-permute-start.67 = (bf16[768,2560]{1,0:T(8,128)(2,1)}, bf16[768,2560]{1,0:T(8,128)(2,1)}, u32[]{:S(2)}, u32[]{:S(2)}) collective-permute-start(bf16[768,2560]{1,0:T(8,128)(2,1)} %multiply_convert_fusion.4), channel_id=1, source_target_pairs={{0,2},{1,3},{2,0},{3,1},{4,6},{5,7},{6,4},{7,5},{8,10},{9,11},{10,... | collective-permute-start | bytes 11796488 | tf_op jit(solution)/shard_map/ppermute | solution.py:75
  515.5 397.2 %reduce-scatter.4.cloned.1.call-start = ((), (), s32[]{:S(2)}) async-start(), calls=%async_computation.6 | async-start | bytes 11059200 | tf_op jit(solution)/shard_map/reduce_scatter | solution.py:105
  515.6 87.8 %collective-permute-start.69 = (bf16[768,2560]{1,0:T(8,128)(2,1)}, bf16[768,2560]{1,0:T(8,128)(2,1)}, u32[]{:S(2)}, u32[]{:S(2)}) collective-permute-start(bf16[768,2560]{1,0:T(8,128)(2,1)} %bitcast.49), channel_id=1, source_target_pairs={{0,2},{1,3},{2,0},{3,1},{4,6},{5,7},{6,4},{7,5},{8,10},{9,11},{10,... | collective-permute-start | bytes 11796488 | tf_op jit(solution)/shard_map/ppermute | solution.py:75
  661.6 373.1 %reduce-scatter.6.cloned.1.call-start = ((), (), s32[]{:S(2)}) async-start(), calls=%async_computation.7 | async-start | bytes 11059200 | tf_op jit(solution)/shard_map/reduce_scatter | solution.py:105
  739.9 78.4 %collective-permute-start.71 = (bf16[768,2560]{1,0:T(8,128)(2,1)}, bf16[768,2560]{1,0:T(8,128)(2,1)}, u32[]{:S(2)}, u32[]{:S(2)}) collective-permute-start(bf16[768,2560]{1,0:T(8,128)(2,1)} %slice.415), channel_id=1, source_target_pairs={{0,1},{1,0},{2,3},{3,2},{4,5},{5,4},{6,7},{7,6},{8,9},{9,8},{10,11... | collective-permute-start | bytes 11796488 | tf_op jit(solution)/shard_map/ppermute | solution.py:75
  748.2 113.0 %collective-permute-start.73 = (bf16[768,2560]{1,0:T(8,128)(2,1)}, bf16[768,2560]{1,0:T(8,128)(2,1)}, u32[]{:S(2)}, u32[]{:S(2)}) collective-permute-start(bf16[768,2560]{1,0:T(8,128)(2,1)} %add_convert_fusion.3), channel_id=1, source_target_pairs={{0,2},{1,3},{2,0},{3,1},{4,6},{5,7},{6,4},{7,5},{8,10},{9,11},{10,... | collective-permute-start | bytes 11796488 | tf_op jit(solution)/shard_map/ppermute | solution.py:75
  858.0 362.3 %reduce-scatter.8.cloned.1.call-start = ((), (), s32[]{:S(2)}) async-start(), calls=%async_computation.8 | async-start | bytes 11059200 | tf_op jit(solution)/shard_map/reduce_scatter | solution.py:105
  912.4 52.3 %collective-permute-start.75 = (bf16[768,2560]{1,0:T(8,128)(2,1)}, bf16[768,2560]{1,0:T(8,128)(2,1)}, u32[]{:S(2)}, u32[]{:S(2)}) collective-permute-start(bf16[768,2560]{1,0:T(8,128)(2,1)} %slice.417), channel_id=1, source_target_pairs={{0,1},{1,0},{2,3},{3,2},{4,5},{5,4},{6,7},{7,6},{8,9},{9,8},{10,11... | collective-permute-start | bytes 11796488 | tf_op jit(solution)/shard_map/ppermute | solution.py:75
  964.5 52.5 %collective-permute-start.74 = (bf16[768,2560]{1,0:T(8,128)(2,1)}, bf16[768,2560]{1,0:T(8,128)(2,1)}, u32[]{:S(2)}, u32[]{:S(2)}) collective-permute-start(bf16[768,2560]{1,0:T(8,128)(2,1)} %slice.419), channel_id=1, source_target_pairs={{0,1},{1,0},{2,3},{3,2},{4,5},{5,4},{6,7},{7,6},{8,9},{9,8},{10,11... | collective-permute-start | bytes 11796488 | tf_op jit(solution)/shard_map/ppermute | solution.py:75
  971.6 45.4 %collective-permute-start.76 = (bf16[384,2560]{1,0:T(8,128)(2,1)}, bf16[384,2560]{1,0:T(8,128)(2,1)S(1)}, u32[]{:S(2)}, u32[]{:S(2)}) collective-permute-start(bf16[384,2560]{1,0:T(8,128)(2,1)} %get-tuple-element.251), channel_id=1, source_target_pairs={{0,2},{1,3},{2,0},{3,1},{4,6},{5,7},{6,4},{7,5},{8,10},{9,11},{10,... | collective-permute-start | bytes 5898248 | tf_op jit(solution)/shard_map/ppermute | solution.py:75
  1017.0 57.1 %collective-permute-start.77 = (bf16[384,2560]{1,0:T(8,128)(2,1)}, bf16[384,2560]{1,0:T(8,128)(2,1)}, u32[]{:S(2)}, u32[]{:S(2)}) collective-permute-start(bf16[384,2560]{1,0:T(8,128)(2,1)} %get-tuple-element.257), channel_id=1, source_target_pairs={{0,2},{1,3},{2,0},{3,1},{4,6},{5,7},{6,4},{7,5},{8,10},{9,11},{10,... | collective-permute-start | bytes 5898248 | tf_op jit(solution)/shard_map/ppermute | solution.py:75
  1137.0 55.9 %collective-permute-start.82 = (bf16[8,2,80,2560]{3,2,0,1:T(8,128)(2,1)}, bf16[8,2,80,2560]{3,2,0,1:T(8,128)(2,1)}, u32[]{:S(2)}, u32[]{:S(2)}) collective-permute-start(bf16[8,2,80,2560]{3,2,0,1:T(8,128)(2,1)} %bitcast.451), channel_id=1, source_target_pairs={{0,1},{1,0},{2,3},{3,2},{4,5},{5,4},{6,7},{7,6},{8,9},{9,8},{10,11... | collective-permute-start | bytes 19660808 | tf_op jit(solution)/shard_map/ppermute | solution.py:75
  1247.5 92.9 %collective-permute-start.89 = (bf16[8,2,80,2560]{3,2,0,1:T(8,128)(2,1)}, bf16[8,2,80,2560]{3,2,0,1:T(8,128)(2,1)}, u32[]{:S(2)}, u32[]{:S(2)}) collective-permute-start(bf16[8,2,80,2560]{3,2,0,1:T(8,128)(2,1)} %bitcast.450), channel_id=1, source_target_pairs={{0,1},{1,0},{2,3},{3,2},{4,5},{5,4},{6,7},{7,6},{8,9},{9,8},{10,11... | collective-permute-start | bytes 19660808 | tf_op jit(solution)/shard_map/ppermute | solution.py:75
  1265.1 72.8 %collective-permute-start.96 = (bf16[8,80,2560]{2,1,0:T(8,128)(2,1)}, bf16[8,80,2560]{2,1,0:T(8,128)(2,1)S(1)}, u32[]{:S(2)}, u32[]{:S(2)}) collective-permute-start(bf16[8,80,2560]{2,1,0:T(8,128)(2,1)} %dynamic-slice_bitcast_fusion.1), channel_id=1, source_target_pairs={{0,2},{1,3},{2,0},{3,1},{4,6},{5,7},{6,4},{7,5},{8,10},{9,11},{10,... | collective-permute-start | bytes 9830408 | tf_op jit(solution)/shard_map/ppermute | solution.py:75
  1386.5 88.4 %collective-permute-start.101 = (bf16[8,80,2560]{2,1,0:T(8,128)(2,1)}, bf16[8,80,2560]{2,1,0:T(8,128)(2,1)}, u32[]{:S(2)}, u32[]{:S(2)}) collective-permute-start(bf16[8,80,2560]{2,1,0:T(8,128)(2,1)} %dynamic-slice_bitcast_fusion), channel_id=1, source_target_pairs={{0,2},{1,3},{2,0},{3,1},{4,6},{5,7},{6,4},{7,5},{8,10},{9,11},{10,... | collective-permute-start | bytes 9830408 | tf_op jit(solution)/shard_map/ppermute | solution.py:75
  1386.8 31.4 %collective-permute-start.99 = (bf16[32,2560]{1,0:T(8,128)(2,1)}, bf16[32,2560]{1,0:T(8,128)(2,1)}, u32[]{:S(2)}, u32[]{:S(2)}) collective-permute-start(bf16[32,2560]{1,0:T(8,128)(2,1)} %get-tuple-element.292), channel_id=1, source_target_pairs={{0,8},{8,16},{16,24},{24,28},{28,20},{20,12},{12,4},{4,0},{1,9},{9... | collective-permute-start | bytes 491528 | tf_op jit(solution)/shard_map/ppermute | solution.py:75
  1424.4 50.3 %collective-permute-start.98 = (bf16[8,80,640]{2,1,0:T(8,128)(2,1)S(1)}, bf16[8,80,640]{2,1,0:T(8,128)(2,1)S(1)}, u32[]{:S(2)}, u32[]{:S(2)}) collective-permute-start(bf16[8,80,640]{2,1,0:T(8,128)(2,1)S(1)} %dynamic-slice_bitcast_fusion.3), channel_id=1, source_target_pairs={{0,2},{1,3},{2,0},{3,1},{4,6},{5,7},{6,4},{7,5},{8,10},{9,11},{10,... | collective-permute-start | bytes 2457608 | tf_op jit(solution)/shard_map/ppermute | solution.py:75
  (179 other events, 3121.0 us)
Sparse Core Ops, SparseCore 0:
  17.4 181.8 all-gather.3
  322.1 144.9 all-gather.5
  515.6 176.1 all-gather.7
  695.3 167.8 reduce-scatter.3
  866.7 167.8 reduce-scatter.5
  1038.2 182.0 reduce-scatter.7
